TPU v7x, 256 devices: a whole 4x4x8 slice. The times are simulated.
256 devices in a mesh: role: 2 (over y_lo), grp: 8 (over z), tp: 16 (over x, y_hi, core).
Axes of the slice: x: 4, y: 4 (y_hi: 2, y_lo: 2; y = y_hi * 2 + y_lo), z: 8, core: 2. Of those that a mesh axis runs over, the one named last changes fastest.
Arguments:
- hidden: bfloat16 [2, 8, 64, 8192], P('role', 'grp', 'tp'), may hold values from -6 to 6
- norm_gain: float32 [8192], replicated, may hold values from 0.1 to 1.9
- w_query: bfloat16 [8192, 4096], P(None, 'tp'), may hold values from -0.0625 to 0.0625
- w_keyval: bfloat16 [8192, 1024], P(None, 'tp'), may hold values from -0.16992188 to 0.16992188
- w_out: bfloat16 [4096, 8192], P('tp'), may hold values from -0.09375 to 0.09375
- kv_cache: bfloat16 [2, 8, 4096, 1024], P('role', 'grp', None, 'tp'), may hold values from -180 to 180
- match: int32 [8], replicated, may hold values from 0 to 7, as said below
- cache_lengths: int32 [8, 31], P('grp'), may hold values from 1 to 256, 4096 in all within a row
Outputs:
- layer_out: bfloat16 [2, 8, 64, 8192], P('role', 'grp', 'tp')
Inputs may be any that keep to these rules, and one draw needn't show every extreme that they name: `match`: a permutation of the groups in which prefill group 8 - 1 hands over to decode group 0. `cache_lengths`: each row sums to 4096, and its largest entry is exactly 256.
All inputs are finite; a program needn't handle non-finite values.
Results may differ from a plain program's by a relative error of at most 0.03.
Values may be sent and summed in bfloat16 or wider, within the bound.
No kernel may reach another device: no remote copies, remote signals or barrier semaphores. Data moves between devices by JAX's collectives and lax.ppermute only.
A program may use at most 64 MiB of HBM per device.

v0:
```python
import math

import jax
import jax.numpy as jnp
from jax import lax
from jax.sharding import PartitionSpec as P

KVH = 4
HD = 128
STEPS = 2


def swapped(block, axis, stride):
    count = lax.axis_size(axis)
    route = []
    for low in range(count):
        high = low | 1 << stride
        if high != low and high < count:
            route += [(low, high), (high, low)]
    return lax.ppermute(block, axis, route)


def rotate(tensor, positions):
    half_dim = HD // 2
    inverse = 500000.0 ** (-(2.0 / HD) * jnp.arange(half_dim, dtype=jnp.float32))
    angles = positions.astype(jnp.float32)[:, None] * inverse[None, :]
    cosine = jnp.cos(angles)[:, None, :]
    sine = jnp.sin(angles)[:, None, :]
    paired = tensor.reshape(tensor.shape[0], tensor.shape[1], half_dim, 2)
    first = paired[..., 0]
    second = paired[..., 1]
    turned = jnp.stack([first * cosine - second * sine, first * sine + second * cosine], -1)
    return turned.reshape(tensor.shape)


def rotate_columns(flat, positions, first_column):
    row_count = flat.shape[0]
    pair_count = flat.shape[1] // 2
    column = first_column + 2 * jnp.arange(pair_count, dtype=jnp.int32)
    pair_index = column % HD // 2
    is_key = column // HD % 2 == 0
    inverse = 500000.0 ** (-(2.0 / HD) * pair_index.astype(jnp.float32))
    angles = positions.astype(jnp.float32)[:, None] * inverse[None, :]
    cosine = jnp.cos(angles)
    sine = jnp.sin(angles)
    paired = flat.reshape(row_count, pair_count, 2)
    first = paired[..., 0]
    second = paired[..., 1]
    turned = jnp.stack([first * cosine - second * sine, first * sine + second * cosine], -1)
    kept = jnp.where(is_key[None, :, None], turned, paired)
    return kept.reshape(row_count, pair_count * 2)


def select_source(wanted, carry, piece):
    inside = (wanted >= 0) & (wanted < piece.shape[0])
    chosen = lax.dynamic_index_in_dim(
        piece, jnp.clip(wanted, 0, piece.shape[0] - 1), 0, keepdims=False
    )
    return jnp.where(inside, chosen, carry)


def pick_row(table, selector):
    return jnp.sum(jnp.where(selector, table[None, :], 0), 1)


def local(hidden, norm_gain, w_query, w_keyval, w_out, kv_cache, match, cache_lengths):
    side_index = lax.axis_index("role")
    group_index = lax.axis_index("grp")
    tp_index = lax.axis_index("tp")
    own_rows = hidden[0, 0]
    floated = own_rows.astype(jnp.float32)
    spread = jnp.mean(floated * floated, axis=-1, keepdims=True)
    normed = (floated * lax.rsqrt(spread + 1e-05) * norm_gain).astype(jnp.bfloat16)
    query_cols = w_query.shape[1]
    kv_cols = w_keyval.shape[1]
    piece = lax.all_gather(normed, "tp", axis=0, tiled=True)
    projected = jnp.concatenate(
        [
            jnp.dot(piece, w_query, preferred_element_type=jnp.float32),
            jnp.dot(piece, w_keyval, preferred_element_type=jnp.float32),
        ],
        1,
    )
    row_count = projected.shape[0]
    head_count = query_cols // HD
    cache_len = kv_cache.shape[2]
    req_total = row_count // STEPS
    row_ids = jnp.arange(row_count, dtype=jnp.int32)
    request = row_ids // STEPS
    step_ids = row_ids % STEPS
    lengths_row = cache_lengths[0]
    zero_one = jnp.zeros((1,), jnp.int32)
    bases = jnp.concatenate([jnp.full((1,), cache_len + row_count, jnp.int32), lengths_row])
    offsets = jnp.cumsum(lengths_row) - lengths_row
    selector = request[:, None] == jnp.arange(req_total, dtype=jnp.int32)[None, :]
    base_row = pick_row(bases, selector)
    start_row = pick_row(jnp.concatenate([zero_one, offsets]), selector)
    span_row = pick_row(jnp.concatenate([zero_one, lengths_row]), selector)
    positions = jnp.where(side_index == 0, cache_len + row_ids, base_row + step_ids)
    query = rotate(projected[:, :query_cols].reshape(row_count, head_count, HD), positions).astype(
        jnp.bfloat16
    )
    fresh_flat = rotate_columns(projected[:, query_cols:], positions, tp_index * kv_cols).astype(
        jnp.bfloat16
    )
    local_cache = kv_cache[0, 0]
    outgoing = jnp.concatenate([local_cache, fresh_flat], 0)
    source = jnp.sum(
        jnp.where(match == group_index, jnp.arange(match.shape[0], dtype=jnp.int32), 0)
    )
    empty = jnp.zeros_like(outgoing)
    arrived = select_source(
        source, empty, lax.all_gather(outgoing[None], ("role", "grp"), axis=0, tiled=True)
    )
    first_block = jnp.where(side_index == 0, outgoing, arrived)
    assembled = jnp.concatenate([first_block, local_cache, fresh_flat], 0)
    entry_count = assembled.shape[0]
    sharers = lax.axis_size("tp") // KVH
    for bit in range(max(0, sharers.bit_length() - 1)):
        partner = swapped(assembled, "tp", bit)
        lower = tp_index // (1 << bit) % 2 == 0
        assembled = jnp.where(
            lower,
            jnp.concatenate([assembled, partner], 1),
            jnp.concatenate([partner, assembled], 1),
        )
    shaped = assembled.reshape(entry_count, -1, 2, HD)
    key_set = shaped[:, :, 0]
    value_set = shaped[:, :, 1]
    kv_heads = shaped.shape[1]
    arrived_len = cache_len + row_count
    first_index = jnp.arange(arrived_len, dtype=jnp.int32)[None, :]
    prefill_ok = first_index <= cache_len + row_ids[:, None]
    decode_first = jnp.broadcast_to((request == 0)[:, None], (row_count, arrived_len))
    first_ok = jnp.where(side_index == 0, prefill_ok, decode_first)
    cache_index = jnp.arange(cache_len, dtype=jnp.int32)[None, :]
    cache_ok = (
        (side_index != 0)
        & (cache_index >= start_row[:, None])
        & (cache_index < (start_row + span_row)[:, None])
    )
    new_index = row_ids[None, :]
    new_ok = (
        (side_index != 0)
        & (new_index // STEPS == request[:, None])
        & (new_index % STEPS <= step_ids[:, None])
    )
    allowed = jnp.concatenate([first_ok, cache_ok, new_ok], 1)
    grouped = query.reshape(row_count, kv_heads, head_count // kv_heads, HD)
    scores = jnp.einsum(
        "rkgd,tkd->kgrt", grouped, key_set, preferred_element_type=jnp.float32
    ) / math.sqrt(HD)
    scores = jnp.where(allowed[None, None], scores, -jnp.inf)
    peak = jnp.max(scores, -1, keepdims=True)
    weights = jnp.exp(scores - peak)
    probs = (weights / jnp.sum(weights, -1, keepdims=True)).astype(jnp.bfloat16)
    mixed = jnp.einsum("kgrt,tkd->rkgd", probs, value_set, preferred_element_type=jnp.float32)
    attended = mixed.reshape(row_count, head_count * HD).astype(jnp.bfloat16)
    piece = attended
    summed = lax.psum_scatter(
        jnp.dot(piece, w_out, preferred_element_type=jnp.float32).astype(jnp.bfloat16),
        "tp",
        scatter_dimension=0,
        tiled=True,
    ).astype(jnp.float32)
    return (floated + summed).astype(jnp.bfloat16)[None, None]


def solution(mesh):
    return jax.shard_map(
        local,
        mesh=mesh,
        in_specs=(
            P("role", "grp", "tp", None),
            P(),
            P(None, "tp"),
            P(None, "tp"),
            P("tp", None),
            P("role", "grp", None, "tp"),
            P(),
            P("grp", None),
        ),
        out_specs=P("role", "grp", "tp", None),
        check_vma=False,
    )
```

profile of v0, /device:TPU:1, one launch (start us, length us, event | category | flops | bytes accessed | tf_op | source)
XLA Modules:
  0.0 390.9 jit_solution(16591365339163709677)
XLA Ops:
  6.5 0.0 copy-start
  6.5 0.0 copy-start.1
  6.5 0.0 copy-start.4
  6.5 0.0 all-gather.6.cloned.1.call-start
  6.5 1.1 fusion.15
  7.7 1.6 fusion.20
  9.3 0.0 all-gather.6.cloned.1.call-update
  9.3 0.0 all-gather.8.cloned.1.call-start
  9.4 0.8 copy.39
  10.1 0.1 reduce-window.9
  10.2 0.1 reduce.2
  10.3 0.1 broadcast_in_dim.92
  10.4 0.1 broadcast_in_dim.93
  10.5 0.7 bitcast_subtract_fusion
  11.2 0.7 pad_add_fusion.2
  11.9 0.1 select_reduce_fusion
  12.0 52.4 %all-gather.6.cloned.1.call-done = bf16[16,4,8192]{2,1,0:T(4,128)(2,1)} async-done(((bf16[1,4,8192]{2,1,0:T(4,128)(2,1)}), bf16[16,4,8192]{2,1,0:T(4,128)(2,1)}) %all-gather.6.cloned.1.call-update) | async-done | bytes 1048592 | tf_op jit(solution)/shard_map/all_gather | solution.py:76
  64.4 1.3 reshape.424
  65.7 0.0 copy-done
  65.8 0.4 fusion.35
  66.2 0.1 fusion.27
  66.4 0.1 select_convert_fusion
  66.5 0.0 copy-done.1
  66.5 0.9 fusion.14
  67.4 0.0 all-gather.8.cloned.1.call-update
  67.4 0.0 all-reduce.3.cloned.1.call-start
  67.4 0.0 copy-done.4
  67.5 0.6 fusion.31
  70.0 0.1 compare_and_fusion
  70.1 99.5 %all-gather.8.cloned.1.call-done = bf16[16,4160,64]{1,2,0:T(8,128)(2,1)} async-done(((bf16[1,4160,64]{1,2,0:T(8,128)(2,1)}), bf16[16,4160,64]{1,2,0:T(8,128)(2,1)}) %all-gather.8.cloned.1.call-update) | async-done | bytes 8519696 | tf_op jit(solution)/shard_map/all_gather | solution.py:113
  169.6 1.2 bitcast_select_fusion
  170.8 2.1 concatenate.32
  172.9 0.7 collective-permute-start
  173.6 0.3 fusion.13
  173.9 2.2 collective-permute-done
  176.1 3.4 maximum_select_fusion.1
  179.5 2.4 collective-permute-start.1
  181.9 0.2 fusion.11
  182.2 1.2 concatenate.39
  183.4 0.2 multiply_cosine_fusion
  183.6 3.9 %fusion.36 = f32[64,256]{0,1:T(8,128)S(1)} fusion(bf16[64,8192]{1,0:T(8,128)(2,1)S(1)} %reshape.424, bf16[8192,256]{1,0:T(8,128)(2,1)} %param.10), kind=kOutput, calls=%fused_computation.92 | convolution fusion | flops 268435456 | bytes 5308416 | tf_op jit(solution)/shard_map/dot_general | solution.py:79
  187.5 0.2 subtract_convert_fusion
  187.7 0.2 pad_maximum_fusion.1
  187.9 40.9 %collective-permute-done.1 = bf16[8320,128]{0,1:T(8,128)(2,1)} collective-permute-done((bf16[8320,128]{0,1:T(8,128)(2,1)}, bf16[8320,128]{0,1:T(8,128)(2,1)}, u32[]{:S(2)}, u32[]{:S(2)}) %collective-permute-start.1) | collective-permute-done | bytes 2129952 | tf_op jit(solution)/shard_map/ppermute | solution.py:20
  228.8 4.0 %maximum_select_fusion = bf16[8320,256]{0,1:T(8,128)(2,1)S(1)} fusion(bf16[8320,128]{0,1:T(8,128)(2,1)} %collective-permute-done.1, bf16[8320,128]{0,1:T(8,128)(2,1)} %maximum_select_fusion.1, pred[]{:T(512)S(6)} %eq.81), kind=kLoop, calls=%fused_computation.4 | loop fusion | flops 19169280 | bytes 8519681 | tf_op jit(solution)/shard_map/jit(_where)/select_n | solution.py:122
  232.9 1.0 fusion.34
  233.9 0.8 fusion.2
  234.7 0.0 copy-start.2
  234.7 0.9 fusion.8
  235.6 0.0 copy-start.5
  235.6 0.0 copy-start.3
  235.7 1.2 copy-done.2
  236.9 1.9 convolution_convert_fusion
  238.8 0.0 all-reduce.3.cloned.1.call-update
  238.8 0.0 copy-done.5
  238.8 0.6 dynamic-slice.1
  240.1 142.7 %all-reduce.3.cloned.1.call-done = bf16[64,8192]{1,0:T(8,128)(2,1)} async-done(((bf16[64,8192]{1,0:T(8,128)(2,1)}), bf16[64,8192]{1,0:T(8,128)(2,1)}) %all-reduce.3.cloned.1.call-update) | async-done | bytes 1048592
  382.7 0.0 copy-done.3
  382.7 1.6 fusion.19
  (13 shorter events, 0.2 us)
Async XLA Ops:
  6.5 59.2 %copy-start = (bf16[8192,64]{0,1:T(8,128)(2,1)S(1)}, bf16[8192,64]{0,1:T(8,128)(2,1)}, u32[]{:S(2)}) copy-start(bf16[8192,64]{0,1:T(8,128)(2,1)} %param.11) | copy-start | bytes 3145732
  6.5 59.9 %copy-start.1 = (bf16[1,1,4096,64]{2,3,1,0:T(8,128)(2,1)S(1)}, bf16[1,1,4096,64]{2,3,1,0:T(8,128)(2,1)}, u32[]{:S(2)}) copy-start(bf16[1,1,4096,64]{2,3,1,0:T(8,128)(2,1)} %param.13) | copy-start | bytes 1572868
  6.5 60.9 %copy-start.4 = (s32[8]{0:T(128)S(1)}, s32[8]{0:T(128)}, u32[]{:S(2)}) copy-start(s32[8]{0:T(128)} %param.14) | copy-start | bytes 100
  6.5 57.9 %all-gather.6.cloned.1.call-start = ((), (), s32[]{:S(2)}) async-start(), calls=%async_computation | async-start | bytes 1114112 | tf_op jit(solution)/shard_map/all_gather | solution.py:76
  9.3 160.3 %all-gather.8.cloned.1.call-start = ((), (), s32[]{:S(2)}) async-start(), calls=%async_computation.1 | async-start | bytes 9191424 | tf_op jit(solution)/shard_map/all_gather | solution.py:113
  67.4 315.3 %all-reduce.3.cloned.1.call-start = ((), (), s32[]{:S(2)}) async-start(), calls=%async_computation.2 | async-start | bytes 2097152
  172.9 3.2 collective-permute-start
  179.5 49.4 %collective-permute-start.1 = (bf16[8320,128]{0,1:T(8,128)(2,1)}, bf16[8320,128]{0,1:T(8,128)(2,1)}, u32[]{:S(2)}, u32[]{:S(2)}) collective-permute-start(bf16[8320,128]{0,1:T(8,128)(2,1)} %maximum_select_fusion.1), channel_id=1, source_target_pairs={{0,2},{2,0},{1,3},{3,1},{4,6},{6,4},{5,7},{7,5},{8,10},{10,8},{9,1... | collective-permute-start | bytes 6389768 | tf_op jit(solution)/shard_map/ppermute | solution.py:20
  234.7 2.2 copy-start.2
  235.6 3.2 copy-start.5
  235.6 147.1 %copy-start.3 = (bf16[1,1,4,8192]{3,2,1,0:T(4,128)(2,1)S(1)}, bf16[1,1,4,8192]{3,2,1,0:T(4,128)(2,1)}, u32[]{:S(2)}) copy-start(bf16[1,1,4,8192]{3,2,1,0:T(4,128)(2,1)} %param.8) | copy-start | bytes 196612
Sparse Core Ops, SparseCore 0:
  10.1 54.2 all-gather.5
  67.5 102.0 all-gather.7
  238.9 143.7 all-reduce.2
where the time goes:
time: 391 us
  waiting for transfers between devices  338 us (86%)
  other arithmetic  18.4 us (5%)
  between operations  15.9 us (4%)
  matrix products  8.17 us (2%)
  local copies, waits for them, and re-layouts  7.49 us (2%)
    unnamed x4, waiting for transfers between devices  143 us
    all_gather x1, waiting for transfers between devices, local(): lax.all_gather(outgoing[None], ('role', 'grp'), axis=0, tiled=True)  99.5 us
    all_gather x1, waiting for transfers between devices, local(): piece = lax.all_gather(normed, 'tp', axis=0, tiled=True)  52.4 us
    ppermute x2, waiting for transfers between devices, swapped(): return lax.ppermute(block, axis, route)  43.1 us
  transfers between devices with their start and end apart: 5, of which 5 were waited for; matrix products, arithmetic and copies ran while one was open for 3% of the time, Pallas kernels for 0%

commit v1 on v0

v1 whole, which is shorter than its diff:
```python
import math

import jax
import jax.numpy as jnp
from jax import lax
from jax.experimental import pallas as pl
from jax.experimental.pallas import tpu as pltpu
from jax.sharding import PartitionSpec as P

HD = 128
STEPS = 2
XN = 4
NEG = -math.inf
F32 = jnp.float32
BF16 = jnp.bfloat16
VMEM = pl.BlockSpec(memory_space=pltpu.VMEM)

CORE = [(i, i ^ 1) for i in range(16)]
YHI = [(i, i ^ 2) for i in range(16)]
BOTH = [(i, i ^ 3) for i in range(16)]


def xshift(k):
    return [(i, (i + 4 * k) % 16) for i in range(16)]


def after(value, *others):
    return lax.optimization_barrier((value,) + others)[0]


def norm_kernel(hidden_ref, gain_ref, out_ref):
    floated = hidden_ref[...].astype(F32)
    spread = jnp.mean(floated * floated, axis=-1, keepdims=True)
    out_ref[...] = (floated * lax.rsqrt(spread + 1e-05) * gain_ref[...]).astype(BF16)


def norm(rows, gain):
    return pl.pallas_call(
        norm_kernel,
        out_shape=jax.ShapeDtypeStruct(rows.shape, BF16),
        in_specs=[VMEM, VMEM],
        out_specs=VMEM,
    )(rows, gain[None, :])


def turn(value, cosine, sine, axis):
    size = value.shape[axis]
    index = lax.broadcasted_iota(jnp.int32, value.shape, axis)
    ahead = pltpu.roll(value, size - 1, axis)
    behind = pltpu.roll(value, 1, axis)
    return value * cosine + jnp.where(index % 2 == 0, ahead, behind) * sine


def project_kernel(
    own_ref, mate_ref, wq_ref, wkv_ref, cq_ref, sq_ref, ck_ref, sk_ref, perm_ref,
    q_ref, fresh_ref, accq, acck,
):
    step = pl.program_id(0)

    @pl.when(step == 0)
    def _():
        accq[...] = jnp.zeros_like(accq)
        acck[...] = jnp.zeros_like(acck)

    rows = jnp.concatenate([own_ref[...], mate_ref[...]], 0)
    accq[...] += jnp.dot(rows, wq_ref[...], preferred_element_type=F32)
    acck[...] += lax.dot_general(
        wkv_ref[...], rows, (((1,), (1,)), ((), ())), preferred_element_type=F32
    )

    @pl.when(step == pl.num_programs(0) - 1)
    def _():
        perm = perm_ref[...]
        query = turn(accq[...], cq_ref[...], sq_ref[...], 1).astype(BF16)
        q_ref[...] = jnp.dot(perm, query, preferred_element_type=F32).astype(BF16)
        fresh = turn(acck[...], ck_ref[...], sk_ref[...], 0).astype(BF16)
        fresh_ref[...] = lax.dot_general(
            fresh, perm, (((1,), (1,)), ((), ())), preferred_element_type=F32
        ).astype(BF16)


def project(own, mate, w_query, w_kv_t, cq, sq, ck, sk, perm):
    half, depth = own.shape
    rows = 2 * half
    qcols = w_query.shape[1]
    kcols = w_kv_t.shape[0]
    chunk = 2048
    full = lambda shape: pl.BlockSpec(shape, lambda k: (0, 0))
    return pl.pallas_call(
        project_kernel,
        grid=(depth // chunk,),
        out_shape=(
            jax.ShapeDtypeStruct((rows, qcols), BF16),
            jax.ShapeDtypeStruct((kcols, rows), BF16),
        ),
        in_specs=[
            pl.BlockSpec((half, chunk), lambda k: (0, k)),
            pl.BlockSpec((half, chunk), lambda k: (0, k)),
            pl.BlockSpec((chunk, qcols), lambda k: (k, 0)),
            pl.BlockSpec((kcols, chunk), lambda k: (0, k)),
            full((rows, qcols)),
            full((rows, qcols)),
            full((kcols, rows)),
            full((kcols, rows)),
            full((rows, rows)),
        ],
        out_specs=(full((rows, qcols)), full((kcols, rows))),
        scratch_shapes=[pltpu.VMEM((rows, qcols), F32), pltpu.VMEM((kcols, rows), F32)],
        compiler_params=pltpu.CompilerParams(vmem_limit_bytes=16 * 1024 * 1024),
    )(own, mate, w_query, w_kv_t, cq, sq, ck, sk, perm)


def softmax_parts(queries, bounds_ref, me, kv_ref, fresh_ref, scores):
    tokens = kv_ref.shape[2]
    chunk = 512
    scale = 1.0 / math.sqrt(HD)
    bounds = bounds_ref[...]
    low, high, fresh_low, fresh_high = (bounds[:, i : i + 1] for i in range(4))
    part = [jnp.bitwise_xor(me, i) for i in range(4)]

    def pair(ref, first, span):
        return jnp.concatenate([ref[part[first], :, span], ref[part[first + 1], :, span]], 0)

    whole = slice(None)
    fresh_scores = jnp.dot(queries, pair(fresh_ref, 0, whole), preferred_element_type=F32) * scale
    index = lax.broadcasted_iota(jnp.int32, fresh_scores.shape, 1)
    fresh_scores = jnp.where((index >= fresh_low) & (index <= fresh_high), fresh_scores, NEG)
    peak = jnp.max(fresh_scores, -1, keepdims=True)
    for start in range(0, tokens, chunk):
        span = slice(start, start + chunk)
        part_scores = jnp.dot(queries, pair(kv_ref, 0, span), preferred_element_type=F32) * scale
        index = lax.broadcasted_iota(jnp.int32, part_scores.shape, 1) + start
        part_scores = jnp.where((index >= low) & (index < high), part_scores, NEG)
        scores[:, span] = part_scores
        peak = jnp.maximum(peak, jnp.max(part_scores, -1, keepdims=True))
    contract = (((1,), (1,)), ((), ()))
    weights = jnp.exp(fresh_scores - peak)
    total = jnp.sum(weights, -1, keepdims=True)
    mixed = lax.dot_general(
        weights.astype(BF16), pair(fresh_ref, 2, whole), contract, preferred_element_type=F32
    )
    for start in range(0, tokens, chunk):
        span = slice(start, start + chunk)
        weights = jnp.exp(scores[:, span] - peak)
        total += jnp.sum(weights, -1, keepdims=True)
        mixed += lax.dot_general(
            weights.astype(BF16), pair(kv_ref, 2, span), contract, preferred_element_type=F32
        )
    return mixed, peak, total


def two_heads(query):
    return jnp.concatenate([query[:, :HD], query[:, HD:]], 0)


def pack_parts(mixed, peak, total):
    spread = lambda column: jnp.broadcast_to(column, mixed.shape)
    return jnp.concatenate([mixed, spread(peak), spread(total)], 1)


def main_kernel(me_ref, q_ref, bounds_ref, kv_ref, fresh_ref, perm_ref, out_ref, first_ref, scores):
    query = q_ref[...]
    rows = query.shape[0]
    mixed, peak, total = softmax_parts(
        two_heads(query), bounds_ref, me_ref[0], kv_ref, fresh_ref, scores
    )
    ready = mixed / total
    attended = jnp.concatenate([ready[:rows], ready[rows:]], 1).astype(BF16)
    out_ref[...] = lax.dot_general(
        perm_ref[...], attended, (((0,), (0,)), ((), ())), preferred_element_type=F32
    ).astype(BF16)
    packed = pack_parts(mixed, peak, total)
    first_ref[...] = jnp.concatenate([packed[:8], packed[rows : rows + 8]], 0)


def first_kernel(me_ref, q_ref, bounds_ref, kv_ref, fresh_ref, out_ref, scores):
    mixed, peak, total = softmax_parts(
        two_heads(q_ref[...]), bounds_ref, me_ref[0], kv_ref, fresh_ref, scores
    )
    out_ref[...] = pack_parts(mixed, peak, total)


SMEM = pl.BlockSpec(memory_space=pltpu.SMEM)
LIMIT = pltpu.CompilerParams(vmem_limit_bytes=24 * 1024 * 1024)


def attend_main(me, query, bounds, kv, fresh, perm):
    rows = query.shape[0]
    return pl.pallas_call(
        main_kernel,
        out_shape=(
            jax.ShapeDtypeStruct(query.shape, BF16),
            jax.ShapeDtypeStruct((16, 3 * HD), F32),
        ),
        in_specs=[SMEM, VMEM, VMEM, VMEM, VMEM, VMEM],
        out_specs=(VMEM, VMEM),
        scratch_shapes=[pltpu.VMEM((2 * rows, kv.shape[2]), F32)],
        compiler_params=LIMIT,
    )(me, query, bounds, kv, fresh, perm)


def attend_first(me, query, bounds, kv, fresh):
    return pl.pallas_call(
        first_kernel,
        out_shape=jax.ShapeDtypeStruct((2 * query.shape[0], 3 * HD), F32),
        in_specs=[SMEM, VMEM, VMEM, VMEM, VMEM],
        out_specs=VMEM,
        scratch_shapes=[pltpu.VMEM((2 * query.shape[0], kv.shape[2]), F32)],
        compiler_params=LIMIT,
    )(me, query, bounds, kv, fresh)


def merge_kernel(own_ref, far_ref, w_ref, out_ref):
    own = own_ref[...]
    far = far_ref[...]
    split = lambda packed: (packed[:, :HD], packed[:, HD : 2 * HD], packed[:, 2 * HD :])
    mixed_a, peak_a, total_a = split(own)
    mixed_b, peak_b, total_b = split(far)
    peak = jnp.maximum(peak_a, peak_b)
    scale_a = jnp.exp(peak_a - peak)
    scale_b = jnp.exp(peak_b - peak)
    ready = (mixed_a * scale_a + mixed_b * scale_b) / (total_a * scale_a + total_b * scale_b)
    attended = jnp.concatenate([ready[:8], ready[8:]], 1).astype(BF16)
    out_ref[...] = jnp.dot(attended, w_ref[...], preferred_element_type=F32).astype(BF16)


def merge(own, far, w_out):
    return pl.pallas_call(
        merge_kernel,
        out_shape=jax.ShapeDtypeStruct((8, w_out.shape[1]), BF16),
        in_specs=[VMEM, VMEM, VMEM],
        out_specs=VMEM,
        compiler_params=LIMIT,
    )(own, far, w_out)


def pick_row(table, selector):
    return jnp.sum(jnp.where(selector, table[None, :], 0), 1)


def local(hidden, norm_gain, w_query, w_keyval, w_out, kv_cache, match, cache_lengths):
    side = lax.axis_index("role")
    group = lax.axis_index("grp")
    tp = lax.axis_index("tp")
    own_rows = hidden[0, 0]
    block = own_rows.shape[0]
    row_count = block * lax.axis_size("tp")
    kv_t = kv_cache[0, 0].T
    cache_len = kv_t.shape[1]
    qcols = w_query.shape[1]
    kcols = w_keyval.shape[1]

    normed = norm(own_rows, norm_gain)
    beside = lax.ppermute(normed, "tp", YHI)
    kv_own = after(kv_t, beside)
    kv_core = lax.ppermute(kv_own, "tp", CORE)
    pair = jnp.concatenate([normed, beside], 0)
    pair = after(pair)
    others = [lax.ppermute(pair, "tp", xshift(-k)) for k in range(1, XN)]
    kv_y = lax.ppermute(kv_own, "tp", YHI)
    own_half = after(jnp.concatenate([pair] + others, 0))
    mate_half = lax.ppermute(own_half, "tp", CORE)
    kv_both = lax.ppermute(kv_y, "tp", CORE)
    kv = jnp.stack([kv_own, kv_core, kv_y, kv_both])

    slot = jnp.arange(row_count, dtype=jnp.int32)
    piece = slot // block
    far_core, far_x, far_y = piece // 8, piece // 2 % XN, piece % 2
    owner = (
        (tp // 4 + far_x) % XN * 4
        + jnp.bitwise_xor(tp // 2 % 2, far_y) * 2
        + jnp.bitwise_xor(tp % 2, far_core)
    )
    row_at = owner * block + slot % block
    row_ids = jnp.arange(row_count, dtype=jnp.int32)
    placed = row_at[None, :] == row_ids[:, None]
    perm = placed.astype(BF16)

    request = row_ids // STEPS
    step_ids = row_ids % STEPS
    lengths = cache_lengths[0]
    zero_one = jnp.zeros((1,), jnp.int32)
    bases = jnp.concatenate([jnp.full((1,), cache_len + row_count, jnp.int32), lengths])
    offsets = jnp.cumsum(lengths) - lengths
    selector = request[:, None] == jnp.arange(row_count // STEPS, dtype=jnp.int32)[None, :]
    start = pick_row(jnp.concatenate([zero_one, offsets]), selector)
    span = pick_row(jnp.concatenate([zero_one, lengths]), selector)
    positions = jnp.where(side == 0, cache_len + row_ids, pick_row(bases, selector) + step_ids)
    low = jnp.where(side == 0, 0, start)
    high = jnp.where(side == 0, cache_len, start + span)
    fresh_low = jnp.where(side == 0, 0, request * STEPS)
    bounds = jnp.stack([low, high, fresh_low, row_ids], 1)
    bounds = jnp.concatenate([bounds, bounds], 0)
    first_bounds = jnp.broadcast_to(
        jnp.array([0, cache_len, 0, row_count - 1], jnp.int32)[None, :], (16, 4)
    )

    position_at = jnp.sum(jnp.where(placed, positions[:, None], 0), 0).astype(F32)
    column = jnp.arange(qcols, dtype=jnp.int32)
    inverse = 500000.0 ** (-(2.0 / HD) * (column % HD // 2).astype(F32))
    angles = position_at[:, None] * inverse[None, :]
    cq = jnp.cos(angles)
    sq = jnp.sin(angles) * jnp.where(column % 2 == 0, -1.0, 1.0)[None, :]
    column = tp * kcols + jnp.arange(kcols, dtype=jnp.int32)
    inverse = 500000.0 ** (-(2.0 / HD) * (column % HD // 2).astype(F32))
    angles = inverse[:, None] * position_at[None, :]
    is_key = (column // HD % 2 == 0)[:, None]
    ck = jnp.where(is_key, jnp.cos(angles), 1.0)
    sk = jnp.where(is_key, jnp.sin(angles) * jnp.where(column % 2 == 0, -1.0, 1.0)[:, None], 0.0)

    query, fresh_own = project(
        own_half, mate_half, w_query, w_keyval.T, cq, sq, ck, sk, perm
    )

    sides = lax.axis_size("role") * lax.axis_size("grp")
    asked = lax.all_to_all(
        jnp.broadcast_to(query[None, :8], (sides, 8, qcols)), ("role", "grp"), 0, 0
    )
    fresh = jnp.stack(
        [fresh_own] + [lax.ppermute(fresh_own, "tp", route) for route in (CORE, YHI, BOTH)]
    )
    me = jnp.reshape(tp % 4, (1,)).astype(jnp.int32)
    attended, first_own = attend_main(me, query, bounds, kv, fresh, perm)
    target = pick_row(match, (jnp.arange(match.shape[0]) == group)[None, :])[0]
    source = jnp.sum(jnp.where(match == group, jnp.arange(match.shape[0], dtype=jnp.int32), 0))
    mine = lax.dynamic_index_in_dim(asked, match.shape[0] + target, 0, keepdims=False)
    told = attend_first(me, mine, first_bounds, kv, fresh)
    answers = lax.all_to_all(
        jnp.broadcast_to(told[None], (sides,) + told.shape), ("role", "grp"), 0, 0
    )

    shares = jnp.dot(attended, w_out, preferred_element_type=F32).astype(BF16)
    half = row_count // 2
    across = lax.ppermute(shares[half:], "tp", CORE)
    total = (shares[:half].astype(F32) + across.astype(F32)).astype(BF16)
    width = half // XN
    parts = [
        lax.ppermute(total[k * width : (k + 1) * width], "tp", xshift(k)) for k in range(1, XN)
    ]
    total = total[:width].astype(F32)
    for part in parts:
        total = total + part.astype(F32)
    total = total.astype(BF16)
    across = lax.ppermute(total[block:], "tp", YHI)
    summed = total[:block].astype(F32) + across.astype(F32)

    far = lax.dynamic_index_in_dim(answers, source, 0, keepdims=False)
    lead = merge(first_own, far, w_out)[:STEPS]
    lead = (lead.astype(F32) + lax.ppermute(lead, "tp", CORE).astype(F32)).astype(BF16)
    lead = (lead.astype(F32) + lax.ppermute(lead, "tp", YHI).astype(F32)).astype(BF16)
    parts = [lax.ppermute(lead, "tp", xshift(k)) for k in range(1, XN)]
    lead = lead.astype(F32)
    for part in parts:
        lead = lead + part.astype(F32)
    lead = jnp.concatenate([lead, summed[STEPS:]], 0)
    summed = jnp.where((side == 1) & (tp == 0), lead, summed)
    return (own_rows.astype(F32) + summed).astype(BF16)[None, None]


def solution(mesh):
    return jax.shard_map(
        local,
        mesh=mesh,
        in_specs=(
            P("role", "grp", "tp", None),
            P(),
            P(None, "tp"),
            P(None, "tp"),
            P("tp", None),
            P("role", "grp", None, "tp"),
            P(),
            P("grp", None),
        ),
        out_specs=P("role", "grp", "tp", None),
        check_vma=False,
    )
```

time: 391 us -> 106 us (0.27)
  waiting for transfers between devices: 338 us -> 33.8 us
  starting transfers between devices: 3.2 us -> 44.1 us
  between operations: 15.9 us -> 3.32 us
  other arithmetic: 18.4 us -> 7.88 us
  matrix products: 8.17 us -> 0.85 us
  Pallas kernels: 0 us -> 6.92 us
    all_gather x2 -> x0, waiting for transfers between devices: 152 us -> none  [the longest x1 99.5 us: local(): lax.all_gather(outgoing[None], ('role', 'grp'), axis=0, tiled=True)]
    unnamed x4 -> x0, waiting for transfers between devices: 143 us -> none
    ppermute x2 -> x21, starting transfers between devices: 3.11 us -> 31.9 us  [the longest x3 4.21 us: local(): parts = [lax.ppermute(lead, 'tp', xshift(k)) for k in range(1, XN)]]
    ppermute x2 -> x21, waiting for transfers between devices: 43.1 us -> 20.2 us  [the longest x3 5.95 us: local(): others = [lax.ppermute(pair, 'tp', xshift(-k)) for k in range(1, XN)]]
    all_to_all x0 -> x2, waiting for transfers between devices: none -> 13.6 us  [the longest x1 9.82 us: local(): lax.all_to_all(jnp.broadcast_to(told[None], (sides,) + told.shape), ('rol...]
    all_to_all x0 -> x2, starting transfers between devices: none -> 12.3 us  [the longest x1 8.43 us: local(): lax.all_to_all(jnp.broadcast_to(query[None, :8], (sides, 8, qcols)), ('ro...]
    select_n x5 -> x7, other arithmetic: 8.85 us -> 0.25 us  [the longest x1 0.19 us: local(): jnp.where(is_key, jnp.sin(angles) * jnp.where(column % 2 == 0, -1.0, 1.0)...]
    dot_general x5 -> x1, matrix products: 8.17 us -> 0.85 us  [local(): shares = jnp.dot(attended, w_out, preferred_element_type=F32).astype(BF16)]
  transfers between devices with their start and end apart: 5 -> 23, of which waited for: 5 -> 13; matrix products, arithmetic and copies ran while one was open for 3% -> 7% of each run, Pallas kernels for 0% -> 3%
where the time goes in v1:
time: 106 us; the launch traced here: 105 us
  starting transfers between devices  44.1 us (42%)
  waiting for transfers between devices  33.8 us (32%)
  other arithmetic  7.88 us (7%)
  local copies, waits for them, and re-layouts  7.76 us (7%)
  Pallas kernels  6.92 us (7%)
  between operations  3.32 us (3%)
    all_to_all x1, waiting for transfers between devices, local(): lax.all_to_all(jnp.broadcast_to(told[None], (sides,) + told.shape), ('rol...  9.82 us
    all_to_all x1, starting transfers between devices, local(): lax.all_to_all(jnp.broadcast_to(query[None, :8], (sides, 8, qcols)), ('ro...  8.43 us
    ppermute x3, waiting for transfers between devices, local(): others = [lax.ppermute(pair, 'tp', xshift(-k)) for k in range(1, XN)]  5.95 us
    unnamed x16, local copies, waits for them, and re-layouts  4.4 us
    ppermute x3, starting transfers between devices, local(): parts = [lax.ppermute(lead, 'tp', xshift(k)) for k in range(1, XN)]  4.21 us
    ppermute x1, waiting for transfers between devices, local(): kv_y = lax.ppermute(kv_own, 'tp', YHI)  4.11 us
    ppermute x3, starting transfers between devices, local(): lax.ppermute(total[k * width:(k + 1) * width], 'tp', xshift(k))  4.09 us
    ppermute x3, waiting for transfers between devices, local(): lax.ppermute(total[k * width:(k + 1) * width], 'tp', xshift(k))  3.98 us
  transfers between devices with their start and end apart: 23, of which 13 were waited for; matrix products, arithmetic and copies ran while one was open for 7% of the time, Pallas kernels for 3%

profile of v1, /device:TPU:1, one launch (start us, length us, event | category | flops | bytes accessed | tf_op | source)
XLA Modules:
  0.0 104.7 jit_solution(3700704831534039271)
XLA Ops:
  0.0 1.8 %shard_map.91 = bf16[4,8192]{1,0:T(4,128)(2,1)} custom-call(bf16[4,8192]{1,0:T(4,128)(2,1)} %bitcast.37, f32[1,8192]{1,0:T(1,128)} %bitcast.38), custom_call_target="tpu_custom_call" | custom-call | tf_op jit(solution)/shard_map/pallas_call | solution.py:38
  1.8 3.7 %collective-permute-start = (bf16[4,8192]{1,0:T(4,128)(2,1)}, bf16[4,8192]{1,0:T(4,128)(2,1)S(1)}, u32[]{:S(2)}, u32[]{:S(2)}) collective-permute-start(bf16[4,8192]{1,0:T(4,128)(2,1)} %shard_map.91), channel_id=1, source_target_pairs={{0,2},{1,3},{2,0},{3,1},{4,6},{5,7},{6,4},{7,5},{8,10},{9,11},{10,... | collective-permute-start | bytes 196616 | tf_op jit(solution)/shard_map/ppermute | solution.py:254
  5.6 0.8 copy.18
  6.4 0.1 reduce.2
  6.5 0.7 bitcast_subtract_fusion
  7.2 0.7 pad_add_fusion.2
  7.9 0.1 select_reduce_fusion.1
  8.0 0.1 select_reduce_fusion
  8.1 0.2 fusion.6
  8.3 0.9 pad_maximum_fusion.2
  9.3 2.6 %collective-permute-start.1 = (bf16[8,8192]{1,0:T(8,128)(2,1)S(1)}, bf16[8,8192]{1,0:T(8,128)(2,1)S(1)}, u32[]{:S(2)}, u32[]{:S(2)}) collective-permute-start(bf16[8,8192]{1,0:T(8,128)(2,1)S(1)} %pad_maximum_fusion.2), channel_id=1, source_target_pairs={{0,12},{1,13},{2,14},{3,15},{4,0},{5,1},{6,2},{7,3},{8,4},{9,5},{1... | collective-permute-start | bytes 393224 | tf_op jit(solution)/shard_map/ppermute | solution.py:259
  11.8 0.5 collective-permute-start.2
  12.3 0.6 collective-permute-start.3
  13.0 2.1 %collective-permute-start.6 = (bf16[64,4096]{1,0:T(8,128)(2,1)}, bf16[64,4096]{1,0:T(8,128)(2,1)S(1)}, u32[]{:S(2)}, u32[]{:S(2)}) collective-permute-start(bf16[64,4096]{1,0:T(8,128)(2,1)} %bitcast.33), channel_id=1, source_target_pairs={{0,2},{1,3},{2,0},{3,1},{4,6},{5,7},{6,4},{7,5},{8,10},{9,11},{10,... | collective-permute-start | bytes 1572872 | tf_op jit(solution)/shard_map/ppermute | solution.py:260
  15.0 0.3 collective-permute-done.1
  15.4 1.8 %collective-permute-done.2 = bf16[8,8192]{1,0:T(8,128)(2,1)S(1)} collective-permute-done((bf16[8,8192]{1,0:T(8,128)(2,1)S(1)}, bf16[8,8192]{1,0:T(8,128)(2,1)S(1)}, u32[]{:S(2)}, u32[]{:S(2)}) %collective-permute-start.2) | collective-permute-done | bytes 131104 | tf_op jit(solution)/shard_map/ppermute | solution.py:259
  17.2 3.8 %collective-permute-done.3 = bf16[8,8192]{1,0:T(8,128)(2,1)S(1)} collective-permute-done((bf16[8,8192]{1,0:T(8,128)(2,1)S(1)}, bf16[8,8192]{1,0:T(8,128)(2,1)S(1)}, u32[]{:S(2)}, u32[]{:S(2)}) %collective-permute-start.3) | collective-permute-done | bytes 131104 | tf_op jit(solution)/shard_map/ppermute | solution.py:259
  21.0 1.1 %collective-permute-start.4 = (bf16[32,8192]{1,0:T(8,128)(2,1)S(1)}, bf16[32,8192]{1,0:T(8,128)(2,1)S(1)}, u32[]{:S(2)}, u32[]{:S(2)}) collective-permute-start(bf16[32,8192]{1,0:T(8,128)(2,1)S(1)} %pad_maximum_fusion.1.own_ref), channel_id=1, source_target_pairs={{0,1},{1,0},{2,3},{3,2},{4,5},{5,4},{6,7},{7,6},{8,9},{9,8},{10,11... | collective-permute-start | bytes 1572872 | tf_op jit(solution)/shard_map/ppermute | solution.py:262
  22.2 0.1 collective-permute-start.5
  22.3 4.1 %collective-permute-done.6 = bf16[64,4096]{1,0:T(8,128)(2,1)S(1)} collective-permute-done((bf16[64,4096]{1,0:T(8,128)(2,1)}, bf16[64,4096]{1,0:T(8,128)(2,1)S(1)}, u32[]{:S(2)}, u32[]{:S(2)}) %collective-permute-start.6) | collective-permute-done | bytes 524320 | tf_op jit(solution)/shard_map/ppermute | solution.py:260
  26.4 2.7 %collective-permute-start.7 = (bf16[64,4096]{1,0:T(8,128)(2,1)S(1)}, bf16[64,4096]{1,0:T(8,128)(2,1)}, u32[]{:S(2)}, u32[]{:S(2)}) collective-permute-start(bf16[64,4096]{1,0:T(8,128)(2,1)S(1)} %collective-permute-done.6), channel_id=1, source_target_pairs={{0,1},{1,0},{2,3},{3,2},{4,5},{5,4},{6,7},{7,6},{8,9},{9,8},{10,11... | collective-permute-start | bytes 1572872 | tf_op jit(solution)/shard_map/ppermute | solution.py:263
  29.1 0.3 fusion.2
  29.5 2.2 %copy-done.2 = bf16[8192,256]{1,0:T(8,128)(2,1)S(1)} copy-done((bf16[8192,256]{1,0:T(8,128)(2,1)S(1)}, bf16[8192,256]{1,0:T(8,128)(2,1)}, u32[]{:S(2)}) %copy-start.2) | copy-done | bytes 4194328
  31.6 2.0 %shard_map.92 = (bf16[64,256]{1,0:T(8,128)(2,1)S(1)}, bf16[64,64]{1,0:T(8,128)(2,1)S(1)}) custom-call(bf16[32,8192]{1,0:T(8,128)(2,1)S(1)} %pad_maximum_fusion.1.own_ref, bf16[32,8192]{1,0:T(8,128)(2,1)S(1)} %collective-permute-done.4.mate_ref, bf16[8192,256]{1,0:T(8,128)(2,1)S(1)} %copy-done.2, bf16[64,8192]{1,0:T(8,128)(2,1)S(1)} %bitcast.31, ...), custom_call_target="tpu_custom_call" | custom-call | tf_op jit(solution)/shard_map/pallas_call | solution.py:89
  33.6 0.1 collective-permute-start.8
  33.7 2.1 %collective-permute-start.9 = (bf16[64,64]{1,0:T(8,128)(2,1)S(1)}, bf16[64,64]{1,0:T(8,128)(2,1)S(1)}, u32[]{:S(2)}, u32[]{:S(2)}) collective-permute-start(bf16[64,64]{1,0:T(8,128)(2,1)S(1)} %get-tuple-element.12), channel_id=1, source_target_pairs={{0,2},{1,3},{2,0},{3,1},{4,6},{5,7},{6,4},{7,5},{8,10},{9,11},{10,... | collective-permute-start | bytes 24584 | tf_op jit(solution)/shard_map/ppermute | solution.py:320
  35.8 1.5 %collective-permute-start.10 = (bf16[64,64]{1,0:T(8,128)(2,1)S(1)}, bf16[64,64]{1,0:T(8,128)(2,1)S(1)}, u32[]{:S(2)}, u32[]{:S(2)}) collective-permute-start(bf16[64,64]{1,0:T(8,128)(2,1)S(1)} %get-tuple-element.12), channel_id=1, source_target_pairs={{0,3},{1,2},{2,1},{3,0},{4,7},{5,6},{6,5},{7,4},{8,11},{9,10},{10,... | collective-permute-start | bytes 24584 | tf_op jit(solution)/shard_map/ppermute | solution.py:320
  37.4 0.1 add_add_fusion
  37.4 0.1 copy.19.bounds_ref
  37.6 0.3 collective-permute-done.9
  37.9 3.0 %collective-permute-done.10 = bf16[64,64]{1,0:T(8,128)(2,1)S(1)} collective-permute-done((bf16[64,64]{1,0:T(8,128)(2,1)S(1)}, bf16[64,64]{1,0:T(8,128)(2,1)S(1)}, u32[]{:S(2)}, u32[]{:S(2)}) %collective-permute-start.10) | collective-permute-done | bytes 8224 | tf_op jit(solution)/shard_map/ppermute | solution.py:320
  41.0 1.6 %pad_maximum_fusion.kv_ref = bf16[4,64,4096]{2,1,0:T(8,128)(2,1)S(1)} fusion(bf16[1,64,4096]{2,1,0:T(8,128)(2,1)} %bitcast.13, bf16[1,64,4096]{2,1,0:T(8,128)(2,1)S(1)} %bitcast.36, bf16[1,64,4096]{2,1,0:T(8,128)(2,1)} %bitcast.11, bf16[1,64,4096]{2,1,0:T(8,128)(2,1)S(1)} %bitcast.35), kind=kLoop, calls=%fused_computation.1 | loop fusion | flops 3145728 | bytes 4194304 | tf_op jit(solution)/shard_map/stack | solution.py:264
  42.6 1.9 %shard_map.93 = (bf16[64,256]{1,0:T(8,128)(2,1)S(1)}, f32[16,384]{1,0:T(8,128)S(1)}) custom-call(s32[1]{0:T(128)} %bitcast.1.me_ref, bf16[64,256]{1,0:T(8,128)(2,1)S(1)} %get-tuple-element.10.q_ref, s32[128,4]{1,0:T(8,128)S(1)} %copy.19.bounds_ref, bf16[4,64,4096]{2,1,0:T(8,128)(2,1)S(1)} %pad_maximum_fusion.kv_ref, ...), custom_call_target="tpu_custom_call" | custom-call | tf_op jit(solution)/shard_map/pallas_call | solution.py:189
  44.5 0.8 convolution_convert_fusion
  45.4 0.8 slice.46
  46.2 0.4 collective-permute-start.16
  46.6 0.6 broadcast_in_dim.135
  47.3 8.4 %all-to-all-start = ((bf16[16,8,256]{2,1,0:T(8,128)(2,1)}), bf16[16,8,256]{2,1,0:T(8,128)(2,1)S(1)}, u32[]{:S(2)}, u32[]{:S(2)}) async-start(bf16[16,8,256]{2,1,0:T(8,128)(2,1)} %broadcast_in_dim.135), calls=%async_computation | async-start | bytes 131072 | tf_op jit(solution)/shard_map/all_to_all | solution.py:316
  55.7 0.7 fusion.21
  59.4 3.8 %all-to-all-done = bf16[16,8,256]{2,1,0:T(8,128)(2,1)S(1)} async-done(((bf16[16,8,256]{2,1,0:T(8,128)(2,1)}), bf16[16,8,256]{2,1,0:T(8,128)(2,1)S(1)}, u32[]{:S(2)}, u32[]{:S(2)}) %all-to-all-start) | async-done | bytes 65568 | tf_op jit(solution)/shard_map/all_to_all | solution.py:316
  63.2 0.7 shard_map.94
  63.9 0.9 broadcast_in_dim.138
  64.7 3.8 %all-to-all-start.1 = ((f32[16,16,384]{2,1,0:T(8,128)}), f32[16,16,384]{2,1,0:T(8,128)S(1)}, u32[]{:S(2)}, u32[]{:S(2)}) async-start(f32[16,16,384]{2,1,0:T(8,128)} %broadcast_in_dim.138), calls=%async_computation.1 | async-start | bytes 786432 | tf_op jit(solution)/shard_map/all_to_all | solution.py:328
  68.6 1.2 %add_convert_fusion = bf16[32,8192]{1,0:T(8,128)(2,1)S(1)} fusion(bf16[32,8192]{1,0:T(8,128)(2,1)} %collective-permute-done.16, bf16[64,8192]{1,0:T(8,128)(2,1)S(1)} %convolution_convert_fusion), kind=kLoop, calls=%fused_computation.2 | loop fusion | flops 1048576 | bytes 1572864 | tf_op jit(solution)/shard_map/convert_element_type | solution.py:335
  69.8 9.8 %all-to-all-done.1 = f32[16,16,384]{2,1,0:T(8,128)S(1)} async-done(((f32[16,16,384]{2,1,0:T(8,128)}), f32[16,16,384]{2,1,0:T(8,128)S(1)}, u32[]{:S(2)}, u32[]{:S(2)}) %all-to-all-start.1) | async-done | bytes 393248 | tf_op jit(solution)/shard_map/all_to_all | solution.py:328
  79.6 2.2 %copy-done.1 = bf16[256,8192]{1,0:T(8,128)(2,1)S(1)} copy-done((bf16[256,8192]{1,0:T(8,128)(2,1)S(1)}, bf16[256,8192]{1,0:T(8,128)(2,1)}, u32[]{:S(2)}) %copy-start.1) | copy-done | bytes 4194328
  81.8 0.6 shard_map.95
  82.5 2.6 %collective-permute-start.11 = (bf16[2,8192]{1,0:T(2,128)(2,1)S(1)}, bf16[2,8192]{1,0:T(2,128)(2,1)S(1)}, u32[]{:S(2)}, u32[]{:S(2)}) collective-permute-start(bf16[2,8192]{1,0:T(2,128)(2,1)S(1)} %slice.44), channel_id=1, source_target_pairs={{0,1},{1,0},{2,3},{3,2},{4,5},{5,4},{6,7},{7,6},{8,9},{9,8},{10,11... | collective-permute-start | bytes 98312 | tf_op jit(solution)/shard_map/ppermute | solution.py:349
  85.1 1.6 %collective-permute-start.17 = (bf16[8,8192]{1,0:T(8,128)(2,1)S(1)}, bf16[8,8192]{1,0:T(8,128)(2,1)S(1)}, u32[]{:S(2)}, u32[]{:S(2)}) collective-permute-start(bf16[8,8192]{1,0:T(8,128)(2,1)S(1)} %get-tuple-element.20), channel_id=1, source_target_pairs={{0,4},{1,5},{2,6},{3,7},{4,8},{5,9},{6,10},{7,11},{8,12},{9,13},{1... | collective-permute-start | bytes 393224 | tf_op jit(solution)/shard_map/ppermute | solution.py:338
  86.7 1.7 %collective-permute-start.18 = (bf16[8,8192]{1,0:T(8,128)(2,1)S(1)}, bf16[8,8192]{1,0:T(8,128)(2,1)S(1)}, u32[]{:S(2)}, u32[]{:S(2)}) collective-permute-start(bf16[8,8192]{1,0:T(8,128)(2,1)S(1)} %get-tuple-element.22), channel_id=1, source_target_pairs={{0,8},{1,9},{2,10},{3,11},{4,12},{5,13},{6,14},{7,15},{8,0},{9,1},... | collective-permute-start | bytes 393224 | tf_op jit(solution)/shard_map/ppermute | solution.py:338
  88.5 0.8 collective-permute-start.19
  89.3 1.7 %collective-permute-start.12 = (bf16[2,8192]{1,0:T(2,128)(2,1)S(1)}, bf16[2,8192]{1,0:T(2,128)(2,1)S(1)}, u32[]{:S(2)}, u32[]{:S(2)}) collective-permute-start(bf16[2,8192]{1,0:T(2,128)(2,1)S(1)} %add_convert_fusion.3), channel_id=1, source_target_pairs={{0,2},{1,3},{2,0},{3,1},{4,6},{5,7},{6,4},{7,5},{8,10},{9,11},{10,... | collective-permute-start | bytes 98312 | tf_op jit(solution)/shard_map/ppermute | solution.py:350
  90.9 0.6 collective-permute-done.17
  91.5 3.4 %collective-permute-done.18 = bf16[8,8192]{1,0:T(8,128)(2,1)S(1)} collective-permute-done((bf16[8,8192]{1,0:T(8,128)(2,1)S(1)}, bf16[8,8192]{1,0:T(8,128)(2,1)S(1)}, u32[]{:S(2)}, u32[]{:S(2)}) %collective-permute-start.18) | collective-permute-done | bytes 131104 | tf_op jit(solution)/shard_map/ppermute | solution.py:338
  94.9 0.1 add_convert_fusion.1
  95.0 1.7 %collective-permute-start.20 = (bf16[4,8192]{1,0:T(4,128)(2,1)S(1)}, bf16[4,8192]{1,0:T(4,128)(2,1)S(1)}, u32[]{:S(2)}, u32[]{:S(2)}) collective-permute-start(bf16[4,8192]{1,0:T(4,128)(2,1)S(1)} %slice.52), channel_id=1, source_target_pairs={{0,2},{1,3},{2,0},{3,1},{4,6},{5,7},{6,4},{7,5},{8,10},{9,11},{10,... | collective-permute-start | bytes 196616 | tf_op jit(solution)/shard_map/ppermute | solution.py:344
  96.7 1.7 %collective-permute-start.13 = (bf16[2,8192]{1,0:T(2,128)(2,1)S(1)}, bf16[2,8192]{1,0:T(2,128)(2,1)S(1)}, u32[]{:S(2)}, u32[]{:S(2)}) collective-permute-start(bf16[2,8192]{1,0:T(2,128)(2,1)S(1)} %add_convert_fusion.2), channel_id=1, source_target_pairs={{0,4},{1,5},{2,6},{3,7},{4,8},{5,9},{6,10},{7,11},{8,12},{9,13},{1... | collective-permute-start | bytes 98312 | tf_op jit(solution)/shard_map/ppermute | solution.py:351
  98.5 2.2 %collective-permute-start.14 = (bf16[2,8192]{1,0:T(2,128)(2,1)S(1)}, bf16[2,8192]{1,0:T(2,128)(2,1)S(1)}, u32[]{:S(2)}, u32[]{:S(2)}) collective-permute-start(bf16[2,8192]{1,0:T(2,128)(2,1)S(1)} %add_convert_fusion.2), channel_id=1, source_target_pairs={{0,8},{1,9},{2,10},{3,11},{4,12},{5,13},{6,14},{7,15},{8,0},{9,1},... | collective-permute-start | bytes 98312 | tf_op jit(solution)/shard_map/ppermute | solution.py:351
  100.7 0.2 collective-permute-start.15
  101.0 0.1 collective-permute-done.13
  101.1 1.6 %collective-permute-done.14 = bf16[2,8192]{1,0:T(2,128)(2,1)S(1)} collective-permute-done((bf16[2,8192]{1,0:T(2,128)(2,1)S(1)}, bf16[2,8192]{1,0:T(2,128)(2,1)S(1)}, u32[]{:S(2)}, u32[]{:S(2)}) %collective-permute-start.14) | collective-permute-done | bytes 32800 | tf_op jit(solution)/shard_map/ppermute | solution.py:351
  102.7 1.1 %collective-permute-done.15 = bf16[2,8192]{1,0:T(2,128)(2,1)S(1)} collective-permute-done((bf16[2,8192]{1,0:T(2,128)(2,1)S(1)}, bf16[2,8192]{1,0:T(2,128)(2,1)S(1)}, u32[]{:S(2)}, u32[]{:S(2)}) %collective-permute-start.15) | collective-permute-done | bytes 32800 | tf_op jit(solution)/shard_map/ppermute | solution.py:351
  103.8 0.1 convert_add_fusion.1
  103.9 0.7 fusion.3
  (49 shorter events, 0.6 us)
Async XLA Ops:
  0.0 29.4 %copy-start.3 = (bf16[8192,64]{0,1:T(8,128)(2,1)S(1)}, bf16[8192,64]{0,1:T(8,128)(2,1)}, u32[]{:S(2)}) copy-start(bf16[8192,64]{0,1:T(8,128)(2,1)} %param.12) | copy-start | bytes 3145732
  1.8 6.6 %collective-permute-start = (bf16[4,8192]{1,0:T(4,128)(2,1)}, bf16[4,8192]{1,0:T(4,128)(2,1)S(1)}, u32[]{:S(2)}, u32[]{:S(2)}) collective-permute-start(bf16[4,8192]{1,0:T(4,128)(2,1)} %shard_map.91), channel_id=1, source_target_pairs={{0,2},{1,3},{2,0},{3,1},{4,6},{5,7},{6,4},{7,5},{8,10},{9,11},{10,... | collective-permute-start | bytes 196616 | tf_op jit(solution)/shard_map/ppermute | solution.py:254
  9.3 6.1 %collective-permute-start.1 = (bf16[8,8192]{1,0:T(8,128)(2,1)S(1)}, bf16[8,8192]{1,0:T(8,128)(2,1)S(1)}, u32[]{:S(2)}, u32[]{:S(2)}) collective-permute-start(bf16[8,8192]{1,0:T(8,128)(2,1)S(1)} %pad_maximum_fusion.2), channel_id=1, source_target_pairs={{0,12},{1,13},{2,14},{3,15},{4,0},{5,1},{6,2},{7,3},{8,4},{9,5},{1... | collective-permute-start | bytes 393224 | tf_op jit(solution)/shard_map/ppermute | solution.py:259
  11.8 5.4 %collective-permute-start.2 = (bf16[8,8192]{1,0:T(8,128)(2,1)S(1)}, bf16[8,8192]{1,0:T(8,128)(2,1)S(1)}, u32[]{:S(2)}, u32[]{:S(2)}) collective-permute-start(bf16[8,8192]{1,0:T(8,128)(2,1)S(1)} %pad_maximum_fusion.2), channel_id=1, source_target_pairs={{0,8},{1,9},{2,10},{3,11},{4,12},{5,13},{6,14},{7,15},{8,0},{9,1},... | collective-permute-start | bytes 393224 | tf_op jit(solution)/shard_map/ppermute | solution.py:259
  12.3 8.7 %collective-permute-start.3 = (bf16[8,8192]{1,0:T(8,128)(2,1)S(1)}, bf16[8,8192]{1,0:T(8,128)(2,1)S(1)}, u32[]{:S(2)}, u32[]{:S(2)}) collective-permute-start(bf16[8,8192]{1,0:T(8,128)(2,1)S(1)} %pad_maximum_fusion.2), channel_id=1, source_target_pairs={{0,4},{1,5},{2,6},{3,7},{4,8},{5,9},{6,10},{7,11},{8,12},{9,13},{1... | collective-permute-start | bytes 393224 | tf_op jit(solution)/shard_map/ppermute | solution.py:259
  13.0 13.4 %collective-permute-start.6 = (bf16[64,4096]{1,0:T(8,128)(2,1)}, bf16[64,4096]{1,0:T(8,128)(2,1)S(1)}, u32[]{:S(2)}, u32[]{:S(2)}) collective-permute-start(bf16[64,4096]{1,0:T(8,128)(2,1)} %bitcast.33), channel_id=1, source_target_pairs={{0,2},{1,3},{2,0},{3,1},{4,6},{5,7},{6,4},{7,5},{8,10},{9,11},{10,... | collective-permute-start | bytes 1572872 | tf_op jit(solution)/shard_map/ppermute | solution.py:260
  21.0 8.4 %collective-permute-start.4 = (bf16[32,8192]{1,0:T(8,128)(2,1)S(1)}, bf16[32,8192]{1,0:T(8,128)(2,1)S(1)}, u32[]{:S(2)}, u32[]{:S(2)}) collective-permute-start(bf16[32,8192]{1,0:T(8,128)(2,1)S(1)} %pad_maximum_fusion.1.own_ref), channel_id=1, source_target_pairs={{0,1},{1,0},{2,3},{3,2},{4,5},{5,4},{6,7},{7,6},{8,9},{9,8},{10,11... | collective-permute-start | bytes 1572872 | tf_op jit(solution)/shard_map/ppermute | solution.py:262
  22.2 18.8 %collective-permute-start.5 = (bf16[64,4096]{1,0:T(8,128)(2,1)}, bf16[64,4096]{1,0:T(8,128)(2,1)}, u32[]{:S(2)}, u32[]{:S(2)}) collective-permute-start(bf16[64,4096]{1,0:T(8,128)(2,1)} %bitcast.34), channel_id=1, source_target_pairs={{0,1},{1,0},{2,3},{3,2},{4,5},{5,4},{6,7},{7,6},{8,9},{9,8},{10,11... | collective-permute-start | bytes 1572872 | tf_op jit(solution)/shard_map/ppermute | solution.py:256
  26.4 14.6 %collective-permute-start.7 = (bf16[64,4096]{1,0:T(8,128)(2,1)S(1)}, bf16[64,4096]{1,0:T(8,128)(2,1)}, u32[]{:S(2)}, u32[]{:S(2)}) collective-permute-start(bf16[64,4096]{1,0:T(8,128)(2,1)S(1)} %collective-permute-done.6), channel_id=1, source_target_pairs={{0,1},{1,0},{2,3},{3,2},{4,5},{5,4},{6,7},{7,6},{8,9},{9,8},{10,11... | collective-permute-start | bytes 1572872 | tf_op jit(solution)/shard_map/ppermute | solution.py:263
  29.4 2.2 %copy-start.2 = (bf16[8192,256]{1,0:T(8,128)(2,1)S(1)}, bf16[8192,256]{1,0:T(8,128)(2,1)}, u32[]{:S(2)}) copy-start(bf16[8192,256]{1,0:T(8,128)(2,1)} %wq_ref.1) | copy-start | bytes 12582916
  31.6 9.3 %copy-start.4 = (bf16[1,1,4096,64]{2,3,1,0:T(8,128)(2,1)S(1)}, bf16[1,1,4096,64]{2,3,1,0:T(8,128)(2,1)}, u32[]{:S(2)}) copy-start(bf16[1,1,4096,64]{2,3,1,0:T(8,128)(2,1)} %param.14) | copy-start | bytes 1572868
  33.6 3.9 %collective-permute-start.8 = (bf16[64,64]{1,0:T(8,128)(2,1)S(1)}, bf16[64,64]{1,0:T(8,128)(2,1)S(1)}, u32[]{:S(2)}, u32[]{:S(2)}) collective-permute-start(bf16[64,64]{1,0:T(8,128)(2,1)S(1)} %get-tuple-element.12), channel_id=1, source_target_pairs={{0,1},{1,0},{2,3},{3,2},{4,5},{5,4},{6,7},{7,6},{8,9},{9,8},{10,11... | collective-permute-start | bytes 24584 | tf_op jit(solution)/shard_map/ppermute | solution.py:320
  33.7 4.2 %collective-permute-start.9 = (bf16[64,64]{1,0:T(8,128)(2,1)S(1)}, bf16[64,64]{1,0:T(8,128)(2,1)S(1)}, u32[]{:S(2)}, u32[]{:S(2)}) collective-permute-start(bf16[64,64]{1,0:T(8,128)(2,1)S(1)} %get-tuple-element.12), channel_id=1, source_target_pairs={{0,2},{1,3},{2,0},{3,1},{4,6},{5,7},{6,4},{7,5},{8,10},{9,11},{10,... | collective-permute-start | bytes 24584 | tf_op jit(solution)/shard_map/ppermute | solution.py:320
  35.8 5.1 %collective-permute-start.10 = (bf16[64,64]{1,0:T(8,128)(2,1)S(1)}, bf16[64,64]{1,0:T(8,128)(2,1)S(1)}, u32[]{:S(2)}, u32[]{:S(2)}) collective-permute-start(bf16[64,64]{1,0:T(8,128)(2,1)S(1)} %get-tuple-element.12), channel_id=1, source_target_pairs={{0,3},{1,2},{2,1},{3,0},{4,7},{5,6},{6,5},{7,4},{8,11},{9,10},{10,... | collective-permute-start | bytes 24584 | tf_op jit(solution)/shard_map/ppermute | solution.py:320
  41.0 3.5 %copy-start = (bf16[256,8192]{1,0:T(8,128)(2,1)S(1)}, bf16[256,8192]{1,0:T(8,128)(2,1)}, u32[]{:S(2)}) copy-start(bf16[256,8192]{1,0:T(8,128)(2,1)} %w_ref.1) | copy-start | bytes 12582916
  44.5 11.2 %copy-start.7 = (s32[8]{0:T(128)S(1)}, s32[8]{0:T(128)}, u32[]{:S(2)}) copy-start(s32[8]{0:T(128)} %param.15) | copy-start | bytes 100
  44.5 18.6 %copy-start.6 = (s32[4]{0:T(128)S(1)}, s32[4]{0:T(128)}, u32[]{:S(2)}) copy-start(s32[4]{0:T(128)} %constant.233.clone) | copy-start | bytes 52
  46.2 22.4 %collective-permute-start.16 = (bf16[32,8192]{1,0:T(8,128)(2,1)}, bf16[32,8192]{1,0:T(8,128)(2,1)}, u32[]{:S(2)}, u32[]{:S(2)}) collective-permute-start(bf16[32,8192]{1,0:T(8,128)(2,1)} %slice.46), channel_id=1, source_target_pairs={{0,1},{1,0},{2,3},{3,2},{4,5},{5,4},{6,7},{7,6},{8,9},{9,8},{10,11... | collective-permute-start | bytes 1572872 | tf_op jit(solution)/shard_map/ppermute | solution.py:334
  47.3 15.9 %all-to-all-start = ((bf16[16,8,256]{2,1,0:T(8,128)(2,1)}), bf16[16,8,256]{2,1,0:T(8,128)(2,1)S(1)}, u32[]{:S(2)}, u32[]{:S(2)}) async-start(bf16[16,8,256]{2,1,0:T(8,128)(2,1)} %broadcast_in_dim.135), calls=%async_computation | async-start | bytes 131072 | tf_op jit(solution)/shard_map/all_to_all | solution.py:316
  64.7 14.8 %all-to-all-start.1 = ((f32[16,16,384]{2,1,0:T(8,128)}), f32[16,16,384]{2,1,0:T(8,128)S(1)}, u32[]{:S(2)}, u32[]{:S(2)}) async-start(f32[16,16,384]{2,1,0:T(8,128)} %broadcast_in_dim.138), calls=%async_computation.1 | async-start | bytes 786432 | tf_op jit(solution)/shard_map/all_to_all | solution.py:328
  79.6 2.2 %copy-start.1 = (bf16[256,8192]{1,0:T(8,128)(2,1)S(1)}, bf16[256,8192]{1,0:T(8,128)(2,1)}, u32[]{:S(2)}) copy-start(bf16[256,8192]{1,0:T(8,128)(2,1)} %w_ref.1) | copy-start | bytes 12582916
  82.4 21.5 %copy-start.5 = (bf16[1,1,4,8192]{3,2,1,0:T(4,128)(2,1)S(1)}, bf16[1,1,4,8192]{3,2,1,0:T(4,128)(2,1)}, u32[]{:S(2)}) copy-start(bf16[1,1,4,8192]{3,2,1,0:T(4,128)(2,1)} %param.9) | copy-start | bytes 196612
  82.5 6.8 %collective-permute-start.11 = (bf16[2,8192]{1,0:T(2,128)(2,1)S(1)}, bf16[2,8192]{1,0:T(2,128)(2,1)S(1)}, u32[]{:S(2)}, u32[]{:S(2)}) collective-permute-start(bf16[2,8192]{1,0:T(2,128)(2,1)S(1)} %slice.44), channel_id=1, source_target_pairs={{0,1},{1,0},{2,3},{3,2},{4,5},{5,4},{6,7},{7,6},{8,9},{9,8},{10,11... | collective-permute-start | bytes 98312 | tf_op jit(solution)/shard_map/ppermute | solution.py:349
  85.1 6.4 %collective-permute-start.17 = (bf16[8,8192]{1,0:T(8,128)(2,1)S(1)}, bf16[8,8192]{1,0:T(8,128)(2,1)S(1)}, u32[]{:S(2)}, u32[]{:S(2)}) collective-permute-start(bf16[8,8192]{1,0:T(8,128)(2,1)S(1)} %get-tuple-element.20), channel_id=1, source_target_pairs={{0,4},{1,5},{2,6},{3,7},{4,8},{5,9},{6,10},{7,11},{8,12},{9,13},{1... | collective-permute-start | bytes 393224 | tf_op jit(solution)/shard_map/ppermute | solution.py:338
  86.7 8.2 %collective-permute-start.18 = (bf16[8,8192]{1,0:T(8,128)(2,1)S(1)}, bf16[8,8192]{1,0:T(8,128)(2,1)S(1)}, u32[]{:S(2)}, u32[]{:S(2)}) collective-permute-start(bf16[8,8192]{1,0:T(8,128)(2,1)S(1)} %get-tuple-element.22), channel_id=1, source_target_pairs={{0,8},{1,9},{2,10},{3,11},{4,12},{5,13},{6,14},{7,15},{8,0},{9,1},... | collective-permute-start | bytes 393224 | tf_op jit(solution)/shard_map/ppermute | solution.py:338
  88.5 6.5 %collective-permute-start.19 = (bf16[8,8192]{1,0:T(8,128)(2,1)S(1)}, bf16[8,8192]{1,0:T(8,128)(2,1)S(1)}, u32[]{:S(2)}, u32[]{:S(2)}) collective-permute-start(bf16[8,8192]{1,0:T(8,128)(2,1)S(1)} %get-tuple-element.21), channel_id=1, source_target_pairs={{0,12},{1,13},{2,14},{3,15},{4,0},{5,1},{6,2},{7,3},{8,4},{9,5},{1... | collective-permute-start | bytes 393224 | tf_op jit(solution)/shard_map/ppermute | solution.py:338
  89.3 7.4 %collective-permute-start.12 = (bf16[2,8192]{1,0:T(2,128)(2,1)S(1)}, bf16[2,8192]{1,0:T(2,128)(2,1)S(1)}, u32[]{:S(2)}, u32[]{:S(2)}) collective-permute-start(bf16[2,8192]{1,0:T(2,128)(2,1)S(1)} %add_convert_fusion.3), channel_id=1, source_target_pairs={{0,2},{1,3},{2,0},{3,1},{4,6},{5,7},{6,4},{7,5},{8,10},{9,11},{10,... | collective-permute-start | bytes 98312 | tf_op jit(solution)/shard_map/ppermute | solution.py:350
  95.0 5.9 %collective-permute-start.20 = (bf16[4,8192]{1,0:T(4,128)(2,1)S(1)}, bf16[4,8192]{1,0:T(4,128)(2,1)S(1)}, u32[]{:S(2)}, u32[]{:S(2)}) collective-permute-start(bf16[4,8192]{1,0:T(4,128)(2,1)S(1)} %slice.52), channel_id=1, source_target_pairs={{0,2},{1,3},{2,0},{3,1},{4,6},{5,7},{6,4},{7,5},{8,10},{9,11},{10,... | collective-permute-start | bytes 196616 | tf_op jit(solution)/shard_map/ppermute | solution.py:344
  96.7 4.4 %collective-permute-start.13 = (bf16[2,8192]{1,0:T(2,128)(2,1)S(1)}, bf16[2,8192]{1,0:T(2,128)(2,1)S(1)}, u32[]{:S(2)}, u32[]{:S(2)}) collective-permute-start(bf16[2,8192]{1,0:T(2,128)(2,1)S(1)} %add_convert_fusion.2), channel_id=1, source_target_pairs={{0,4},{1,5},{2,6},{3,7},{4,8},{5,9},{6,10},{7,11},{8,12},{9,13},{1... | collective-permute-start | bytes 98312 | tf_op jit(solution)/shard_map/ppermute | solution.py:351
  98.5 4.3 %collective-permute-start.14 = (bf16[2,8192]{1,0:T(2,128)(2,1)S(1)}, bf16[2,8192]{1,0:T(2,128)(2,1)S(1)}, u32[]{:S(2)}, u32[]{:S(2)}) collective-permute-start(bf16[2,8192]{1,0:T(2,128)(2,1)S(1)} %add_convert_fusion.2), channel_id=1, source_target_pairs={{0,8},{1,9},{2,10},{3,11},{4,12},{5,13},{6,14},{7,15},{8,0},{9,1},... | collective-permute-start | bytes 98312 | tf_op jit(solution)/shard_map/ppermute | solution.py:351
  100.7 3.1 %collective-permute-start.15 = (bf16[2,8192]{1,0:T(2,128)(2,1)S(1)}, bf16[2,8192]{1,0:T(2,128)(2,1)S(1)}, u32[]{:S(2)}, u32[]{:S(2)}) collective-permute-start(bf16[2,8192]{1,0:T(2,128)(2,1)S(1)} %add_convert_fusion.2), channel_id=1, source_target_pairs={{0,12},{1,13},{2,14},{3,15},{4,0},{5,1},{6,2},{7,3},{8,4},{9,5},{1... | collective-permute-start | bytes 98312 | tf_op jit(solution)/shard_map/ppermute | solution.py:351

commit v2 on v1

v2 whole, which is shorter than its diff:
```python
import functools
import math

import jax
import jax.numpy as jnp
from jax import lax
from jax.experimental import pallas as pl
from jax.experimental.pallas import tpu as pltpu
from jax.sharding import PartitionSpec as P

HD = 128
STEPS = 2
XN = 4
NEG = -math.inf
F32 = jnp.float32
BF16 = jnp.bfloat16
VMEM = pl.BlockSpec(memory_space=pltpu.VMEM)
COST = pl.CostEstimate(flops=1, bytes_accessed=1, transcendentals=0)

CORE = [(i, i ^ 1) for i in range(16)]
YHI = [(i, i ^ 2) for i in range(16)]
BOTH = [(i, i ^ 3) for i in range(16)]


def xshift(k):
    return [(i, (i + 4 * k) % 16) for i in range(16)]


def after(value, *others):
    return lax.optimization_barrier((value,) + others)[0]


def norm_kernel(own_ref, beside_ref, gain_ref, out_ref):
    floated = jnp.concatenate([own_ref[...].astype(F32), beside_ref[...].astype(F32)], 0)
    spread = jnp.mean(floated * floated, axis=-1, keepdims=True)
    out_ref[...] = (floated * lax.rsqrt(spread + 1e-05) * gain_ref[...]).astype(BF16)


def norm(own, beside, gain):
    return pl.pallas_call(
        norm_kernel,
        cost_estimate=COST,
        out_shape=jax.ShapeDtypeStruct((2 * own.shape[0], own.shape[1]), BF16),
        in_specs=[VMEM, VMEM, VMEM],
        out_specs=VMEM,
    )(own, beside, gain[None, :])


def fetch_kernel(source_ref, out_ref, sem):
    copy = pltpu.make_async_copy(source_ref, out_ref, sem)
    copy.start()
    copy.wait()


def fetch(weights):
    return pl.pallas_call(
        fetch_kernel,
        cost_estimate=COST,
        out_shape=jax.ShapeDtypeStruct(weights.shape, weights.dtype),
        in_specs=[pl.BlockSpec(memory_space=pltpu.HBM)],
        out_specs=VMEM,
        scratch_shapes=[pltpu.SemaphoreType.DMA],
        compiler_params=pltpu.CompilerParams(vmem_limit_bytes=8 * 1024 * 1024),
    )(weights)


def turn(value, cosine, sine, axis):
    size = value.shape[axis]
    index = lax.broadcasted_iota(jnp.int32, value.shape, axis)
    ahead = pltpu.roll(value, size - 1, axis)
    behind = pltpu.roll(value, 1, axis)
    return value * cosine + jnp.where(index % 2 == 0, ahead, behind) * sine


def project_kernel(
    own_ref, mate_ref, wq_ref, wkv_ref, cq_ref, sq_ref, ck_ref, sk_ref, perm_ref,
    q_ref, pack_ref,
):
    rows = jnp.concatenate([own_ref[...], mate_ref[...]], 0)
    query = jnp.dot(rows, wq_ref[...], preferred_element_type=F32)
    fresh = lax.dot_general(
        wkv_ref[...], rows, (((1,), (1,)), ((), ())), preferred_element_type=F32
    )
    perm = perm_ref[...]
    query = turn(query, cq_ref[...], sq_ref[...], 1).astype(BF16)
    query = jnp.dot(perm, query, preferred_element_type=F32)
    q_ref[...] = query.astype(BF16)
    fresh = turn(fresh, ck_ref[...], sk_ref[...], 0).astype(BF16)
    fresh = lax.dot_general(fresh, perm, (((1,), (1,)), ((), ())), preferred_element_type=F32)
    size = fresh.shape[0]
    pack_ref[:size, :] = jnp.concatenate([fresh, jnp.zeros_like(fresh)], 1).astype(BF16)
    lead = lead_rows(query[:, :HD], query[:, HD:])
    pack_ref[size:, :] = jnp.concatenate([lead, jnp.zeros_like(lead)], 0).astype(BF16)


def lead_rows(first, second):
    both = jnp.concatenate([first[:STEPS], second[:STEPS]], 0)
    return jnp.concatenate([both, jnp.zeros_like(both)], 0)


def project(own, mate, w_query, w_kv_t, cq, sq, ck, sk, perm):
    rows = 2 * own.shape[0]
    return pl.pallas_call(
        project_kernel,
        cost_estimate=COST,
        out_shape=(
            jax.ShapeDtypeStruct((rows, w_query.shape[1]), BF16),
            jax.ShapeDtypeStruct((w_kv_t.shape[0] + 16, HD), BF16),
        ),
        in_specs=[VMEM] * 9,
        out_specs=(VMEM,) * 2,
        compiler_params=pltpu.CompilerParams(vmem_limit_bytes=16 * 1024 * 1024),
    )(own, mate, w_query, w_kv_t, cq, sq, ck, sk, perm)


def softmax_parts(queries, bounds, kv_refs, fresh, scores):
    tokens = kv_refs[0].shape[1]
    chunk = 512
    scale = 1.0 / math.sqrt(HD)
    low, high, fresh_low, fresh_high = bounds

    def pair(first, span):
        return jnp.concatenate([kv_refs[first][:, span], kv_refs[first + 1][:, span]], 0)

    fresh_keys = jnp.concatenate(fresh[:2], 0)
    fresh_values = jnp.concatenate(fresh[2:], 0)
    fresh_scores = jnp.dot(queries, fresh_keys, preferred_element_type=F32) * scale
    index = lax.broadcasted_iota(jnp.int32, fresh_scores.shape, 1)
    fresh_scores = jnp.where((index >= fresh_low) & (index <= fresh_high), fresh_scores, NEG)
    peak = jnp.max(fresh_scores, -1, keepdims=True)
    for start in range(0, tokens, chunk):
        span = slice(start, start + chunk)
        part_scores = jnp.dot(queries, pair(0, span), preferred_element_type=F32) * scale
        index = lax.broadcasted_iota(jnp.int32, part_scores.shape, 1) + start
        part_scores = jnp.where((index >= low) & (index < high), part_scores, NEG)
        scores[:, span] = part_scores
        peak = jnp.maximum(peak, jnp.max(part_scores, -1, keepdims=True))
    contract = (((1,), (1,)), ((), ()))
    weights = jnp.exp(fresh_scores - peak)
    total = jnp.sum(weights, -1, keepdims=True)
    mixed = lax.dot_general(
        weights.astype(BF16), fresh_values, contract, preferred_element_type=F32
    )
    for start in range(0, tokens, chunk):
        span = slice(start, start + chunk)
        weights = jnp.exp(scores[:, span] - peak)
        total += jnp.sum(weights, -1, keepdims=True)
        mixed += lax.dot_general(
            weights.astype(BF16), pair(2, span), contract, preferred_element_type=F32
        )
    return mixed, peak, total


def pack_parts(mixed, peak, total):
    lane = lax.broadcasted_iota(jnp.int32, mixed.shape, 1)
    return jnp.concatenate([mixed, jnp.where(lane < HD // 2, peak, total)], 1)


def in_order(place, held):
    return [held[place ^ part] for part in range(4)]


def attend_kernel(me_ref, q_ref, bounds_ref, *refs):
    kv_refs, pack_refs, asked = refs[:4], refs[4:6], refs[6:10]
    out_ref, lead_ref = refs[10:12]
    answers = refs[12:16]
    scores = refs[16]
    size = kv_refs[0].shape[0]
    other = pack_refs[0].shape[0] // 2

    def body(place):
        query = q_ref[...]
        rows = query.shape[0]
        held = [ref[first : first + size, :rows] for ref in pack_refs for first in (0, other)]
        far = []
        for ref in asked:
            both = ref[...].astype(F32)
            far += [both[:4], both[16:20]]
        far = jnp.concatenate(far, 0).astype(BF16)
        bounds = bounds_ref[...]
        mixed, peak, total = softmax_parts(
            jnp.concatenate([query[:, :HD], query[:, HD:], far], 0),
            [bounds[:, i : i + 1] for i in range(4)],
            in_order(place, kv_refs),
            in_order(place, held),
            scores,
        )
        ready = mixed / total
        out_ref[...] = jnp.concatenate([ready[:rows], ready[rows : 2 * rows]], 1).astype(BF16)
        packed = pack_parts(mixed, peak, total)
        lead_ref[...] = lead_rows(packed[:8], packed[rows : rows + 8])
        for i, ref in enumerate(answers):
            ref[...] = packed[2 * rows + 8 * i : 2 * rows + 8 * i + 8]

    for place in range(4):
        pl.when(me_ref[0] == place)(functools.partial(body, place))


SMEM = pl.BlockSpec(memory_space=pltpu.SMEM)
LIMIT = pltpu.CompilerParams(vmem_limit_bytes=16 * 1024 * 1024)


def attend(me, query, bounds, kv, packs, asked):
    packed = jax.ShapeDtypeStruct((8, 2 * HD), F32)
    return pl.pallas_call(
        attend_kernel,
        cost_estimate=COST,
        out_shape=(jax.ShapeDtypeStruct(query.shape, BF16), packed) + (packed,) * 4,
        in_specs=[SMEM] + [VMEM] * 12,
        out_specs=(VMEM,) * 6,
        scratch_shapes=[pltpu.VMEM((bounds.shape[0], kv[0].shape[1]), F32)],
        compiler_params=LIMIT,
    )(me, query, bounds, *kv, *packs, *asked)


def merge_kernel(flags_ref, attended_ref, own_ref, far_ref, mate_ref, perm_ref, keep_ref, give_ref):
    own = own_ref[...]
    far = jnp.where(flags_ref[1] == 1, far_ref[:4], mate_ref[4:])
    far = jnp.concatenate([far, far], 0)
    split = lambda packed: (
        packed[:, :HD], packed[:, HD : HD + 1], packed[:, 2 * HD - 1 : 2 * HD]
    )
    mixed_a, peak_a, total_a = split(own)
    mixed_b, peak_b, total_b = split(far)
    peak = jnp.maximum(peak_a, peak_b)
    scale_a = jnp.exp(peak_a - peak)
    scale_b = jnp.exp(peak_b - peak)
    ready = (mixed_a * scale_a + mixed_b * scale_b) / (total_a * scale_a + total_b * scale_b)
    ready = jnp.concatenate([ready[:STEPS], ready[STEPS : 2 * STEPS]], 1)
    attended = attended_ref[...]
    rows = attended.shape[0]
    lead = jnp.concatenate([ready] + [jnp.zeros_like(ready)] * (rows // STEPS - 1), 0)
    row = lax.broadcasted_iota(jnp.int32, lead.shape, 0)
    swap = (row < STEPS) & (flags_ref[0] == 1)
    attended = jnp.where(swap, lead, attended.astype(F32)).astype(BF16)
    attended = lax.dot_general(
        perm_ref[...], attended, (((0,), (0,)), ((), ())), preferred_element_type=F32
    ).astype(BF16)
    keep_ref[...] = attended[: rows // 2]
    give_ref[...] = attended[rows // 2 :]


def merge(flags, attended, own, far, mate, perm):
    rows, columns = attended.shape
    return pl.pallas_call(
        merge_kernel,
        cost_estimate=COST,
        out_shape=(jax.ShapeDtypeStruct((rows // 2, columns), BF16),) * 2,
        in_specs=[SMEM] + [VMEM] * 5,
        out_specs=(VMEM,) * 2,
    )(flags, attended, own, far, mate, perm)


def add_core_kernel(own_ref, across_ref, *out_refs):
    total = (own_ref[...].astype(F32) + across_ref[...].astype(F32)).astype(BF16)
    width = total.shape[0] // len(out_refs)
    for i, ref in enumerate(out_refs):
        ref[...] = total[i * width : (i + 1) * width]


def add_core(own, across):
    rows, columns = own.shape
    return pl.pallas_call(
        add_core_kernel,
        cost_estimate=COST,
        out_shape=(jax.ShapeDtypeStruct((rows // XN, columns), BF16),) * XN,
        in_specs=[VMEM, VMEM],
        out_specs=(VMEM,) * XN,
        compiler_params=LIMIT,
    )(own, across)


def add_x_kernel(a_ref, b_ref, c_ref, d_ref, own_ref, send_ref):
    total = a_ref[...].astype(F32)
    for ref in (b_ref, c_ref, d_ref):
        total = total + ref[...].astype(F32)
    half = total.shape[0] // 2
    own_ref[...] = total[:half]
    send_ref[...] = total[half:].astype(BF16)


def add_x(parts):
    rows, columns = parts[0].shape
    return pl.pallas_call(
        add_x_kernel,
        cost_estimate=COST,
        out_shape=(
            jax.ShapeDtypeStruct((rows // 2, columns), F32),
            jax.ShapeDtypeStruct((rows // 2, columns), BF16),
        ),
        in_specs=[VMEM] * 4,
        out_specs=(VMEM,) * 2,
    )(*parts)


def pick_row(table, selector):
    return jnp.sum(jnp.where(selector, table[None, :], 0), 1)


DISTANCES = ((3, 4), (-2, -3), (1, 2), (0, -1))


def carry(distances, groups, count, back):
    route = []
    for group in range(groups):
        for tp in range(count):
            far = (group + distances[tp % 2]) % groups
            asking = (groups + group) * count + tp
            asked = far * count + tp
            route.append((asked, asking) if back else (asking, asked))
    return route


def local(hidden, norm_gain, w_query, w_keyval, w_out, kv_cache, match, cache_lengths):
    side = lax.axis_index("role")
    group = lax.axis_index("grp")
    tp = lax.axis_index("tp")
    groups = lax.axis_size("grp")
    count = lax.axis_size("tp")
    own_rows = hidden[0, 0]
    block = own_rows.shape[0]
    row_count = block * count
    kv_t = kv_cache[0, 0].T
    cache_len = kv_t.shape[1]
    qcols = w_query.shape[1]
    kcols = w_keyval.shape[1]

    beside = lax.ppermute(own_rows, "tp", YHI)
    kv_y = lax.ppermute(kv_t, "tp", YHI)
    kv_core = lax.ppermute(kv_t, "tp", CORE)
    pair = norm(own_rows, beside, norm_gain)
    others = [lax.ppermute(pair, "tp", xshift(-k)) for k in range(1, XN)]
    w_query = fetch(after(w_query, pair))
    others = after(others, w_query, kv_core)
    own_half = jnp.concatenate([pair] + others, 0)
    mate_half = after(lax.ppermute(own_half, "tp", CORE), kv_y)
    kv_both = lax.ppermute(kv_y, "tp", CORE)

    slot = jnp.arange(row_count, dtype=jnp.int32)
    piece = slot // block
    far_core, far_x, far_y = piece // 8, piece // 2 % XN, piece % 2
    owner = (
        (tp // 4 + far_x) % XN * 4
        + jnp.bitwise_xor(tp // 2 % 2, far_y) * 2
        + jnp.bitwise_xor(tp % 2, far_core)
    )
    row_at = owner * block + slot % block
    row_ids = jnp.arange(row_count, dtype=jnp.int32)
    placed = row_at[None, :] == row_ids[:, None]
    perm = placed.astype(BF16)

    request = row_ids // STEPS
    step_ids = row_ids % STEPS
    lengths = cache_lengths[0]
    zero_one = jnp.zeros((1,), jnp.int32)
    bases = jnp.concatenate([jnp.full((1,), cache_len + row_count, jnp.int32), lengths])
    before = jnp.arange(lengths.shape[0])[None, :] < jnp.arange(lengths.shape[0])[:, None]
    offsets = pick_row(lengths, before)
    selector = request[:, None] == jnp.arange(row_count // STEPS, dtype=jnp.int32)[None, :]
    start = pick_row(jnp.concatenate([zero_one, offsets]), selector)
    span = pick_row(jnp.concatenate([zero_one, lengths]), selector)
    positions = jnp.where(side == 0, cache_len + row_ids, pick_row(bases, selector) + step_ids)
    low = jnp.where(side == 0, 0, start)
    high = jnp.where(side == 0, cache_len, start + span)
    fresh_low = jnp.where(side == 0, 0, request * STEPS)
    bounds = jnp.stack([low, high, fresh_low, row_ids], 1)
    whole = jnp.array([0, cache_len, 0, row_count - 1], jnp.int32)
    bounds = jnp.concatenate([bounds, bounds, jnp.broadcast_to(whole[None, :], (32, 4))], 0)

    position_at = jnp.sum(jnp.where(placed, positions[:, None], 0), 0).astype(F32)
    column = jnp.arange(qcols, dtype=jnp.int32)
    inverse = 500000.0 ** (-(2.0 / HD) * (column % HD // 2).astype(F32))
    angles = position_at[:, None] * inverse[None, :]
    cq = jnp.cos(angles)
    sq = jnp.sin(angles) * jnp.where(column % 2 == 0, -1.0, 1.0)[None, :]
    column = tp * kcols + jnp.arange(kcols, dtype=jnp.int32)
    inverse = 500000.0 ** (-(2.0 / HD) * (column % HD // 2).astype(F32))
    angles = inverse[:, None] * position_at[None, :]
    is_key = (column // HD % 2 == 0)[:, None]
    ck = jnp.where(is_key, jnp.cos(angles), 1.0)
    sk = jnp.where(is_key, jnp.sin(angles) * jnp.where(column % 2 == 0, -1.0, 1.0)[:, None], 0.0)

    query, pack = project(own_half, mate_half, w_query, w_keyval.T, cq, sq, ck, sk, perm)

    mate_pack = lax.ppermute(pack, "tp", CORE)
    packs = jnp.concatenate([pack, mate_pack], 0)
    leads = after(jnp.concatenate([pack[kcols:], mate_pack[kcols:]], 0), kv_both)
    axes = ("role", "grp", "tp")
    asked = [lax.ppermute(leads, axes, carry(d, groups, count, False)) for d in DISTANCES]
    packs = [packs, lax.ppermute(after(packs, leads), "tp", YHI)]
    kv = [kv_t, kv_core, kv_y, kv_both]
    me = jnp.reshape(tp % 4, (1,)).astype(jnp.int32)
    attended, lead_own, *answers = attend(me, query, bounds, kv, packs, asked)
    answers = [
        lax.ppermute(answer, axes, carry(d, groups, count, True))
        for answer, d in zip(answers, DISTANCES)
    ]

    far = jnp.zeros_like(answers[0])
    here = jnp.zeros((), jnp.bool_)
    for answer, pair_of in zip(answers, DISTANCES):
        distance = jnp.where(tp % 2 == 0, pair_of[0], pair_of[1])
        valid = jnp.sum(
            jnp.where(jnp.arange(groups) == (group + distance) % groups, match, 0)
        ) == group
        far = jnp.where(valid, answer, far)
        here = here | valid
    mate = lax.ppermute(far, "tp", CORE)
    flags = jnp.stack([side, here.astype(jnp.int32)])
    own_att, mate_att = merge(flags, attended, lead_own, far, mate, perm)

    give = jnp.dot(mate_att, w_out, preferred_element_type=F32).astype(BF16)
    across = lax.ppermute(give, "tp", CORE)
    keep = jnp.dot(own_att, w_out, preferred_element_type=F32).astype(BF16)
    parts = add_core(keep, across)
    parts = [parts[0]] + [lax.ppermute(parts[k], "tp", xshift(k)) for k in range(1, XN)]
    summed, send = add_x(parts)
    summed = summed + lax.ppermute(send, "tp", YHI).astype(F32)
    return (own_rows.astype(F32) + summed).astype(BF16)[None, None]


def solution(mesh):
    return jax.shard_map(
        local,
        mesh=mesh,
        in_specs=(
            P("role", "grp", "tp", None),
            P(),
            P(None, "tp"),
            P(None, "tp"),
            P("tp", None),
            P("role", "grp", None, "tp"),
            P(),
            P("grp", None),
        ),
        out_specs=P("role", "grp", "tp", None),
        check_vma=False,
    )
```

time: 106 us -> 101 us (0.953)
  the two profiles are of different devices: /device:TPU:1 before, /device:TPU:24 now
where the time goes in v2:
time: 101 us; the launch traced here: 100 us
  waiting for transfers between devices  40 us (40%)
  starting transfers between devices  33.2 us (33%)
  Pallas kernels  8.8 us (9%)
  local copies, waits for them, and re-layouts  6.14 us (6%)
  other arithmetic  5.37 us (5%)
  matrix products  4.01 us (4%)
  between operations  2.88 us (3%)
    ppermute x4, starting transfers between devices, local(): lax.ppermute(leads, axes, carry(d, groups, count, False))  12.3 us
    ppermute x1, waiting for transfers between devices, local(): beside = lax.ppermute(own_rows, 'tp', YHI)  11.9 us
    ppermute x3, waiting for transfers between devices, local(): lax.ppermute(parts[k], 'tp', xshift(k))  6.95 us
    unnamed x39, local copies, waits for them, and re-layouts  5.95 us
    ppermute x4, starting transfers between devices, local(): lax.ppermute(answer, axes, carry(d, groups, count, True))  5.16 us
    ppermute x3, waiting for transfers between devices, local(): others = [lax.ppermute(pair, 'tp', xshift(-k)) for k in range(1, XN)]  5.13 us
    ppermute x1, waiting for transfers between devices, local(): summed = summed + lax.ppermute(send, 'tp', YHI).astype(F32)  4.85 us
    ppermute x3, starting transfers between devices, local(): others = [lax.ppermute(pair, 'tp', xshift(-k)) for k in range(1, XN)]  4.44 us
  transfers between devices with their start and end apart: 24, of which 14 were waited for; matrix products, arithmetic and copies ran while one was open for 5% of the time, Pallas kernels for 3%

profile of v2, /device:TPU:24, one launch (start us, length us, event | category | flops | bytes accessed | tf_op | source)
XLA Modules:
  0.0 100.5 jit_solution(1721105034377392245)
XLA Ops:
  0.0 1.2 %collective-permute-start.6 = (bf16[64,4096]{1,0:T(8,128)(2,1)}, bf16[64,4096]{1,0:T(8,128)(2,1)S(1)}, u32[]{:S(2)}, u32[]{:S(2)}) collective-permute-start(bf16[64,4096]{1,0:T(8,128)(2,1)} %bitcast.23), channel_id=1, source_target_pairs={{0,2},{1,3},{2,0},{3,1},{4,6},{5,7},{6,4},{7,5},{8,10},{9,11},{10,... | collective-permute-start | bytes 1572872 | tf_op jit(solution)/shard_map/ppermute | solution.py:329
  1.2 2.3 %collective-permute-start = (bf16[4,8192]{1,0:T(4,128)(2,1)}, bf16[4,8192]{1,0:T(4,128)(2,1)S(1)}, u32[]{:S(2)}, u32[]{:S(2)}) collective-permute-start(bf16[4,8192]{1,0:T(4,128)(2,1)} %bitcast.25), channel_id=1, source_target_pairs={{0,2},{1,3},{2,0},{3,1},{4,6},{5,7},{6,4},{7,5},{8,10},{9,11},{10,... | collective-permute-start | bytes 196616 | tf_op jit(solution)/shard_map/ppermute | solution.py:328
  3.6 0.8 select_reduce_fusion.3
  4.4 0.7 pad_add_fusion.4
  5.1 0.1 select_reduce_fusion.1
  5.3 0.1 select_reduce_fusion
  5.4 0.2 fusion.4
  5.6 11.9 %collective-permute-done.beside_ref = bf16[4,8192]{1,0:T(4,128)(2,1)S(1)} collective-permute-done((bf16[4,8192]{1,0:T(4,128)(2,1)}, bf16[4,8192]{1,0:T(4,128)(2,1)S(1)}, u32[]{:S(2)}, u32[]{:S(2)}) %collective-permute-start) | collective-permute-done | bytes 65568 | tf_op jit(solution)/shard_map/ppermute | solution.py:328
  17.5 0.6 copy-done.13
  18.1 1.7 %shard_map.91 = bf16[8,8192]{1,0:T(8,128)(2,1)} custom-call(bf16[4,8192]{1,0:T(4,128)(2,1)} %bitcast.26, bf16[4,8192]{1,0:T(4,128)(2,1)} %copy-done.13, f32[1,8192]{1,0:T(1,128)} %bitcast.27), custom_call_target="tpu_custom_call" | custom-call | flops 1 | bytes 1 | tf_op jit(solution)/shard_map/pallas_call | solution.py:40
  19.8 2.8 %collective-permute-start.1 = (bf16[8,8192]{1,0:T(8,128)(2,1)}, bf16[8,8192]{1,0:T(8,128)(2,1)S(1)}, u32[]{:S(2)}, u32[]{:S(2)}) collective-permute-start(bf16[8,8192]{1,0:T(8,128)(2,1)} %shard_map.91), channel_id=1, source_target_pairs={{0,12},{1,13},{2,14},{3,15},{4,0},{5,1},{6,2},{7,3},{8,4},{9,5},{1... | collective-permute-start | bytes 393224 | tf_op jit(solution)/shard_map/ppermute | solution.py:332
  22.6 0.8 collective-permute-start.2
  23.4 0.9 collective-permute-start.3
  24.3 2.2 %copy-done = bf16[8192,256]{1,0:T(8,128)(2,1)S(1)} copy-done((bf16[8192,256]{1,0:T(8,128)(2,1)S(1)}, bf16[8192,256]{1,0:T(8,128)(2,1)}, u32[]{:S(2)}) %copy-start) | copy-done | bytes 4194328
  26.5 0.3 shard_map.92.wq_ref
  26.8 1.5 %collective-permute-done.1 = bf16[8,8192]{1,0:T(8,128)(2,1)S(1)} collective-permute-done((bf16[8,8192]{1,0:T(8,128)(2,1)}, bf16[8,8192]{1,0:T(8,128)(2,1)S(1)}, u32[]{:S(2)}, u32[]{:S(2)}) %collective-permute-start.1) | collective-permute-done | bytes 131104 | tf_op jit(solution)/shard_map/ppermute | solution.py:332
  28.3 2.2 %collective-permute-done.2 = bf16[8,8192]{1,0:T(8,128)(2,1)S(1)} collective-permute-done((bf16[8,8192]{1,0:T(8,128)(2,1)}, bf16[8,8192]{1,0:T(8,128)(2,1)S(1)}, u32[]{:S(2)}, u32[]{:S(2)}) %collective-permute-start.2) | collective-permute-done | bytes 131104 | tf_op jit(solution)/shard_map/ppermute | solution.py:332
  30.5 1.4 %collective-permute-done.3 = bf16[8,8192]{1,0:T(8,128)(2,1)S(1)} collective-permute-done((bf16[8,8192]{1,0:T(8,128)(2,1)}, bf16[8,8192]{1,0:T(8,128)(2,1)S(1)}, u32[]{:S(2)}, u32[]{:S(2)}) %collective-permute-start.3) | collective-permute-done | bytes 131104 | tf_op jit(solution)/shard_map/ppermute | solution.py:332
  32.0 0.1 collective-permute-start.5
  32.1 0.5 collective-permute-start.7
  32.6 0.3 fusion
  32.9 1.1 %collective-permute-done.5.mate_ref = bf16[32,8192]{1,0:T(8,128)(2,1)S(1)} collective-permute-done((bf16[32,8192]{1,0:T(8,128)(2,1)S(1)}, bf16[32,8192]{1,0:T(8,128)(2,1)S(1)}, u32[]{:S(2)}, u32[]{:S(2)}) %collective-permute-start.5) | collective-permute-done | bytes 524320 | tf_op jit(solution)/shard_map/ppermute | solution.py:336
  34.0 1.3 %shard_map.93 = (bf16[64,256]{1,0:T(8,128)(2,1)S(1)}, bf16[80,128]{1,0:T(8,128)(2,1)S(1)}) custom-call(bf16[32,8192]{1,0:T(8,128)(2,1)S(1)} %pad_maximum_fusion.own_ref, bf16[32,8192]{1,0:T(8,128)(2,1)S(1)} %collective-permute-done.5.mate_ref, bf16[8192,256]{1,0:T(8,128)(2,1)S(1)} %shard_map.92.wq_ref, bf16[64,8192]{1,0:T(8,128)(2,1)S(1)} %bitcast.21, ...), custom_call_target="tpu_custom_call" | custom-call | flops 1 | bytes 1 | tf_op jit(solution)/shard_map/pallas_call | solution.py:103
  35.3 0.2 collective-permute-start.8
  35.6 1.0 %collective-permute-done.8 = bf16[80,128]{1,0:T(8,128)(2,1)S(1)} collective-permute-done((bf16[80,128]{1,0:T(8,128)(2,1)S(1)}, bf16[80,128]{1,0:T(8,128)(2,1)S(1)}, u32[]{:S(2)}, u32[]{:S(2)}) %collective-permute-start.8) | collective-permute-done | bytes 20512 | tf_op jit(solution)/shard_map/ppermute | solution.py:385
  36.6 6.7 %collective-permute-start.10 = (bf16[32,128]{1,0:T(8,128)(2,1)S(1)}, bf16[32,128]{1,0:T(8,128)(2,1)S(1)}, u32[]{:S(2)}, u32[]{:S(2)}) collective-permute-start(bf16[32,128]{1,0:T(8,128)(2,1)S(1)} %pad_maximum_fusion.1), channel_id=1, source_target_pairs={{128,48},{129,65},{130,50},{131,67},{132,52},{133,69},{134,54},{13... | collective-permute-start | bytes 24584 | tf_op jit(solution)/shard_map/ppermute | solution.py:389
  43.3 3.0 %collective-permute-start.11 = (bf16[32,128]{1,0:T(8,128)(2,1)S(1)}, bf16[32,128]{1,0:T(8,128)(2,1)S(1)}, u32[]{:S(2)}, u32[]{:S(2)}) collective-permute-start(bf16[32,128]{1,0:T(8,128)(2,1)S(1)} %pad_maximum_fusion.1), channel_id=1, source_target_pairs={{128,96},{129,81},{130,98},{131,83},{132,100},{133,85},{134,102},{... | collective-permute-start | bytes 24584 | tf_op jit(solution)/shard_map/ppermute | solution.py:389
  46.3 1.3 %collective-permute-start.12 = (bf16[32,128]{1,0:T(8,128)(2,1)S(1)}, bf16[32,128]{1,0:T(8,128)(2,1)S(1)}, u32[]{:S(2)}, u32[]{:S(2)}) collective-permute-start(bf16[32,128]{1,0:T(8,128)(2,1)S(1)} %pad_maximum_fusion.1), channel_id=1, source_target_pairs={{128,16},{129,33},{130,18},{131,35},{132,20},{133,37},{134,22},{13... | collective-permute-start | bytes 24584 | tf_op jit(solution)/shard_map/ppermute | solution.py:389
  47.6 1.3 %collective-permute-start.13 = (bf16[32,128]{1,0:T(8,128)(2,1)S(1)}, bf16[32,128]{1,0:T(8,128)(2,1)S(1)}, u32[]{:S(2)}, u32[]{:S(2)}) collective-permute-start(bf16[32,128]{1,0:T(8,128)(2,1)S(1)} %pad_maximum_fusion.1), channel_id=1, source_target_pairs={{128,0},{129,113},{130,2},{131,115},{132,4},{133,117},{134,6},{135... | collective-permute-start | bytes 24584 | tf_op jit(solution)/shard_map/ppermute | solution.py:389
  48.9 1.0 %collective-permute-start.9 = (bf16[160,128]{1,0:T(8,128)(2,1)S(1)}, bf16[160,128]{1,0:T(8,128)(2,1)S(1)}, u32[]{:S(2)}, u32[]{:S(2)}) collective-permute-start(bf16[160,128]{1,0:T(8,128)(2,1)S(1)} %constant_dynamic-update-slice_fusion.refs_4_), channel_id=1, source_target_pairs={{0,2},{1,3},{2,0},{3,1},{4,6},{5,7},{6,4},{7,5},{8,10},{9,11},{10,... | collective-permute-start | bytes 122888 | tf_op jit(solution)/shard_map/ppermute | solution.py:390
  50.0 0.1 broadcast_in_dim.142
  50.0 0.1 pad_add_fusion
  50.1 0.1 copy.13.bounds_ref
  50.3 4.4 %collective-permute-done.9.refs_5_ = bf16[160,128]{1,0:T(8,128)(2,1)S(1)} collective-permute-done((bf16[160,128]{1,0:T(8,128)(2,1)S(1)}, bf16[160,128]{1,0:T(8,128)(2,1)S(1)}, u32[]{:S(2)}, u32[]{:S(2)}) %collective-permute-start.9) | collective-permute-done | bytes 40992 | tf_op jit(solution)/shard_map/ppermute | solution.py:390
  54.8 1.8 %shard_map.94 = (bf16[64,256]{1,0:T(8,128)(2,1)S(1)}, f32[8,256]{1,0:T(8,128)S(1)}, f32[8,256]{1,0:T(8,128)S(1)}, f32[8,256]{1,0:T(8,128)S(1)}, f32[8,256]{1,0:T(8,128)S(1)}, /*index=5*/f32[8,256]{1,0:T(8,128)S(1)}) custom-call(s32[1]{0:T(128)} %bitcast.3.me_ref, bf16[64,256]{1,0:T(8,128)(2,1)S(1)} %get-tuple-element.33.q_ref, ...), custom_call_target="tpu_custom_call" | custom-call | flops 1 | bytes 1 | tf_op jit(solution)/shard_map/pallas_call | solution.py:205
  56.6 0.6 copy-done.5
  57.2 0.6 copy-done.6
  57.7 1.3 %collective-permute-start.14 = (f32[8,256]{1,0:T(8,128)S(1)}, f32[8,256]{1,0:T(8,128)S(1)}, u32[]{:S(2)}, u32[]{:S(2)}) collective-permute-start(f32[8,256]{1,0:T(8,128)S(1)} %get-tuple-element.39), channel_id=1, source_target_pairs={{0,128},{113,129},{2,130},{115,131},{4,132},{117,133},{6,134},{119... | collective-permute-start | bytes 24584 | tf_op jit(solution)/shard_map/ppermute | solution.py:395
  59.0 1.3 %collective-permute-start.15 = (f32[8,256]{1,0:T(8,128)S(1)}, f32[8,256]{1,0:T(8,128)S(1)}, u32[]{:S(2)}, u32[]{:S(2)}) collective-permute-start(f32[8,256]{1,0:T(8,128)S(1)} %get-tuple-element.40), channel_id=1, source_target_pairs={{16,128},{33,129},{18,130},{35,131},{20,132},{37,133},{22,134},{39... | collective-permute-start | bytes 24584 | tf_op jit(solution)/shard_map/ppermute | solution.py:395
  60.3 1.3 %collective-permute-start.16 = (f32[8,256]{1,0:T(8,128)S(1)}, f32[8,256]{1,0:T(8,128)S(1)}, u32[]{:S(2)}, u32[]{:S(2)}) collective-permute-start(f32[8,256]{1,0:T(8,128)S(1)} %get-tuple-element.41), channel_id=1, source_target_pairs={{96,128},{81,129},{98,130},{83,131},{100,132},{85,133},{102,134},{... | collective-permute-start | bytes 24584 | tf_op jit(solution)/shard_map/ppermute | solution.py:395
  61.6 1.3 %collective-permute-start.17 = (f32[8,256]{1,0:T(8,128)S(1)}, f32[8,256]{1,0:T(8,128)S(1)}, u32[]{:S(2)}, u32[]{:S(2)}) collective-permute-start(f32[8,256]{1,0:T(8,128)S(1)} %get-tuple-element.42), channel_id=1, source_target_pairs={{48,128},{65,129},{50,130},{67,131},{52,132},{69,133},{54,134},{71... | collective-permute-start | bytes 24584 | tf_op jit(solution)/shard_map/ppermute | solution.py:395
  62.9 0.7 fusion.13
  66.2 2.7 %collective-permute-done.16 = f32[8,256]{1,0:T(8,128)S(1)} collective-permute-done((f32[8,256]{1,0:T(8,128)S(1)}, f32[8,256]{1,0:T(8,128)S(1)}, u32[]{:S(2)}, u32[]{:S(2)}) %collective-permute-start.16) | collective-permute-done | bytes 8224 | tf_op jit(solution)/shard_map/ppermute | solution.py:395
  68.9 1.0 collective-permute-done.17
  69.9 1.0 %collective-permute-start.18 = (f32[8,256]{1,0:T(8,128)S(1)}, f32[8,256]{1,0:T(8,128)S(1)}, u32[]{:S(2)}, u32[]{:S(2)}) collective-permute-start(f32[8,256]{1,0:T(8,128)S(1)} %select_select_fusion.far_ref), channel_id=1, source_target_pairs={{0,1},{1,0},{2,3},{3,2},{4,5},{5,4},{6,7},{7,6},{8,9},{9,8},{10,11... | collective-permute-start | bytes 24584 | tf_op jit(solution)/shard_map/ppermute | solution.py:408
  70.9 0.6 pad_add_fusion.3.flags_ref
  71.5 0.2 collective-permute-done.18.mate_ref
  71.8 0.6 copy-done.16
  72.3 1.7 %shard_map.95 = (bf16[32,256]{1,0:T(8,128)(2,1)}, bf16[32,256]{1,0:T(8,128)(2,1)}) custom-call(s32[2]{0:T(128)} %pad_add_fusion.3.flags_ref, bf16[64,256]{1,0:T(8,128)(2,1)} %copy-done.5, f32[8,256]{1,0:T(8,128)} %copy-done.6, f32[8,256]{1,0:T(8,128)} %copy-done.14, f32[8,256]{1,0:T(8,128)} %copy-done.16, bf16[64,64]{1,0:T(8,128)(2,1)} %copy-done.3), custom_call_target="tpu_custom_call" | custom-call | flops 1 | bytes 1 | tf_op jit(solution)/shard_map/pallas_call | solution.py:245
  74.0 3.2 %convolution_convert_fusion = bf16[32,8192]{1,0:T(8,128)(2,1)S(1)} fusion(bf16[32,256]{1,0:T(8,128)(2,1)} %get-tuple-element.44, bf16[256,8192]{1,0:T(8,128)(2,1)} %param.13), kind=kOutput, calls=%fused_computation | convolution fusion | flops 134479872 | bytes 4734976 | tf_op jit(solution)/shard_map/dot_general | solution.py:412
  77.2 0.4 collective-permute-start.19
  77.7 0.8 convolution_convert_fusion.1.own_ref
  78.5 0.7 collective-permute-done.19.across_ref
  79.2 0.1 shard_map.96
  79.4 0.6 copy-done.4
  80.0 2.0 %collective-permute-start.21 = (bf16[8,8192]{1,0:T(8,128)(2,1)S(1)}, bf16[8,8192]{1,0:T(8,128)(2,1)S(1)}, u32[]{:S(2)}, u32[]{:S(2)}) collective-permute-start(bf16[8,8192]{1,0:T(8,128)(2,1)S(1)} %get-tuple-element.47), channel_id=1, source_target_pairs={{0,8},{1,9},{2,10},{3,11},{4,12},{5,13},{6,14},{7,15},{8,0},{9,1},... | collective-permute-start | bytes 393224 | tf_op jit(solution)/shard_map/ppermute | solution.py:416
  82.0 1.4 %collective-permute-start.22 = (bf16[8,8192]{1,0:T(8,128)(2,1)S(1)}, bf16[8,8192]{1,0:T(8,128)(2,1)S(1)}, u32[]{:S(2)}, u32[]{:S(2)}) collective-permute-start(bf16[8,8192]{1,0:T(8,128)(2,1)S(1)} %get-tuple-element.48), channel_id=1, source_target_pairs={{0,12},{1,13},{2,14},{3,15},{4,0},{5,1},{6,2},{7,3},{8,4},{9,5},{1... | collective-permute-start | bytes 393224 | tf_op jit(solution)/shard_map/ppermute | solution.py:416
  83.5 6.3 %collective-permute-done.20.b_ref = bf16[8,8192]{1,0:T(8,128)(2,1)S(1)} collective-permute-done((bf16[8,8192]{1,0:T(8,128)(2,1)S(1)}, bf16[8,8192]{1,0:T(8,128)(2,1)S(1)}, u32[]{:S(2)}, u32[]{:S(2)}) %collective-permute-start.20) | collective-permute-done | bytes 131104 | tf_op jit(solution)/shard_map/ppermute | solution.py:416
  89.8 0.6 collective-permute-done.22.d_ref
  90.5 0.6 copy-done.12
  91.1 1.8 %shard_map.97 = (f32[4,8192]{1,0:T(4,128)}, bf16[4,8192]{1,0:T(4,128)(2,1)}) custom-call(bf16[8,8192]{1,0:T(8,128)(2,1)} %copy-done.4, bf16[8,8192]{1,0:T(8,128)(2,1)} %copy-done.10, bf16[8,8192]{1,0:T(8,128)(2,1)} %copy-done.11, bf16[8,8192]{1,0:T(8,128)(2,1)} %copy-done.12), custom_call_target="tpu_custom_call" | custom-call | flops 1 | bytes 1 | tf_op jit(solution)/shard_map/pallas_call | solution.py:284
  92.9 1.1 %collective-permute-start.23 = (bf16[4,8192]{1,0:T(4,128)(2,1)}, bf16[4,8192]{1,0:T(4,128)(2,1)S(1)}, u32[]{:S(2)}, u32[]{:S(2)}) collective-permute-start(bf16[4,8192]{1,0:T(4,128)(2,1)} %get-tuple-element.50), channel_id=1, source_target_pairs={{0,2},{1,3},{2,0},{3,1},{4,6},{5,7},{6,4},{7,5},{8,10},{9,11},{10,... | collective-permute-start | bytes 196616 | tf_op jit(solution)/shard_map/ppermute | solution.py:418
  94.0 4.9 %collective-permute-done.23 = bf16[4,8192]{1,0:T(4,128)(2,1)S(1)} collective-permute-done((bf16[4,8192]{1,0:T(4,128)(2,1)}, bf16[4,8192]{1,0:T(4,128)(2,1)S(1)}, u32[]{:S(2)}, u32[]{:S(2)}) %collective-permute-start.23) | collective-permute-done | bytes 65568 | tf_op jit(solution)/shard_map/ppermute | solution.py:418
  98.9 1.6 %fusion.1 = bf16[1,1,4,8192]{3,2,1,0:T(4,128)(2,1)} fusion(f32[4,8192]{1,0:T(4,128)} %get-tuple-element.49, bf16[4,8192]{1,0:T(4,128)(2,1)S(1)} %collective-permute-done.23, bf16[1,1,4,8192]{3,2,1,0:T(4,128)(2,1)S(1)} %copy-done.9), kind=kLoop, calls=%fused_computation.7 | loop fusion | flops 163840 | bytes 327680 | tf_op jit(solution)/shard_map/broadcast_in_dim | solution.py:419
  (61 shorter events, 0.4 us)
Async XLA Ops:
  0.0 31.9 %collective-permute-start.4 = (bf16[64,4096]{1,0:T(8,128)(2,1)}, bf16[64,4096]{1,0:T(8,128)(2,1)S(1)}, u32[]{:S(2)}, u32[]{:S(2)}) collective-permute-start(bf16[64,4096]{1,0:T(8,128)(2,1)} %bitcast.22), channel_id=1, source_target_pairs={{0,1},{1,0},{2,3},{3,2},{4,5},{5,4},{6,7},{7,6},{8,9},{9,8},{10,11... | collective-permute-start | bytes 1572872 | tf_op jit(solution)/shard_map/ppermute | solution.py:330
  0.0 32.1 %collective-permute-start.6 = (bf16[64,4096]{1,0:T(8,128)(2,1)}, bf16[64,4096]{1,0:T(8,128)(2,1)S(1)}, u32[]{:S(2)}, u32[]{:S(2)}) collective-permute-start(bf16[64,4096]{1,0:T(8,128)(2,1)} %bitcast.23), channel_id=1, source_target_pairs={{0,2},{1,3},{2,0},{3,1},{4,6},{5,7},{6,4},{7,5},{8,10},{9,11},{10,... | collective-permute-start | bytes 1572872 | tf_op jit(solution)/shard_map/ppermute | solution.py:329
  1.2 16.2 %collective-permute-start = (bf16[4,8192]{1,0:T(4,128)(2,1)}, bf16[4,8192]{1,0:T(4,128)(2,1)S(1)}, u32[]{:S(2)}, u32[]{:S(2)}) collective-permute-start(bf16[4,8192]{1,0:T(4,128)(2,1)} %bitcast.25), channel_id=1, source_target_pairs={{0,2},{1,3},{2,0},{3,1},{4,6},{5,7},{6,4},{7,5},{8,10},{9,11},{10,... | collective-permute-start | bytes 196616 | tf_op jit(solution)/shard_map/ppermute | solution.py:328
  17.5 0.6 copy-start.13
  19.8 8.5 %collective-permute-start.1 = (bf16[8,8192]{1,0:T(8,128)(2,1)}, bf16[8,8192]{1,0:T(8,128)(2,1)S(1)}, u32[]{:S(2)}, u32[]{:S(2)}) collective-permute-start(bf16[8,8192]{1,0:T(8,128)(2,1)} %shard_map.91), channel_id=1, source_target_pairs={{0,12},{1,13},{2,14},{3,15},{4,0},{5,1},{6,2},{7,3},{8,4},{9,5},{1... | collective-permute-start | bytes 393224 | tf_op jit(solution)/shard_map/ppermute | solution.py:332
  22.6 8.0 %collective-permute-start.2 = (bf16[8,8192]{1,0:T(8,128)(2,1)}, bf16[8,8192]{1,0:T(8,128)(2,1)S(1)}, u32[]{:S(2)}, u32[]{:S(2)}) collective-permute-start(bf16[8,8192]{1,0:T(8,128)(2,1)} %shard_map.91), channel_id=1, source_target_pairs={{0,8},{1,9},{2,10},{3,11},{4,12},{5,13},{6,14},{7,15},{8,0},{9,1},... | collective-permute-start | bytes 393224 | tf_op jit(solution)/shard_map/ppermute | solution.py:332
  23.4 8.6 %collective-permute-start.3 = (bf16[8,8192]{1,0:T(8,128)(2,1)}, bf16[8,8192]{1,0:T(8,128)(2,1)S(1)}, u32[]{:S(2)}, u32[]{:S(2)}) collective-permute-start(bf16[8,8192]{1,0:T(8,128)(2,1)} %shard_map.91), channel_id=1, source_target_pairs={{0,4},{1,5},{2,6},{3,7},{4,8},{5,9},{6,10},{7,11},{8,12},{9,13},{1... | collective-permute-start | bytes 393224 | tf_op jit(solution)/shard_map/ppermute | solution.py:332
  24.3 9.7 %copy-start.3 = (bf16[64,64]{1,0:T(8,128)(2,1)}, bf16[64,64]{1,0:T(8,128)(2,1)S(1)}, u32[]{:S(2)}) copy-start(bf16[64,64]{1,0:T(8,128)(2,1)S(1)} %fusion.5.perm_ref) | copy-start | bytes 24580
  24.3 2.2 %copy-start = (bf16[8192,256]{1,0:T(8,128)(2,1)S(1)}, bf16[8192,256]{1,0:T(8,128)(2,1)}, u32[]{:S(2)}) copy-start(bf16[8192,256]{1,0:T(8,128)(2,1)} %source_ref) | copy-start | bytes 12582916
  26.5 5.5 %copy-start.8 = (bf16[8,8192]{1,0:T(8,128)(2,1)S(1)}, bf16[8,8192]{1,0:T(8,128)(2,1)}, u32[]{:S(2)}) copy-start(bf16[8,8192]{1,0:T(8,128)(2,1)} %shard_map.91) | copy-start | bytes 393220
  26.5 7.5 %copy-start.1 = (bf16[8192,64]{0,1:T(8,128)(2,1)S(1)}, bf16[8192,64]{0,1:T(8,128)(2,1)}, u32[]{:S(2)}) copy-start(bf16[8192,64]{0,1:T(8,128)(2,1)} %param.12) | copy-start | bytes 3145732
  26.8 23.2 %copy-start.18 = (s32[4]{0:T(128)S(1)}, s32[4]{0:T(128)}, u32[]{:S(2)}) copy-start(s32[4]{0:T(128)} %constant.253.clone) | copy-start | bytes 52
  26.8 28.0 %copy-start.2 = (bf16[1,1,4096,64]{2,3,1,0:T(8,128)(2,1)S(1)}, bf16[1,1,4096,64]{2,3,1,0:T(8,128)(2,1)}, u32[]{:S(2)}) copy-start(bf16[1,1,4096,64]{2,3,1,0:T(8,128)(2,1)} %param.14) | copy-start | bytes 1572868
  32.0 2.0 %collective-permute-start.5 = (bf16[32,8192]{1,0:T(8,128)(2,1)S(1)}, bf16[32,8192]{1,0:T(8,128)(2,1)S(1)}, u32[]{:S(2)}, u32[]{:S(2)}) collective-permute-start(bf16[32,8192]{1,0:T(8,128)(2,1)S(1)} %pad_maximum_fusion.own_ref), channel_id=1, source_target_pairs={{0,1},{1,0},{2,3},{3,2},{4,5},{5,4},{6,7},{7,6},{8,9},{9,8},{10,11... | collective-permute-start | bytes 1572872 | tf_op jit(solution)/shard_map/ppermute | solution.py:336
  32.1 4.5 %collective-permute-start.7 = (bf16[64,4096]{1,0:T(8,128)(2,1)S(1)}, bf16[64,4096]{1,0:T(8,128)(2,1)S(1)}, u32[]{:S(2)}, u32[]{:S(2)}) collective-permute-start(bf16[64,4096]{1,0:T(8,128)(2,1)S(1)} %collective-permute-done.6.refs_2_), channel_id=1, source_target_pairs={{0,1},{1,0},{2,3},{3,2},{4,5},{5,4},{6,7},{7,6},{8,9},{9,8},{10,11... | collective-permute-start | bytes 1572872 | tf_op jit(solution)/shard_map/ppermute | solution.py:337
  34.0 29.0 %copy-start.17 = (s32[8]{0:T(128)S(1)}, s32[8]{0:T(128)}, u32[]{:S(2)}) copy-start(s32[8]{0:T(128)} %param.15) | copy-start | bytes 100
  35.3 1.3 %collective-permute-start.8 = (bf16[80,128]{1,0:T(8,128)(2,1)S(1)}, bf16[80,128]{1,0:T(8,128)(2,1)S(1)}, u32[]{:S(2)}, u32[]{:S(2)}) collective-permute-start(bf16[80,128]{1,0:T(8,128)(2,1)S(1)} %get-tuple-element.34), channel_id=1, source_target_pairs={{0,1},{1,0},{2,3},{3,2},{4,5},{5,4},{6,7},{7,6},{8,9},{9,8},{10,11... | collective-permute-start | bytes 61448 | tf_op jit(solution)/shard_map/ppermute | solution.py:385
  36.6 13.7 %collective-permute-start.10 = (bf16[32,128]{1,0:T(8,128)(2,1)S(1)}, bf16[32,128]{1,0:T(8,128)(2,1)S(1)}, u32[]{:S(2)}, u32[]{:S(2)}) collective-permute-start(bf16[32,128]{1,0:T(8,128)(2,1)S(1)} %pad_maximum_fusion.1), channel_id=1, source_target_pairs={{128,48},{129,65},{130,50},{131,67},{132,52},{133,69},{134,54},{13... | collective-permute-start | bytes 24584 | tf_op jit(solution)/shard_map/ppermute | solution.py:389
  43.3 7.0 %collective-permute-start.11 = (bf16[32,128]{1,0:T(8,128)(2,1)S(1)}, bf16[32,128]{1,0:T(8,128)(2,1)S(1)}, u32[]{:S(2)}, u32[]{:S(2)}) collective-permute-start(bf16[32,128]{1,0:T(8,128)(2,1)S(1)} %pad_maximum_fusion.1), channel_id=1, source_target_pairs={{128,96},{129,81},{130,98},{131,83},{132,100},{133,85},{134,102},{... | collective-permute-start | bytes 24584 | tf_op jit(solution)/shard_map/ppermute | solution.py:389
  46.3 4.0 %collective-permute-start.12 = (bf16[32,128]{1,0:T(8,128)(2,1)S(1)}, bf16[32,128]{1,0:T(8,128)(2,1)S(1)}, u32[]{:S(2)}, u32[]{:S(2)}) collective-permute-start(bf16[32,128]{1,0:T(8,128)(2,1)S(1)} %pad_maximum_fusion.1), channel_id=1, source_target_pairs={{128,16},{129,33},{130,18},{131,35},{132,20},{133,37},{134,22},{13... | collective-permute-start | bytes 24584 | tf_op jit(solution)/shard_map/ppermute | solution.py:389
  47.6 2.7 %collective-permute-start.13 = (bf16[32,128]{1,0:T(8,128)(2,1)S(1)}, bf16[32,128]{1,0:T(8,128)(2,1)S(1)}, u32[]{:S(2)}, u32[]{:S(2)}) collective-permute-start(bf16[32,128]{1,0:T(8,128)(2,1)S(1)} %pad_maximum_fusion.1), channel_id=1, source_target_pairs={{128,0},{129,113},{130,2},{131,115},{132,4},{133,117},{134,6},{135... | collective-permute-start | bytes 24584 | tf_op jit(solution)/shard_map/ppermute | solution.py:389
  48.9 5.8 %collective-permute-start.9 = (bf16[160,128]{1,0:T(8,128)(2,1)S(1)}, bf16[160,128]{1,0:T(8,128)(2,1)S(1)}, u32[]{:S(2)}, u32[]{:S(2)}) collective-permute-start(bf16[160,128]{1,0:T(8,128)(2,1)S(1)} %constant_dynamic-update-slice_fusion.refs_4_), channel_id=1, source_target_pairs={{0,2},{1,3},{2,0},{3,1},{4,6},{5,7},{6,4},{7,5},{8,10},{9,11},{10,... | collective-permute-start | bytes 122888 | tf_op jit(solution)/shard_map/ppermute | solution.py:390
  56.5 0.6 copy-start.5
  57.2 0.6 copy-start.6
  57.7 8.4 %collective-permute-start.14 = (f32[8,256]{1,0:T(8,128)S(1)}, f32[8,256]{1,0:T(8,128)S(1)}, u32[]{:S(2)}, u32[]{:S(2)}) collective-permute-start(f32[8,256]{1,0:T(8,128)S(1)} %get-tuple-element.39), channel_id=1, source_target_pairs={{0,128},{113,129},{2,130},{115,131},{4,132},{117,133},{6,134},{119... | collective-permute-start | bytes 24584 | tf_op jit(solution)/shard_map/ppermute | solution.py:395
  59.0 7.1 %collective-permute-start.15 = (f32[8,256]{1,0:T(8,128)S(1)}, f32[8,256]{1,0:T(8,128)S(1)}, u32[]{:S(2)}, u32[]{:S(2)}) collective-permute-start(f32[8,256]{1,0:T(8,128)S(1)} %get-tuple-element.40), channel_id=1, source_target_pairs={{16,128},{33,129},{18,130},{35,131},{20,132},{37,133},{22,134},{39... | collective-permute-start | bytes 24584 | tf_op jit(solution)/shard_map/ppermute | solution.py:395
  60.3 8.6 %collective-permute-start.16 = (f32[8,256]{1,0:T(8,128)S(1)}, f32[8,256]{1,0:T(8,128)S(1)}, u32[]{:S(2)}, u32[]{:S(2)}) collective-permute-start(f32[8,256]{1,0:T(8,128)S(1)} %get-tuple-element.41), channel_id=1, source_target_pairs={{96,128},{81,129},{98,130},{83,131},{100,132},{85,133},{102,134},{... | collective-permute-start | bytes 24584 | tf_op jit(solution)/shard_map/ppermute | solution.py:395
  61.6 8.2 %collective-permute-start.17 = (f32[8,256]{1,0:T(8,128)S(1)}, f32[8,256]{1,0:T(8,128)S(1)}, u32[]{:S(2)}, u32[]{:S(2)}) collective-permute-start(f32[8,256]{1,0:T(8,128)S(1)} %get-tuple-element.42), channel_id=1, source_target_pairs={{48,128},{65,129},{50,130},{67,131},{52,132},{69,133},{54,134},{71... | collective-permute-start | bytes 24584 | tf_op jit(solution)/shard_map/ppermute | solution.py:395
  69.9 1.9 %copy-start.14 = (f32[8,256]{1,0:T(8,128)}, f32[8,256]{1,0:T(8,128)S(1)}, u32[]{:S(2)}) copy-start(f32[8,256]{1,0:T(8,128)S(1)} %select_select_fusion.far_ref) | copy-start | bytes 24580
  69.9 1.9 %collective-permute-start.18 = (f32[8,256]{1,0:T(8,128)S(1)}, f32[8,256]{1,0:T(8,128)S(1)}, u32[]{:S(2)}, u32[]{:S(2)}) collective-permute-start(f32[8,256]{1,0:T(8,128)S(1)} %select_select_fusion.far_ref), channel_id=1, source_target_pairs={{0,1},{1,0},{2,3},{3,2},{4,5},{5,4},{6,7},{7,6},{8,9},{9,8},{10,11... | collective-permute-start | bytes 24584 | tf_op jit(solution)/shard_map/ppermute | solution.py:408
  71.7 0.6 copy-start.16
  74.0 3.6 %copy-start.7 = (bf16[256,8192]{1,0:T(8,128)(2,1)S(1)}, bf16[256,8192]{1,0:T(8,128)(2,1)}, u32[]{:S(2)}) copy-start(bf16[256,8192]{1,0:T(8,128)(2,1)} %param.13) | copy-start | bytes 12582916
  74.0 3.6 %copy-start.15 = (bf16[32,256]{1,0:T(8,128)(2,1)S(1)}, bf16[32,256]{1,0:T(8,128)(2,1)}, u32[]{:S(2)}) copy-start(bf16[32,256]{1,0:T(8,128)(2,1)} %get-tuple-element.43) | copy-start | bytes 49156
  77.2 21.7 %copy-start.9 = (bf16[1,1,4,8192]{3,2,1,0:T(4,128)(2,1)S(1)}, bf16[1,1,4,8192]{3,2,1,0:T(4,128)(2,1)}, u32[]{:S(2)}) copy-start(bf16[1,1,4,8192]{3,2,1,0:T(4,128)(2,1)} %param.9) | copy-start | bytes 196612
  77.2 2.0 %collective-permute-start.19 = (bf16[32,8192]{1,0:T(8,128)(2,1)S(1)}, bf16[32,8192]{1,0:T(8,128)(2,1)S(1)}, u32[]{:S(2)}, u32[]{:S(2)}) collective-permute-start(bf16[32,8192]{1,0:T(8,128)(2,1)S(1)} %convolution_convert_fusion), channel_id=1, source_target_pairs={{0,1},{1,0},{2,3},{3,2},{4,5},{5,4},{6,7},{7,6},{8,9},{9,8},{10,11... | collective-permute-start | bytes 1572872 | tf_op jit(solution)/shard_map/ppermute | solution.py:413
  79.4 0.7 copy-start.4
  80.0 9.8 %collective-permute-start.20 = (bf16[8,8192]{1,0:T(8,128)(2,1)S(1)}, bf16[8,8192]{1,0:T(8,128)(2,1)S(1)}, u32[]{:S(2)}, u32[]{:S(2)}) collective-permute-start(bf16[8,8192]{1,0:T(8,128)(2,1)S(1)} %get-tuple-element.46), channel_id=1, source_target_pairs={{0,4},{1,5},{2,6},{3,7},{4,8},{5,9},{6,10},{7,11},{8,12},{9,13},{1... | collective-permute-start | bytes 393224 | tf_op jit(solution)/shard_map/ppermute | solution.py:416
  80.0 9.8 %collective-permute-start.21 = (bf16[8,8192]{1,0:T(8,128)(2,1)S(1)}, bf16[8,8192]{1,0:T(8,128)(2,1)S(1)}, u32[]{:S(2)}, u32[]{:S(2)}) collective-permute-start(bf16[8,8192]{1,0:T(8,128)(2,1)S(1)} %get-tuple-element.47), channel_id=1, source_target_pairs={{0,8},{1,9},{2,10},{3,11},{4,12},{5,13},{6,14},{7,15},{8,0},{9,1},... | collective-permute-start | bytes 393224 | tf_op jit(solution)/shard_map/ppermute | solution.py:416
  82.0 8.4 %collective-permute-start.22 = (bf16[8,8192]{1,0:T(8,128)(2,1)S(1)}, bf16[8,8192]{1,0:T(8,128)(2,1)S(1)}, u32[]{:S(2)}, u32[]{:S(2)}) collective-permute-start(bf16[8,8192]{1,0:T(8,128)(2,1)S(1)} %get-tuple-element.48), channel_id=1, source_target_pairs={{0,12},{1,13},{2,14},{3,15},{4,0},{5,1},{6,2},{7,3},{8,4},{9,5},{1... | collective-permute-start | bytes 393224 | tf_op jit(solution)/shard_map/ppermute | solution.py:416
  89.8 0.6 copy-start.10
  89.8 0.7 copy-start.11
  90.4 0.7 copy-start.12
  92.9 6.0 %collective-permute-start.23 = (bf16[4,8192]{1,0:T(4,128)(2,1)}, bf16[4,8192]{1,0:T(4,128)(2,1)S(1)}, u32[]{:S(2)}, u32[]{:S(2)}) collective-permute-start(bf16[4,8192]{1,0:T(4,128)(2,1)} %get-tuple-element.50), channel_id=1, source_target_pairs={{0,2},{1,3},{2,0},{3,1},{4,6},{5,7},{6,4},{7,5},{8,10},{9,11},{10,... | collective-permute-start | bytes 196616 | tf_op jit(solution)/shard_map/ppermute | solution.py:418

commit v3 on v2

--- a/solution.py
+++ b/solution.py
@@ -15,6 +15,7 @@
 F32 = jnp.float32
 BF16 = jnp.bfloat16
 VMEM = pl.BlockSpec(memory_space=pltpu.VMEM)
+LIMIT = pltpu.CompilerParams(vmem_limit_bytes=8 * 1024 * 1024)
 COST = pl.CostEstimate(flops=1, bytes_accessed=1, transcendentals=0)
 
 CORE = [(i, i ^ 1) for i in range(16)]
@@ -40,28 +41,26 @@
     return pl.pallas_call(
         norm_kernel,
         cost_estimate=COST,
+        compiler_params=LIMIT,
         out_shape=jax.ShapeDtypeStruct((2 * own.shape[0], own.shape[1]), BF16),
         in_specs=[VMEM, VMEM, VMEM],
         out_specs=VMEM,
     )(own, beside, gain[None, :])
 
 
-def fetch_kernel(source_ref, out_ref, sem):
-    copy = pltpu.make_async_copy(source_ref, out_ref, sem)
-    copy.start()
-    copy.wait()
-
-
-def fetch(weights):
-    return pl.pallas_call(
-        fetch_kernel,
-        cost_estimate=COST,
-        out_shape=jax.ShapeDtypeStruct(weights.shape, weights.dtype),
-        in_specs=[pl.BlockSpec(memory_space=pltpu.HBM)],
+def touch_kernel(*refs):
+    refs[-1][...] = jnp.zeros(refs[-1].shape, F32)
+
+
+def touch(*arrays):
+    return pl.pallas_call(
+        touch_kernel,
+        cost_estimate=COST,
+        compiler_params=LIMIT,
+        out_shape=jax.ShapeDtypeStruct((8, HD), F32),
+        in_specs=[VMEM] * len(arrays),
         out_specs=VMEM,
-        scratch_shapes=[pltpu.SemaphoreType.DMA],
-        compiler_params=pltpu.CompilerParams(vmem_limit_bytes=8 * 1024 * 1024),
-    )(weights)
+    )(*arrays)
 
 
 def turn(value, cosine, sine, axis):
@@ -74,8 +73,9 @@
 
 def project_kernel(
     own_ref, mate_ref, wq_ref, wkv_ref, cq_ref, sq_ref, ck_ref, sk_ref, perm_ref,
-    q_ref, pack_ref,
+    token_ref, q_ref, pack_ref,
 ):
+    del token_ref
     rows = jnp.concatenate([own_ref[...], mate_ref[...]], 0)
     query = jnp.dot(rows, wq_ref[...], preferred_element_type=F32)
     fresh = lax.dot_general(
@@ -98,26 +98,27 @@
     return jnp.concatenate([both, jnp.zeros_like(both)], 0)
 
 
-def project(own, mate, w_query, w_kv_t, cq, sq, ck, sk, perm):
+def project(own, mate, w_query, w_kv_t, cq, sq, ck, sk, perm, token):
     rows = 2 * own.shape[0]
     return pl.pallas_call(
         project_kernel,
         cost_estimate=COST,
+        compiler_params=LIMIT,
         out_shape=(
             jax.ShapeDtypeStruct((rows, w_query.shape[1]), BF16),
             jax.ShapeDtypeStruct((w_kv_t.shape[0] + 16, HD), BF16),
         ),
-        in_specs=[VMEM] * 9,
+        in_specs=[VMEM] * 10,
         out_specs=(VMEM,) * 2,
-        compiler_params=pltpu.CompilerParams(vmem_limit_bytes=16 * 1024 * 1024),
-    )(own, mate, w_query, w_kv_t, cq, sq, ck, sk, perm)
+    )(own, mate, w_query, w_kv_t, cq, sq, ck, sk, perm, token)
 
 
 def softmax_parts(queries, bounds, kv_refs, fresh, scores):
     tokens = kv_refs[0].shape[1]
     chunk = 512
     scale = 1.0 / math.sqrt(HD)
-    low, high, fresh_low, fresh_high = bounds
+    if bounds is not None:
+        low, high, fresh_low, fresh_high = bounds
 
     def pair(first, span):
         return jnp.concatenate([kv_refs[first][:, span], kv_refs[first + 1][:, span]], 0)
@@ -125,14 +126,16 @@
     fresh_keys = jnp.concatenate(fresh[:2], 0)
     fresh_values = jnp.concatenate(fresh[2:], 0)
     fresh_scores = jnp.dot(queries, fresh_keys, preferred_element_type=F32) * scale
-    index = lax.broadcasted_iota(jnp.int32, fresh_scores.shape, 1)
-    fresh_scores = jnp.where((index >= fresh_low) & (index <= fresh_high), fresh_scores, NEG)
+    if bounds is not None:
+        index = lax.broadcasted_iota(jnp.int32, fresh_scores.shape, 1)
+        fresh_scores = jnp.where((index >= fresh_low) & (index <= fresh_high), fresh_scores, NEG)
     peak = jnp.max(fresh_scores, -1, keepdims=True)
     for start in range(0, tokens, chunk):
         span = slice(start, start + chunk)
         part_scores = jnp.dot(queries, pair(0, span), preferred_element_type=F32) * scale
-        index = lax.broadcasted_iota(jnp.int32, part_scores.shape, 1) + start
-        part_scores = jnp.where((index >= low) & (index < high), part_scores, NEG)
+        if bounds is not None:
+            index = lax.broadcasted_iota(jnp.int32, part_scores.shape, 1) + start
+            part_scores = jnp.where((index >= low) & (index < high), part_scores, NEG)
         scores[:, span] = part_scores
         peak = jnp.maximum(peak, jnp.max(part_scores, -1, keepdims=True))
     contract = (((1,), (1,)), ((), ()))
@@ -160,60 +163,93 @@
     return [held[place ^ part] for part in range(4)]
 
 
-def attend_kernel(me_ref, q_ref, bounds_ref, *refs):
-    kv_refs, pack_refs, asked = refs[:4], refs[4:6], refs[6:10]
-    out_ref, lead_ref = refs[10:12]
-    answers = refs[12:16]
-    scores = refs[16]
-    size = kv_refs[0].shape[0]
-    other = pack_refs[0].shape[0] // 2
+def each_place(me_ref, body):
+    for place in range(4):
+        pl.when(me_ref[0] == place)(functools.partial(body, place))
+
+
+def held_fresh(pack_refs, size):
+    return [ref[:size, :size] for ref in pack_refs]
+
+
+def main_kernel(me_ref, q_ref, bounds_ref, w_ref, *refs):
+    del w_ref
+    kv_refs, pack_refs = refs[:4], refs[4:8]
+    out_ref, lead_ref, scores = refs[8:]
 
     def body(place):
         query = q_ref[...]
         rows = query.shape[0]
-        held = [ref[first : first + size, :rows] for ref in pack_refs for first in (0, other)]
+        bounds = bounds_ref[...]
+        mixed, peak, total = softmax_parts(
+            jnp.concatenate([query[:, :HD], query[:, HD:]], 0),
+            [bounds[:, i : i + 1] for i in range(4)],
+            in_order(place, kv_refs),
+            in_order(place, held_fresh(pack_refs, kv_refs[0].shape[0])),
+            scores,
+        )
+        ready = mixed / total
+        out_ref[...] = jnp.concatenate([ready[:rows], ready[rows:]], 1).astype(BF16)
+        packed = pack_parts(mixed, peak, total)
+        lead_ref[...] = lead_rows(packed[:8], packed[rows : rows + 8])
+
+    each_place(me_ref, body)
+
+
+def far_kernel(me_ref, *refs):
+    kv_refs, pack_refs, asked = refs[:4], refs[4:8], refs[8:12]
+    answers, scores = refs[12:16], refs[16]
+
+    def body(place):
         far = []
         for ref in asked:
             both = ref[...].astype(F32)
             far += [both[:4], both[16:20]]
-        far = jnp.concatenate(far, 0).astype(BF16)
-        bounds = bounds_ref[...]
         mixed, peak, total = softmax_parts(
-            jnp.concatenate([query[:, :HD], query[:, HD:], far], 0),
-            [bounds[:, i : i + 1] for i in range(4)],
+            jnp.concatenate(far, 0).astype(BF16),
+            None,
             in_order(place, kv_refs),
-            in_order(place, held),
+            in_order(place, held_fresh(pack_refs, kv_refs[0].shape[0])),
             scores,
         )
-        ready = mixed / total
-        out_ref[...] = jnp.concatenate([ready[:rows], ready[rows : 2 * rows]], 1).astype(BF16)
         packed = pack_parts(mixed, peak, total)
-        lead_ref[...] = lead_rows(packed[:8], packed[rows : rows + 8])
         for i, ref in enumerate(answers):
-            ref[...] = packed[2 * rows + 8 * i : 2 * rows + 8 * i + 8]
-
-    for place in range(4):
-        pl.when(me_ref[0] == place)(functools.partial(body, place))
+            ref[...] = packed[8 * i : 8 * i + 8]
+
+    each_place(me_ref, body)
 
 
 SMEM = pl.BlockSpec(memory_space=pltpu.SMEM)
-LIMIT = pltpu.CompilerParams(vmem_limit_bytes=16 * 1024 * 1024)
-
-
-def attend(me, query, bounds, kv, packs, asked):
-    packed = jax.ShapeDtypeStruct((8, 2 * HD), F32)
-    return pl.pallas_call(
-        attend_kernel,
-        cost_estimate=COST,
-        out_shape=(jax.ShapeDtypeStruct(query.shape, BF16), packed) + (packed,) * 4,
+
+
+def attend_main(me, query, bounds, w_out, kv, packs):
+    return pl.pallas_call(
+        main_kernel,
+        cost_estimate=COST,
+        compiler_params=LIMIT,
+        out_shape=(
+            jax.ShapeDtypeStruct(query.shape, BF16),
+            jax.ShapeDtypeStruct((8, 2 * HD), F32),
+        ),
+        in_specs=[SMEM] + [VMEM] * 11,
+        out_specs=(VMEM,) * 2,
+        scratch_shapes=[pltpu.VMEM((bounds.shape[0], kv[0].shape[1]), F32)],
+    )(me, query, bounds, w_out, *kv, *packs)
+
+
+def attend_far(me, kv, packs, asked):
+    return pl.pallas_call(
+        far_kernel,
+        cost_estimate=COST,
+        compiler_params=LIMIT,
+        out_shape=(jax.ShapeDtypeStruct((8, 2 * HD), F32),) * 4,
         in_specs=[SMEM] + [VMEM] * 12,
-        out_specs=(VMEM,) * 6,
-        scratch_shapes=[pltpu.VMEM((bounds.shape[0], kv[0].shape[1]), F32)],
-        compiler_params=LIMIT,
-    )(me, query, bounds, *kv, *packs, *asked)
-
-
-def merge_kernel(flags_ref, attended_ref, own_ref, far_ref, mate_ref, perm_ref, keep_ref, give_ref):
+        out_specs=(VMEM,) * 4,
+        scratch_shapes=[pltpu.VMEM((32, kv[0].shape[1]), F32)],
+    )(me, *kv, *packs, *asked)
+
+
+def merge_kernel(flags_ref, attended_ref, own_ref, far_ref, mate_ref, perm_ref, w_ref, keep_ref, give_ref):
     own = own_ref[...]
     far = jnp.where(flags_ref[1] == 1, far_ref[:4], mate_ref[4:])
     far = jnp.concatenate([far, far], 0)
@@ -236,19 +272,24 @@
     attended = lax.dot_general(
         perm_ref[...], attended, (((0,), (0,)), ((), ())), preferred_element_type=F32
     ).astype(BF16)
-    keep_ref[...] = attended[: rows // 2]
-    give_ref[...] = attended[rows // 2 :]
-
-
-def merge(flags, attended, own, far, mate, perm):
-    rows, columns = attended.shape
+    width = 1024
+    for first in range(0, w_ref.shape[1], width):
+        span = slice(first, first + width)
+        share = jnp.dot(attended, w_ref[:, span], preferred_element_type=F32).astype(BF16)
+        keep_ref[:, span] = share[: rows // 2]
+        give_ref[:, span] = share[rows // 2 :]
+
+
+def merge(flags, attended, own, far, mate, perm, w_out):
+    half = jax.ShapeDtypeStruct((attended.shape[0] // 2, w_out.shape[1]), BF16)
     return pl.pallas_call(
         merge_kernel,
         cost_estimate=COST,
-        out_shape=(jax.ShapeDtypeStruct((rows // 2, columns), BF16),) * 2,
-        in_specs=[SMEM] + [VMEM] * 5,
+        compiler_params=LIMIT,
+        out_shape=(half, half),
+        in_specs=[SMEM] + [VMEM] * 6,
         out_specs=(VMEM,) * 2,
-    )(flags, attended, own, far, mate, perm)
+    )(flags, attended, own, far, mate, perm, w_out)
 
 
 def add_core_kernel(own_ref, across_ref, *out_refs):
@@ -263,10 +304,10 @@
     return pl.pallas_call(
         add_core_kernel,
         cost_estimate=COST,
+        compiler_params=LIMIT,
         out_shape=(jax.ShapeDtypeStruct((rows // XN, columns), BF16),) * XN,
         in_specs=[VMEM, VMEM],
         out_specs=(VMEM,) * XN,
-        compiler_params=LIMIT,
     )(own, across)
 
 
@@ -284,6 +325,7 @@
     return pl.pallas_call(
         add_x_kernel,
         cost_estimate=COST,
+        compiler_params=LIMIT,
         out_shape=(
             jax.ShapeDtypeStruct((rows // 2, columns), F32),
             jax.ShapeDtypeStruct((rows // 2, columns), BF16),
@@ -297,7 +339,7 @@
     return jnp.sum(jnp.where(selector, table[None, :], 0), 1)
 
 
-DISTANCES = ((3, 4), (-2, -3), (1, 2), (0, -1))
+DISTANCES = ((0, -1), (1, 2), (-2, -3), (3, 4))
 
 
 def carry(distances, groups, count, back):
@@ -326,14 +368,15 @@
     kcols = w_keyval.shape[1]
 
     beside = lax.ppermute(own_rows, "tp", YHI)
-    kv_y = lax.ppermute(kv_t, "tp", YHI)
-    kv_core = lax.ppermute(kv_t, "tp", CORE)
+    kv_sent = after(kv_t, beside)
+    kv_y = lax.ppermute(kv_sent, "tp", YHI)
+    kv_core = lax.ppermute(kv_sent, "tp", CORE)
     pair = norm(own_rows, beside, norm_gain)
     others = [lax.ppermute(pair, "tp", xshift(-k)) for k in range(1, XN)]
-    w_query = fetch(after(w_query, pair))
-    others = after(others, w_query, kv_core)
+    token = touch(pair, w_query, w_keyval.T)
+    others = after(others, kv_y, token)
     own_half = jnp.concatenate([pair] + others, 0)
-    mate_half = after(lax.ppermute(own_half, "tp", CORE), kv_y)
+    mate_half = after(lax.ppermute(own_half, "tp", CORE), kv_core)
     kv_both = lax.ppermute(kv_y, "tp", CORE)
 
     slot = jnp.arange(row_count, dtype=jnp.int32)
@@ -364,8 +407,7 @@
     high = jnp.where(side == 0, cache_len, start + span)
     fresh_low = jnp.where(side == 0, 0, request * STEPS)
     bounds = jnp.stack([low, high, fresh_low, row_ids], 1)
-    whole = jnp.array([0, cache_len, 0, row_count - 1], jnp.int32)
-    bounds = jnp.concatenate([bounds, bounds, jnp.broadcast_to(whole[None, :], (32, 4))], 0)
+    bounds = jnp.concatenate([bounds, bounds], 0)
 
     position_at = jnp.sum(jnp.where(placed, positions[:, None], 0), 0).astype(F32)
     column = jnp.arange(qcols, dtype=jnp.int32)
@@ -380,22 +422,25 @@
     ck = jnp.where(is_key, jnp.cos(angles), 1.0)
     sk = jnp.where(is_key, jnp.sin(angles) * jnp.where(column % 2 == 0, -1.0, 1.0)[:, None], 0.0)
 
-    query, pack = project(own_half, mate_half, w_query, w_keyval.T, cq, sq, ck, sk, perm)
-
+    query, pack = project(own_half, mate_half, w_query, w_keyval.T, cq, sq, ck, sk, perm, token)
+
+    y_pack = lax.ppermute(pack, "tp", YHI)
     mate_pack = lax.ppermute(pack, "tp", CORE)
-    packs = jnp.concatenate([pack, mate_pack], 0)
+    packs = [pack, mate_pack, y_pack, lax.ppermute(y_pack, "tp", CORE)]
     leads = after(jnp.concatenate([pack[kcols:], mate_pack[kcols:]], 0), kv_both)
     axes = ("role", "grp", "tp")
     asked = [lax.ppermute(leads, axes, carry(d, groups, count, False)) for d in DISTANCES]
-    packs = [packs, lax.ppermute(after(packs, leads), "tp", YHI)]
     kv = [kv_t, kv_core, kv_y, kv_both]
     me = jnp.reshape(tp % 4, (1,)).astype(jnp.int32)
-    attended, lead_own, *answers = attend(me, query, bounds, kv, packs, asked)
+    answers = attend_far(me, kv, packs, asked)
     answers = [
         lax.ppermute(answer, axes, carry(d, groups, count, True))
         for answer, d in zip(answers, DISTANCES)
     ]
-
+    query = after(query, asked)
+    attended, lead_own = attend_main(me, query, bounds, w_out, kv, packs)
+
+    answers = after(answers, attended)
     far = jnp.zeros_like(answers[0])
     here = jnp.zeros((), jnp.bool_)
     for answer, pair_of in zip(answers, DISTANCES):
@@ -407,11 +452,9 @@
         here = here | valid
     mate = lax.ppermute(far, "tp", CORE)
     flags = jnp.stack([side, here.astype(jnp.int32)])
-    own_att, mate_att = merge(flags, attended, lead_own, far, mate, perm)
-
-    give = jnp.dot(mate_att, w_out, preferred_element_type=F32).astype(BF16)
+    keep, give = merge(flags, attended, lead_own, far, mate, perm, w_out)
+
     across = lax.ppermute(give, "tp", CORE)
-    keep = jnp.dot(own_att, w_out, preferred_element_type=F32).astype(BF16)
     parts = add_core(keep, across)
     parts = [parts[0]] + [lax.ppermute(parts[k], "tp", xshift(k)) for k in range(1, XN)]
     summed, send = add_x(parts)

time: 101 us -> 80.4 us (0.80)
  the two profiles are of different devices: /device:TPU:24 before, /device:TPU:1 now
where the time goes in v3:
time: 80.4 us; the launch traced here: 79.5 us
  starting transfers between devices  37.3 us (46%)
  waiting for transfers between devices  22.3 us (28%)
  local copies, waits for them, and re-layouts  7.34 us (9%)
  Pallas kernels  5.68 us (7%)
  other arithmetic  3.95 us (5%)
  between operations  2.93 us (4%)
    ppermute x4, waiting for transfers between devices, local(): lax.ppermute(leads, axes, carry(d, groups, count, False))  9.63 us
    ppermute x4, starting transfers between devices, local(): lax.ppermute(answer, axes, carry(d, groups, count, True))  7.33 us
    unnamed x22, local copies, waits for them, and re-layouts  7.21 us
    ppermute x4, starting transfers between devices, local(): lax.ppermute(leads, axes, carry(d, groups, count, False))  5.17 us
    ppermute x3, waiting for transfers between devices, local(): lax.ppermute(parts[k], 'tp', xshift(k))  5.14 us
    ppermute x3, starting transfers between devices, local(): lax.ppermute(parts[k], 'tp', xshift(k))  4.89 us
    ppermute x1, starting transfers between devices, local(): beside = lax.ppermute(own_rows, 'tp', YHI)  3.74 us
    ppermute x3, starting transfers between devices, local(): others = [lax.ppermute(pair, 'tp', xshift(-k)) for k in range(1, XN)]  3.68 us
  transfers between devices with their start and end apart: 25, of which 10 were waited for; matrix products, arithmetic and copies ran while one was open for 4% of the time, Pallas kernels for 4%

profile of v3, /device:TPU:1, one launch (start us, length us, event | category | flops | bytes accessed | tf_op | source)
XLA Modules:
  0.0 79.5 jit_solution(7624509674380700138)
XLA Ops:
  0.0 3.7 %collective-permute-start = (bf16[4,8192]{1,0:T(4,128)(2,1)}, bf16[4,8192]{1,0:T(4,128)(2,1)S(1)}, u32[]{:S(2)}, u32[]{:S(2)}) collective-permute-start(bf16[4,8192]{1,0:T(4,128)(2,1)} %bitcast.23), channel_id=1, source_target_pairs={{0,2},{1,3},{2,0},{3,1},{4,6},{5,7},{6,4},{7,5},{8,10},{9,11},{10,... | collective-permute-start | bytes 196616 | tf_op jit(solution)/shard_map/ppermute | solution.py:370
  3.7 0.8 select_reduce_fusion.3
  4.6 0.7 pad_add_fusion.3
  5.3 0.1 select_reduce_fusion.1
  5.4 0.1 select_reduce_fusion
  5.6 0.0 collective-permute-done.beside_ref
  5.6 3.0 %collective-permute-start.4 = (bf16[64,4096]{1,0:T(8,128)(2,1)}, bf16[64,4096]{1,0:T(8,128)(2,1)S(1)}, u32[]{:S(2)}, u32[]{:S(2)}) collective-permute-start(bf16[64,4096]{1,0:T(8,128)(2,1)} %bitcast.19), channel_id=1, source_target_pairs={{0,2},{1,3},{2,0},{3,1},{4,6},{5,7},{6,4},{7,5},{8,10},{9,11},{10,... | collective-permute-start | bytes 1572872 | tf_op jit(solution)/shard_map/ppermute | solution.py:372
  8.6 0.2 fusion.4
  8.8 0.0 copy-start.7
  8.8 0.8 %copy-done.7 = bf16[1,1,4,8192]{3,2,1,0:T(4,128)(2,1)S(1)} copy-done((bf16[1,1,4,8192]{3,2,1,0:T(4,128)(2,1)S(1)}, bf16[1,1,4,8192]{3,2,1,0:T(4,128)(2,1)}, u32[]{:S(2)}) %copy-start.7) | copy-done | bytes 65560
  9.6 0.8 copy-done.9
  10.4 0.2 shard_map.82.refs_0_
  10.6 2.6 %collective-permute-start.1 = (bf16[8,8192]{1,0:T(8,128)(2,1)S(1)}, bf16[8,8192]{1,0:T(8,128)(2,1)S(1)}, u32[]{:S(2)}, u32[]{:S(2)}) collective-permute-start(bf16[8,8192]{1,0:T(8,128)(2,1)S(1)} %shard_map.82.refs_0_), channel_id=1, source_target_pairs={{0,12},{1,13},{2,14},{3,15},{4,0},{5,1},{6,2},{7,3},{8,4},{9,5},{1... | collective-permute-start | bytes 393224 | tf_op jit(solution)/shard_map/ppermute | solution.py:375
  13.2 0.5 collective-permute-start.2
  13.7 0.6 collective-permute-start.3
  14.3 3.0 %collective-permute-start.6 = (bf16[64,4096]{1,0:T(8,128)(2,1)}, bf16[64,4096]{1,0:T(8,128)(2,1)S(1)}, u32[]{:S(2)}, u32[]{:S(2)}) collective-permute-start(bf16[64,4096]{1,0:T(8,128)(2,1)} %bitcast.20), channel_id=1, source_target_pairs={{0,1},{1,0},{2,3},{3,2},{4,5},{5,4},{6,7},{7,6},{8,9},{9,8},{10,11... | collective-permute-start | bytes 1572872 | tf_op jit(solution)/shard_map/ppermute | solution.py:373
  17.3 2.2 %copy-done = bf16[8192,256]{1,0:T(8,128)(2,1)S(1)} copy-done((bf16[8192,256]{1,0:T(8,128)(2,1)S(1)}, bf16[8192,256]{1,0:T(8,128)(2,1)}, u32[]{:S(2)}) %copy-start) | copy-done | bytes 4194328
  19.5 1.2 %copy-done.4 = bf16[8192,64]{0,1:T(8,128)(2,1)S(1)} copy-done((bf16[8192,64]{0,1:T(8,128)(2,1)S(1)}, bf16[8192,64]{0,1:T(8,128)(2,1)}, u32[]{:S(2)}) %copy-start.4) | copy-done | bytes 1048600
  20.8 0.0 copy-start.6
  20.8 0.0 collective-permute-done.2
  20.9 2.7 %collective-permute-start.5 = (bf16[32,8192]{1,0:T(8,128)(2,1)S(1)}, bf16[32,8192]{1,0:T(8,128)(2,1)S(1)}, u32[]{:S(2)}, u32[]{:S(2)}) collective-permute-start(bf16[32,8192]{1,0:T(8,128)(2,1)S(1)} %pad_maximum_fusion.own_ref), channel_id=1, source_target_pairs={{0,1},{1,0},{2,3},{3,2},{4,5},{5,4},{6,7},{7,6},{8,9},{9,8},{10,11... | collective-permute-start | bytes 1572872 | tf_op jit(solution)/shard_map/ppermute | solution.py:379
  23.6 0.1 collective-permute-start.8
  23.7 0.3 fusion
  24.0 1.1 %collective-permute-done.5.mate_ref = bf16[32,8192]{1,0:T(8,128)(2,1)S(1)} collective-permute-done((bf16[32,8192]{1,0:T(8,128)(2,1)S(1)}, bf16[32,8192]{1,0:T(8,128)(2,1)S(1)}, u32[]{:S(2)}, u32[]{:S(2)}) %collective-permute-start.5) | collective-permute-done | bytes 524320 | tf_op jit(solution)/shard_map/ppermute | solution.py:379
  25.1 1.4 %shard_map.84 = (bf16[64,256]{1,0:T(8,128)(2,1)S(1)}, bf16[80,128]{1,0:T(8,128)(2,1)S(1)}) custom-call(bf16[32,8192]{1,0:T(8,128)(2,1)S(1)} %pad_maximum_fusion.own_ref, bf16[32,8192]{1,0:T(8,128)(2,1)S(1)} %collective-permute-done.5.mate_ref, bf16[8192,256]{1,0:T(8,128)(2,1)S(1)} %copy-done.1, bf16[64,8192]{1,0:T(8,128)(2,1)S(1)} %bitcast.18, ...), custom_call_target="tpu_custom_call" | custom-call | flops 1 | bytes 1 | tf_op jit(solution)/shard_map/pallas_call | solution.py:103
  26.4 0.5 collective-permute-start.7
  26.9 0.7 fusion.13
  27.7 1.2 %collective-permute-start.13 = (bf16[80,128]{1,0:T(8,128)(2,1)S(1)}, bf16[80,128]{1,0:T(8,128)(2,1)S(1)}, u32[]{:S(2)}, u32[]{:S(2)}) collective-permute-start(bf16[80,128]{1,0:T(8,128)(2,1)S(1)} %get-tuple-element.38.refs_4_), channel_id=1, source_target_pairs={{0,2},{1,3},{2,0},{3,1},{4,6},{5,7},{6,4},{7,5},{8,10},{9,11},{10,... | collective-permute-start | bytes 61448 | tf_op jit(solution)/shard_map/ppermute | solution.py:427
  28.9 1.3 %collective-permute-start.10 = (bf16[32,128]{1,0:T(8,128)(2,1)S(1)}, bf16[32,128]{1,0:T(8,128)(2,1)S(1)}, u32[]{:S(2)}, u32[]{:S(2)}) collective-permute-start(bf16[32,128]{1,0:T(8,128)(2,1)S(1)} %pad_maximum_fusion.1), channel_id=1, source_target_pairs={{128,16},{129,33},{130,18},{131,35},{132,20},{133,37},{134,22},{13... | collective-permute-start | bytes 24584 | tf_op jit(solution)/shard_map/ppermute | solution.py:432
  30.2 1.3 %collective-permute-start.11 = (bf16[32,128]{1,0:T(8,128)(2,1)S(1)}, bf16[32,128]{1,0:T(8,128)(2,1)S(1)}, u32[]{:S(2)}, u32[]{:S(2)}) collective-permute-start(bf16[32,128]{1,0:T(8,128)(2,1)S(1)} %pad_maximum_fusion.1), channel_id=1, source_target_pairs={{128,96},{129,81},{130,98},{131,83},{132,100},{133,85},{134,102},{... | collective-permute-start | bytes 24584 | tf_op jit(solution)/shard_map/ppermute | solution.py:432
  31.5 1.3 %collective-permute-start.12 = (bf16[32,128]{1,0:T(8,128)(2,1)S(1)}, bf16[32,128]{1,0:T(8,128)(2,1)S(1)}, u32[]{:S(2)}, u32[]{:S(2)}) collective-permute-start(bf16[32,128]{1,0:T(8,128)(2,1)S(1)} %pad_maximum_fusion.1), channel_id=1, source_target_pairs={{128,48},{129,65},{130,50},{131,67},{132,52},{133,69},{134,54},{13... | collective-permute-start | bytes 24584 | tf_op jit(solution)/shard_map/ppermute | solution.py:432
  32.8 1.3 %collective-permute-start.9 = (bf16[32,128]{1,0:T(8,128)(2,1)S(1)}, bf16[32,128]{1,0:T(8,128)(2,1)S(1)}, u32[]{:S(2)}, u32[]{:S(2)}) collective-permute-start(bf16[32,128]{1,0:T(8,128)(2,1)S(1)} %pad_maximum_fusion.1), channel_id=1, source_target_pairs={{128,0},{129,113},{130,2},{131,115},{132,4},{133,117},{134,6},{135... | collective-permute-start | bytes 24584 | tf_op jit(solution)/shard_map/ppermute | solution.py:432
  34.1 0.5 collective-permute-start.14
  34.6 2.7 %collective-permute-done.10.refs_9_ = bf16[32,128]{1,0:T(8,128)(2,1)S(1)} collective-permute-done((bf16[32,128]{1,0:T(8,128)(2,1)S(1)}, bf16[32,128]{1,0:T(8,128)(2,1)S(1)}, u32[]{:S(2)}, u32[]{:S(2)}) %collective-permute-start.10) | collective-permute-done | bytes 8224 | tf_op jit(solution)/shard_map/ppermute | solution.py:432
  37.3 4.3 %collective-permute-done.11.refs_10_ = bf16[32,128]{1,0:T(8,128)(2,1)S(1)} collective-permute-done((bf16[32,128]{1,0:T(8,128)(2,1)S(1)}, bf16[32,128]{1,0:T(8,128)(2,1)S(1)}, u32[]{:S(2)}, u32[]{:S(2)}) %collective-permute-start.11) | collective-permute-done | bytes 8224 | tf_op jit(solution)/shard_map/ppermute | solution.py:432
  41.7 1.9 %collective-permute-done.12.refs_11_ = bf16[32,128]{1,0:T(8,128)(2,1)S(1)} collective-permute-done((bf16[32,128]{1,0:T(8,128)(2,1)S(1)}, bf16[32,128]{1,0:T(8,128)(2,1)S(1)}, u32[]{:S(2)}, u32[]{:S(2)}) %collective-permute-start.12) | collective-permute-done | bytes 8224 | tf_op jit(solution)/shard_map/ppermute | solution.py:432
  43.6 0.7 collective-permute-done.9.refs_8_
  44.3 0.8 %shard_map.86 = (f32[8,256]{1,0:T(8,128)S(1)}, f32[8,256]{1,0:T(8,128)S(1)}, f32[8,256]{1,0:T(8,128)S(1)}, f32[8,256]{1,0:T(8,128)S(1)}) custom-call(s32[1]{0:T(128)} %bitcast.3.me_ref, bf16[64,4096]{1,0:T(8,128)(2,1)S(1)} %bitcast.21, bf16[64,4096]{1,0:T(8,128)(2,1)S(1)} %collective-permute-done.6.refs_1_, ...), custom_call_target="tpu_custom_call" | custom-call | flops 1 | bytes 1 | tf_op jit(solution)/shard_map/pallas_call | solution.py:241
  45.1 2.2 %collective-permute-start.15 = (f32[8,256]{1,0:T(8,128)S(1)}, f32[8,256]{1,0:T(8,128)S(1)}, u32[]{:S(2)}, u32[]{:S(2)}) collective-permute-start(f32[8,256]{1,0:T(8,128)S(1)} %get-tuple-element.43), channel_id=1, source_target_pairs={{0,128},{113,129},{2,130},{115,131},{4,132},{117,133},{6,134},{119... | collective-permute-start | bytes 24584 | tf_op jit(solution)/shard_map/ppermute | solution.py:437
  47.3 1.3 %collective-permute-start.16 = (f32[8,256]{1,0:T(8,128)S(1)}, f32[8,256]{1,0:T(8,128)S(1)}, u32[]{:S(2)}, u32[]{:S(2)}) collective-permute-start(f32[8,256]{1,0:T(8,128)S(1)} %get-tuple-element.44), channel_id=1, source_target_pairs={{16,128},{33,129},{18,130},{35,131},{20,132},{37,133},{22,134},{39... | collective-permute-start | bytes 24584 | tf_op jit(solution)/shard_map/ppermute | solution.py:437
  48.6 2.2 %collective-permute-start.17 = (f32[8,256]{1,0:T(8,128)S(1)}, f32[8,256]{1,0:T(8,128)S(1)}, u32[]{:S(2)}, u32[]{:S(2)}) collective-permute-start(f32[8,256]{1,0:T(8,128)S(1)} %get-tuple-element.45), channel_id=1, source_target_pairs={{96,128},{81,129},{98,130},{83,131},{100,132},{85,133},{102,134},{... | collective-permute-start | bytes 24584 | tf_op jit(solution)/shard_map/ppermute | solution.py:437
  50.8 1.7 %collective-permute-start.18 = (f32[8,256]{1,0:T(8,128)S(1)}, f32[8,256]{1,0:T(8,128)S(1)}, u32[]{:S(2)}, u32[]{:S(2)}) collective-permute-start(f32[8,256]{1,0:T(8,128)S(1)} %get-tuple-element.46), channel_id=1, source_target_pairs={{48,128},{65,129},{50,130},{67,131},{52,132},{69,133},{54,134},{71... | collective-permute-start | bytes 24584 | tf_op jit(solution)/shard_map/ppermute | solution.py:437
  52.4 0.1 add_add_fusion
  52.5 0.1 copy.12.bounds_ref
  55.2 0.0 copy-start.2
  55.2 2.2 %copy-done.2 = bf16[256,8192]{1,0:T(8,128)(2,1)S(1)} copy-done((bf16[256,8192]{1,0:T(8,128)(2,1)S(1)}, bf16[256,8192]{1,0:T(8,128)(2,1)}, u32[]{:S(2)}) %copy-start.2) | copy-done | bytes 4194328
  57.4 1.5 %shard_map.85 = (bf16[64,256]{1,0:T(8,128)(2,1)S(1)}, f32[8,256]{1,0:T(8,128)S(1)}) custom-call(s32[1]{0:T(128)} %bitcast.3.me_ref, bf16[64,256]{1,0:T(8,128)(2,1)S(1)} %get-tuple-element.40.q_ref, s32[128,4]{1,0:T(8,128)S(1)} %copy.12.bounds_ref, bf16[256,8192]{1,0:T(8,128)(2,1)S(1)} %copy-done.2, bf16[64,4096]{1,0:T(8,128)(2,1)S(1)} %bitcast.22, ...), custom_call_target="tpu_custom_call" | custom-call | flops 1 | bytes 1 | tf_op jit(solution)/shard_map/pallas_call | solution.py:226
  58.9 0.0 copy-start.8
  58.9 0.1 collective-permute-start.19
  59.0 0.1 pad_add_fusion.2.flags_ref
  59.1 1.1 %collective-permute-done.19.mate_ref = f32[8,256]{1,0:T(8,128)S(1)} collective-permute-done((f32[8,256]{1,0:T(8,128)S(1)}, f32[8,256]{1,0:T(8,128)S(1)}, u32[]{:S(2)}, u32[]{:S(2)}) %collective-permute-start.19) | collective-permute-done | bytes 8224 | tf_op jit(solution)/shard_map/ppermute | solution.py:453
  60.2 1.6 %shard_map.87 = (bf16[32,8192]{1,0:T(8,128)(2,1)S(1)}, bf16[32,8192]{1,0:T(8,128)(2,1)S(1)}) custom-call(s32[2]{0:T(128)S(1)} %pad_add_fusion.2.flags_ref, bf16[64,256]{1,0:T(8,128)(2,1)S(1)} %get-tuple-element.41.attended_ref, f32[8,256]{1,0:T(8,128)S(1)} %get-tuple-element.42.own_ref, f32[8,256]{1,0:T(8,128)S(1)} %select_select_fusion.far_ref, ...), custom_call_target="tpu_custom_call" | custom-call | flops 1 | bytes 1 | tf_op jit(solution)/shard_map/pallas_call | solution.py:285
  61.8 0.3 collective-permute-start.20
  62.1 1.7 %collective-permute-done.20.across_ref = bf16[32,8192]{1,0:T(8,128)(2,1)S(1)} collective-permute-done((bf16[32,8192]{1,0:T(8,128)(2,1)S(1)}, bf16[32,8192]{1,0:T(8,128)(2,1)S(1)}, u32[]{:S(2)}, u32[]{:S(2)}) %collective-permute-start.20) | collective-permute-done | bytes 524320 | tf_op jit(solution)/shard_map/ppermute | solution.py:457
  63.8 0.1 shard_map.88
  64.0 1.3 %collective-permute-start.21 = (bf16[8,8192]{1,0:T(8,128)(2,1)S(1)}, bf16[8,8192]{1,0:T(8,128)(2,1)S(1)}, u32[]{:S(2)}, u32[]{:S(2)}) collective-permute-start(bf16[8,8192]{1,0:T(8,128)(2,1)S(1)} %get-tuple-element.54), channel_id=1, source_target_pairs={{0,4},{1,5},{2,6},{3,7},{4,8},{5,9},{6,10},{7,11},{8,12},{9,13},{1... | collective-permute-start | bytes 393224 | tf_op jit(solution)/shard_map/ppermute | solution.py:459
  65.3 2.5 %collective-permute-start.22 = (bf16[8,8192]{1,0:T(8,128)(2,1)S(1)}, bf16[8,8192]{1,0:T(8,128)(2,1)S(1)}, u32[]{:S(2)}, u32[]{:S(2)}) collective-permute-start(bf16[8,8192]{1,0:T(8,128)(2,1)S(1)} %get-tuple-element.55), channel_id=1, source_target_pairs={{0,8},{1,9},{2,10},{3,11},{4,12},{5,13},{6,14},{7,15},{8,0},{9,1},... | collective-permute-start | bytes 393224 | tf_op jit(solution)/shard_map/ppermute | solution.py:459
  67.7 1.2 %collective-permute-start.23 = (bf16[8,8192]{1,0:T(8,128)(2,1)S(1)}, bf16[8,8192]{1,0:T(8,128)(2,1)S(1)}, u32[]{:S(2)}, u32[]{:S(2)}) collective-permute-start(bf16[8,8192]{1,0:T(8,128)(2,1)S(1)} %get-tuple-element.56), channel_id=1, source_target_pairs={{0,12},{1,13},{2,14},{3,15},{4,0},{5,1},{6,2},{7,3},{8,4},{9,5},{1... | collective-permute-start | bytes 393224 | tf_op jit(solution)/shard_map/ppermute | solution.py:459
  68.9 1.3 %collective-permute-done.21.b_ref = bf16[8,8192]{1,0:T(8,128)(2,1)S(1)} collective-permute-done((bf16[8,8192]{1,0:T(8,128)(2,1)S(1)}, bf16[8,8192]{1,0:T(8,128)(2,1)S(1)}, u32[]{:S(2)}, u32[]{:S(2)}) %collective-permute-start.21) | collective-permute-done | bytes 131104 | tf_op jit(solution)/shard_map/ppermute | solution.py:459
  70.2 3.8 %collective-permute-done.22.c_ref = bf16[8,8192]{1,0:T(8,128)(2,1)S(1)} collective-permute-done((bf16[8,8192]{1,0:T(8,128)(2,1)S(1)}, bf16[8,8192]{1,0:T(8,128)(2,1)S(1)}, u32[]{:S(2)}, u32[]{:S(2)}) %collective-permute-start.22) | collective-permute-done | bytes 131104 | tf_op jit(solution)/shard_map/ppermute | solution.py:459
  74.0 0.1 shard_map.89
  74.1 1.1 %collective-permute-start.24 = (bf16[4,8192]{1,0:T(4,128)(2,1)S(1)}, bf16[4,8192]{1,0:T(4,128)(2,1)S(1)}, u32[]{:S(2)}, u32[]{:S(2)}) collective-permute-start(bf16[4,8192]{1,0:T(4,128)(2,1)S(1)} %get-tuple-element.58), channel_id=1, source_target_pairs={{0,2},{1,3},{2,0},{3,1},{4,6},{5,7},{6,4},{7,5},{8,10},{9,11},{10,... | collective-permute-start | bytes 196616 | tf_op jit(solution)/shard_map/ppermute | solution.py:461
  75.2 3.6 %collective-permute-done.24 = bf16[4,8192]{1,0:T(4,128)(2,1)S(1)} collective-permute-done((bf16[4,8192]{1,0:T(4,128)(2,1)S(1)}, bf16[4,8192]{1,0:T(4,128)(2,1)S(1)}, u32[]{:S(2)}, u32[]{:S(2)}) %collective-permute-start.24) | collective-permute-done | bytes 65568 | tf_op jit(solution)/shard_map/ppermute | solution.py:461
  78.8 0.7 fusion.1
  (43 shorter events, 0.2 us)
Async XLA Ops:
  0.0 5.6 %collective-permute-start = (bf16[4,8192]{1,0:T(4,128)(2,1)}, bf16[4,8192]{1,0:T(4,128)(2,1)S(1)}, u32[]{:S(2)}, u32[]{:S(2)}) collective-permute-start(bf16[4,8192]{1,0:T(4,128)(2,1)} %bitcast.23), channel_id=1, source_target_pairs={{0,2},{1,3},{2,0},{3,1},{4,6},{5,7},{6,4},{7,5},{8,10},{9,11},{10,... | collective-permute-start | bytes 196616 | tf_op jit(solution)/shard_map/ppermute | solution.py:370
  5.6 15.2 %collective-permute-start.4 = (bf16[64,4096]{1,0:T(8,128)(2,1)}, bf16[64,4096]{1,0:T(8,128)(2,1)S(1)}, u32[]{:S(2)}, u32[]{:S(2)}) collective-permute-start(bf16[64,4096]{1,0:T(8,128)(2,1)} %bitcast.19), channel_id=1, source_target_pairs={{0,2},{1,3},{2,0},{3,1},{4,6},{5,7},{6,4},{7,5},{8,10},{9,11},{10,... | collective-permute-start | bytes 1572872 | tf_op jit(solution)/shard_map/ppermute | solution.py:372
  8.8 0.8 %copy-start.7 = (bf16[1,1,4,8192]{3,2,1,0:T(4,128)(2,1)S(1)}, bf16[1,1,4,8192]{3,2,1,0:T(4,128)(2,1)}, u32[]{:S(2)}) copy-start(bf16[1,1,4,8192]{3,2,1,0:T(4,128)(2,1)} %param.8) | copy-start | bytes 196612
  9.6 0.8 copy-start.9
  10.6 10.2 %collective-permute-start.1 = (bf16[8,8192]{1,0:T(8,128)(2,1)S(1)}, bf16[8,8192]{1,0:T(8,128)(2,1)S(1)}, u32[]{:S(2)}, u32[]{:S(2)}) collective-permute-start(bf16[8,8192]{1,0:T(8,128)(2,1)S(1)} %shard_map.82.refs_0_), channel_id=1, source_target_pairs={{0,12},{1,13},{2,14},{3,15},{4,0},{5,1},{6,2},{7,3},{8,4},{9,5},{1... | collective-permute-start | bytes 393224 | tf_op jit(solution)/shard_map/ppermute | solution.py:375
  13.2 7.6 %collective-permute-start.2 = (bf16[8,8192]{1,0:T(8,128)(2,1)S(1)}, bf16[8,8192]{1,0:T(8,128)(2,1)S(1)}, u32[]{:S(2)}, u32[]{:S(2)}) collective-permute-start(bf16[8,8192]{1,0:T(8,128)(2,1)S(1)} %shard_map.82.refs_0_), channel_id=1, source_target_pairs={{0,8},{1,9},{2,10},{3,11},{4,12},{5,13},{6,14},{7,15},{8,0},{9,1},... | collective-permute-start | bytes 393224 | tf_op jit(solution)/shard_map/ppermute | solution.py:375
  13.7 7.1 %collective-permute-start.3 = (bf16[8,8192]{1,0:T(8,128)(2,1)S(1)}, bf16[8,8192]{1,0:T(8,128)(2,1)S(1)}, u32[]{:S(2)}, u32[]{:S(2)}) collective-permute-start(bf16[8,8192]{1,0:T(8,128)(2,1)S(1)} %shard_map.82.refs_0_), channel_id=1, source_target_pairs={{0,4},{1,5},{2,6},{3,7},{4,8},{5,9},{6,10},{7,11},{8,12},{9,13},{1... | collective-permute-start | bytes 393224 | tf_op jit(solution)/shard_map/ppermute | solution.py:375
  14.3 9.7 %collective-permute-start.6 = (bf16[64,4096]{1,0:T(8,128)(2,1)}, bf16[64,4096]{1,0:T(8,128)(2,1)S(1)}, u32[]{:S(2)}, u32[]{:S(2)}) collective-permute-start(bf16[64,4096]{1,0:T(8,128)(2,1)} %bitcast.20), channel_id=1, source_target_pairs={{0,1},{1,0},{2,3},{3,2},{4,5},{5,4},{6,7},{7,6},{8,9},{9,8},{10,11... | collective-permute-start | bytes 1572872 | tf_op jit(solution)/shard_map/ppermute | solution.py:373
  17.3 2.2 %copy-start = (bf16[8192,256]{1,0:T(8,128)(2,1)S(1)}, bf16[8192,256]{1,0:T(8,128)(2,1)}, u32[]{:S(2)}) copy-start(bf16[8192,256]{1,0:T(8,128)(2,1)} %wq_ref.1) | copy-start | bytes 12582916
  19.5 1.2 %copy-start.4 = (bf16[8192,64]{0,1:T(8,128)(2,1)S(1)}, bf16[8192,64]{0,1:T(8,128)(2,1)}, u32[]{:S(2)}) copy-start(bf16[8192,64]{0,1:T(8,128)(2,1)} %param.11) | copy-start | bytes 3145732
  20.7 4.3 %copy-start.1 = (bf16[8192,256]{1,0:T(8,128)(2,1)S(1)}, bf16[8192,256]{1,0:T(8,128)(2,1)}, u32[]{:S(2)}) copy-start(bf16[8192,256]{1,0:T(8,128)(2,1)} %wq_ref.1) | copy-start | bytes 12582916
  20.7 4.3 %copy-start.5 = (bf16[8192,64]{0,1:T(8,128)(2,1)S(1)}, bf16[8192,64]{0,1:T(8,128)(2,1)}, u32[]{:S(2)}) copy-start(bf16[8192,64]{0,1:T(8,128)(2,1)} %param.11) | copy-start | bytes 3145732
  20.7 6.2 %copy-start.10 = (s32[8]{0:T(128)S(1)}, s32[8]{0:T(128)}, u32[]{:S(2)}) copy-start(s32[8]{0:T(128)} %param.14) | copy-start | bytes 100
  20.8 23.5 %copy-start.6 = (bf16[1,1,4096,64]{2,3,1,0:T(8,128)(2,1)S(1)}, bf16[1,1,4096,64]{2,3,1,0:T(8,128)(2,1)}, u32[]{:S(2)}) copy-start(bf16[1,1,4096,64]{2,3,1,0:T(8,128)(2,1)} %param.13) | copy-start | bytes 1572868
  20.9 4.2 %collective-permute-start.5 = (bf16[32,8192]{1,0:T(8,128)(2,1)S(1)}, bf16[32,8192]{1,0:T(8,128)(2,1)S(1)}, u32[]{:S(2)}, u32[]{:S(2)}) collective-permute-start(bf16[32,8192]{1,0:T(8,128)(2,1)S(1)} %pad_maximum_fusion.own_ref), channel_id=1, source_target_pairs={{0,1},{1,0},{2,3},{3,2},{4,5},{5,4},{6,7},{7,6},{8,9},{9,8},{10,11... | collective-permute-start | bytes 1572872 | tf_op jit(solution)/shard_map/ppermute | solution.py:379
  23.6 5.3 %collective-permute-start.8 = (bf16[64,4096]{1,0:T(8,128)(2,1)S(1)}, bf16[64,4096]{1,0:T(8,128)(2,1)S(1)}, u32[]{:S(2)}, u32[]{:S(2)}) collective-permute-start(bf16[64,4096]{1,0:T(8,128)(2,1)S(1)} %collective-permute-done.4.refs_2_), channel_id=1, source_target_pairs={{0,1},{1,0},{2,3},{3,2},{4,5},{5,4},{6,7},{7,6},{8,9},{9,8},{10,11... | collective-permute-start | bytes 1572872 | tf_op jit(solution)/shard_map/ppermute | solution.py:380
  26.4 2.4 %collective-permute-start.7 = (bf16[80,128]{1,0:T(8,128)(2,1)S(1)}, bf16[80,128]{1,0:T(8,128)(2,1)S(1)}, u32[]{:S(2)}, u32[]{:S(2)}) collective-permute-start(bf16[80,128]{1,0:T(8,128)(2,1)S(1)} %get-tuple-element.38.refs_4_), channel_id=1, source_target_pairs={{0,1},{1,0},{2,3},{3,2},{4,5},{5,4},{6,7},{7,6},{8,9},{9,8},{10,11... | collective-permute-start | bytes 61448 | tf_op jit(solution)/shard_map/ppermute | solution.py:428
  27.7 6.4 %collective-permute-start.13 = (bf16[80,128]{1,0:T(8,128)(2,1)S(1)}, bf16[80,128]{1,0:T(8,128)(2,1)S(1)}, u32[]{:S(2)}, u32[]{:S(2)}) collective-permute-start(bf16[80,128]{1,0:T(8,128)(2,1)S(1)} %get-tuple-element.38.refs_4_), channel_id=1, source_target_pairs={{0,2},{1,3},{2,0},{3,1},{4,6},{5,7},{6,4},{7,5},{8,10},{9,11},{10,... | collective-permute-start | bytes 61448 | tf_op jit(solution)/shard_map/ppermute | solution.py:427
  28.9 8.5 %collective-permute-start.10 = (bf16[32,128]{1,0:T(8,128)(2,1)S(1)}, bf16[32,128]{1,0:T(8,128)(2,1)S(1)}, u32[]{:S(2)}, u32[]{:S(2)}) collective-permute-start(bf16[32,128]{1,0:T(8,128)(2,1)S(1)} %pad_maximum_fusion.1), channel_id=1, source_target_pairs={{128,16},{129,33},{130,18},{131,35},{132,20},{133,37},{134,22},{13... | collective-permute-start | bytes 24584 | tf_op jit(solution)/shard_map/ppermute | solution.py:432
  30.2 11.5 %collective-permute-start.11 = (bf16[32,128]{1,0:T(8,128)(2,1)S(1)}, bf16[32,128]{1,0:T(8,128)(2,1)S(1)}, u32[]{:S(2)}, u32[]{:S(2)}) collective-permute-start(bf16[32,128]{1,0:T(8,128)(2,1)S(1)} %pad_maximum_fusion.1), channel_id=1, source_target_pairs={{128,96},{129,81},{130,98},{131,83},{132,100},{133,85},{134,102},{... | collective-permute-start | bytes 24584 | tf_op jit(solution)/shard_map/ppermute | solution.py:432
  31.5 12.1 %collective-permute-start.12 = (bf16[32,128]{1,0:T(8,128)(2,1)S(1)}, bf16[32,128]{1,0:T(8,128)(2,1)S(1)}, u32[]{:S(2)}, u32[]{:S(2)}) collective-permute-start(bf16[32,128]{1,0:T(8,128)(2,1)S(1)} %pad_maximum_fusion.1), channel_id=1, source_target_pairs={{128,48},{129,65},{130,50},{131,67},{132,52},{133,69},{134,54},{13... | collective-permute-start | bytes 24584 | tf_op jit(solution)/shard_map/ppermute | solution.py:432
  32.8 11.5 %collective-permute-start.9 = (bf16[32,128]{1,0:T(8,128)(2,1)S(1)}, bf16[32,128]{1,0:T(8,128)(2,1)S(1)}, u32[]{:S(2)}, u32[]{:S(2)}) collective-permute-start(bf16[32,128]{1,0:T(8,128)(2,1)S(1)} %pad_maximum_fusion.1), channel_id=1, source_target_pairs={{128,0},{129,113},{130,2},{131,115},{132,4},{133,117},{134,6},{135... | collective-permute-start | bytes 24584 | tf_op jit(solution)/shard_map/ppermute | solution.py:432
  34.1 10.2 %collective-permute-start.14 = (bf16[80,128]{1,0:T(8,128)(2,1)S(1)}, bf16[80,128]{1,0:T(8,128)(2,1)S(1)}, u32[]{:S(2)}, u32[]{:S(2)}) collective-permute-start(bf16[80,128]{1,0:T(8,128)(2,1)S(1)} %collective-permute-done.13.refs_6_), channel_id=1, source_target_pairs={{0,1},{1,0},{2,3},{3,2},{4,5},{5,4},{6,7},{7,6},{8,9},{9,8},{10,11... | collective-permute-start | bytes 61448 | tf_op jit(solution)/shard_map/ppermute | solution.py:429
  45.1 13.8 %collective-permute-start.15 = (f32[8,256]{1,0:T(8,128)S(1)}, f32[8,256]{1,0:T(8,128)S(1)}, u32[]{:S(2)}, u32[]{:S(2)}) collective-permute-start(f32[8,256]{1,0:T(8,128)S(1)} %get-tuple-element.43), channel_id=1, source_target_pairs={{0,128},{113,129},{2,130},{115,131},{4,132},{117,133},{6,134},{119... | collective-permute-start | bytes 24584 | tf_op jit(solution)/shard_map/ppermute | solution.py:437
  47.3 11.6 %collective-permute-start.16 = (f32[8,256]{1,0:T(8,128)S(1)}, f32[8,256]{1,0:T(8,128)S(1)}, u32[]{:S(2)}, u32[]{:S(2)}) collective-permute-start(f32[8,256]{1,0:T(8,128)S(1)} %get-tuple-element.44), channel_id=1, source_target_pairs={{16,128},{33,129},{18,130},{35,131},{20,132},{37,133},{22,134},{39... | collective-permute-start | bytes 24584 | tf_op jit(solution)/shard_map/ppermute | solution.py:437
  48.6 10.3 %collective-permute-start.17 = (f32[8,256]{1,0:T(8,128)S(1)}, f32[8,256]{1,0:T(8,128)S(1)}, u32[]{:S(2)}, u32[]{:S(2)}) collective-permute-start(f32[8,256]{1,0:T(8,128)S(1)} %get-tuple-element.45), channel_id=1, source_target_pairs={{96,128},{81,129},{98,130},{83,131},{100,132},{85,133},{102,134},{... | collective-permute-start | bytes 24584 | tf_op jit(solution)/shard_map/ppermute | solution.py:437
  50.8 8.1 %collective-permute-start.18 = (f32[8,256]{1,0:T(8,128)S(1)}, f32[8,256]{1,0:T(8,128)S(1)}, u32[]{:S(2)}, u32[]{:S(2)}) collective-permute-start(f32[8,256]{1,0:T(8,128)S(1)} %get-tuple-element.46), channel_id=1, source_target_pairs={{48,128},{65,129},{50,130},{67,131},{52,132},{69,133},{54,134},{71... | collective-permute-start | bytes 24584 | tf_op jit(solution)/shard_map/ppermute | solution.py:437
  55.2 2.2 %copy-start.2 = (bf16[256,8192]{1,0:T(8,128)(2,1)S(1)}, bf16[256,8192]{1,0:T(8,128)(2,1)}, u32[]{:S(2)}) copy-start(bf16[256,8192]{1,0:T(8,128)(2,1)} %w_ref.3) | copy-start | bytes 12582916
  57.4 2.8 %copy-start.3 = (bf16[256,8192]{1,0:T(8,128)(2,1)S(1)}, bf16[256,8192]{1,0:T(8,128)(2,1)}, u32[]{:S(2)}) copy-start(bf16[256,8192]{1,0:T(8,128)(2,1)} %w_ref.3) | copy-start | bytes 12582916
  58.9 19.9 %copy-start.8 = (bf16[1,1,4,8192]{3,2,1,0:T(4,128)(2,1)S(1)}, bf16[1,1,4,8192]{3,2,1,0:T(4,128)(2,1)}, u32[]{:S(2)}) copy-start(bf16[1,1,4,8192]{3,2,1,0:T(4,128)(2,1)} %param.8) | copy-start | bytes 196612
  58.9 1.3 %collective-permute-start.19 = (f32[8,256]{1,0:T(8,128)S(1)}, f32[8,256]{1,0:T(8,128)S(1)}, u32[]{:S(2)}, u32[]{:S(2)}) collective-permute-start(f32[8,256]{1,0:T(8,128)S(1)} %select_select_fusion.far_ref), channel_id=1, source_target_pairs={{0,1},{1,0},{2,3},{3,2},{4,5},{5,4},{6,7},{7,6},{8,9},{9,8},{10,11... | collective-permute-start | bytes 24584 | tf_op jit(solution)/shard_map/ppermute | solution.py:453
  61.8 2.0 %collective-permute-start.20 = (bf16[32,8192]{1,0:T(8,128)(2,1)S(1)}, bf16[32,8192]{1,0:T(8,128)(2,1)S(1)}, u32[]{:S(2)}, u32[]{:S(2)}) collective-permute-start(bf16[32,8192]{1,0:T(8,128)(2,1)S(1)} %get-tuple-element.52), channel_id=1, source_target_pairs={{0,1},{1,0},{2,3},{3,2},{4,5},{5,4},{6,7},{7,6},{8,9},{9,8},{10,11... | collective-permute-start | bytes 1572872 | tf_op jit(solution)/shard_map/ppermute | solution.py:457
  64.0 6.2 %collective-permute-start.21 = (bf16[8,8192]{1,0:T(8,128)(2,1)S(1)}, bf16[8,8192]{1,0:T(8,128)(2,1)S(1)}, u32[]{:S(2)}, u32[]{:S(2)}) collective-permute-start(bf16[8,8192]{1,0:T(8,128)(2,1)S(1)} %get-tuple-element.54), channel_id=1, source_target_pairs={{0,4},{1,5},{2,6},{3,7},{4,8},{5,9},{6,10},{7,11},{8,12},{9,13},{1... | collective-permute-start | bytes 393224 | tf_op jit(solution)/shard_map/ppermute | solution.py:459
  65.3 8.7 %collective-permute-start.22 = (bf16[8,8192]{1,0:T(8,128)(2,1)S(1)}, bf16[8,8192]{1,0:T(8,128)(2,1)S(1)}, u32[]{:S(2)}, u32[]{:S(2)}) collective-permute-start(bf16[8,8192]{1,0:T(8,128)(2,1)S(1)} %get-tuple-element.55), channel_id=1, source_target_pairs={{0,8},{1,9},{2,10},{3,11},{4,12},{5,13},{6,14},{7,15},{8,0},{9,1},... | collective-permute-start | bytes 393224 | tf_op jit(solution)/shard_map/ppermute | solution.py:459
  67.7 6.3 %collective-permute-start.23 = (bf16[8,8192]{1,0:T(8,128)(2,1)S(1)}, bf16[8,8192]{1,0:T(8,128)(2,1)S(1)}, u32[]{:S(2)}, u32[]{:S(2)}) collective-permute-start(bf16[8,8192]{1,0:T(8,128)(2,1)S(1)} %get-tuple-element.56), channel_id=1, source_target_pairs={{0,12},{1,13},{2,14},{3,15},{4,0},{5,1},{6,2},{7,3},{8,4},{9,5},{1... | collective-permute-start | bytes 393224 | tf_op jit(solution)/shard_map/ppermute | solution.py:459
  74.1 4.7 %collective-permute-start.24 = (bf16[4,8192]{1,0:T(4,128)(2,1)S(1)}, bf16[4,8192]{1,0:T(4,128)(2,1)S(1)}, u32[]{:S(2)}, u32[]{:S(2)}) collective-permute-start(bf16[4,8192]{1,0:T(4,128)(2,1)S(1)} %get-tuple-element.58), channel_id=1, source_target_pairs={{0,2},{1,3},{2,0},{3,1},{4,6},{5,7},{6,4},{7,5},{8,10},{9,11},{10,... | collective-permute-start | bytes 196616 | tf_op jit(solution)/shard_map/ppermute | solution.py:461

commit v4 on v3

--- a/solution.py
+++ b/solution.py
@@ -27,25 +27,52 @@
     return [(i, (i + 4 * k) % 16) for i in range(16)]
 
 
+DISTANCES = ((0, -1), (1, 2), (-2, -3), (3, 4))
+
+
 def after(value, *others):
     return lax.optimization_barrier((value,) + others)[0]
 
 
-def norm_kernel(own_ref, beside_ref, gain_ref, out_ref):
-    floated = jnp.concatenate([own_ref[...].astype(F32), beside_ref[...].astype(F32)], 0)
+def scaled(rows, gain):
+    floated = rows.astype(F32)
     spread = jnp.mean(floated * floated, axis=-1, keepdims=True)
-    out_ref[...] = (floated * lax.rsqrt(spread + 1e-05) * gain_ref[...]).astype(BF16)
-
-
-def norm(own, beside, gain):
+    return floated * lax.rsqrt(spread + 1e-05) * gain
+
+
+def stage_kernel(own_ref, gain_ref, out_ref, kept_ref):
+    out_ref[...] = scaled(own_ref[...], gain_ref[...])
+    kept_ref[...] = gain_ref[...]
+
+
+def norm_kernel(own_ref, gain_ref, beside_ref, out_ref):
+    beside = scaled(beside_ref[...], gain_ref[...])
+    out_ref[...] = jnp.concatenate([own_ref[...], beside], 0).astype(BF16)
+
+
+def stage(own, gain):
+    return pl.pallas_call(
+        stage_kernel,
+        cost_estimate=COST,
+        compiler_params=LIMIT,
+        out_shape=(
+            jax.ShapeDtypeStruct(own.shape, F32),
+            jax.ShapeDtypeStruct(gain.shape, F32),
+        ),
+        in_specs=[VMEM] * 2,
+        out_specs=(VMEM,) * 2,
+    )(own, gain)
+
+
+def norm(own, gain, beside):
     return pl.pallas_call(
         norm_kernel,
         cost_estimate=COST,
         compiler_params=LIMIT,
         out_shape=jax.ShapeDtypeStruct((2 * own.shape[0], own.shape[1]), BF16),
-        in_specs=[VMEM, VMEM, VMEM],
+        in_specs=[VMEM] * 3,
         out_specs=VMEM,
-    )(own, beside, gain[None, :])
+    )(own, gain, beside)
 
 
 def touch_kernel(*refs):
@@ -249,9 +276,33 @@
     )(me, *kv, *packs, *asked)
 
 
+def distance_of(flags_ref, distances):
+    return jnp.where(flags_ref[2] == 0, distances[0], distances[1])
+
+
+def pick_kernel(flags_ref, match_ref, *refs):
+    far = jnp.zeros(refs[-1].shape, F32)
+    group, groups = flags_ref[1], match_ref.shape[0]
+    for ref, distances in zip(refs, DISTANCES):
+        prompt = lax.rem(group + distance_of(flags_ref, distances) + groups, groups)
+        far = jnp.where(match_ref[prompt] == group, ref[...], far)
+    refs[-1][...] = far
+
+
+def pick(flags, match, answers):
+    return pl.pallas_call(
+        pick_kernel,
+        cost_estimate=COST,
+        compiler_params=LIMIT,
+        out_shape=jax.ShapeDtypeStruct(answers[0].shape, F32),
+        in_specs=[SMEM] * 2 + [VMEM] * len(answers),
+        out_specs=VMEM,
+    )(flags, match, *answers)
+
+
 def merge_kernel(flags_ref, attended_ref, own_ref, far_ref, mate_ref, perm_ref, w_ref, keep_ref, give_ref):
     own = own_ref[...]
-    far = jnp.where(flags_ref[1] == 1, far_ref[:4], mate_ref[4:])
+    far = far_ref[:4] + mate_ref[4:]
     far = jnp.concatenate([far, far], 0)
     split = lambda packed: (
         packed[:, :HD], packed[:, HD : HD + 1], packed[:, 2 * HD - 1 : 2 * HD]
@@ -272,12 +323,30 @@
     attended = lax.dot_general(
         perm_ref[...], attended, (((0,), (0,)), ((), ())), preferred_element_type=F32
     ).astype(BF16)
+    keep_ref[...] = attended[: rows // 2]
+    shares_kernel_body(attended[rows // 2 :], w_ref, give_ref)
+
+
+def shares_kernel_body(attended, w_ref, out_ref):
     width = 1024
     for first in range(0, w_ref.shape[1], width):
         span = slice(first, first + width)
-        share = jnp.dot(attended, w_ref[:, span], preferred_element_type=F32).astype(BF16)
-        keep_ref[:, span] = share[: rows // 2]
-        give_ref[:, span] = share[rows // 2 :]
+        out_ref[:, span] = jnp.dot(attended, w_ref[:, span], preferred_element_type=F32).astype(BF16)
+
+
+def shares_kernel(attended_ref, w_ref, out_ref):
+    shares_kernel_body(attended_ref[...], w_ref, out_ref)
+
+
+def shares(attended, w_out):
+    return pl.pallas_call(
+        shares_kernel,
+        cost_estimate=COST,
+        compiler_params=LIMIT,
+        out_shape=jax.ShapeDtypeStruct((attended.shape[0], w_out.shape[1]), BF16),
+        in_specs=[VMEM] * 2,
+        out_specs=VMEM,
+    )(attended, w_out)
 
 
 def merge(flags, attended, own, far, mate, perm, w_out):
@@ -286,7 +355,7 @@
         merge_kernel,
         cost_estimate=COST,
         compiler_params=LIMIT,
-        out_shape=(half, half),
+        out_shape=(jax.ShapeDtypeStruct((half.shape[0], attended.shape[1]), BF16), half),
         in_specs=[SMEM] + [VMEM] * 6,
         out_specs=(VMEM,) * 2,
     )(flags, attended, own, far, mate, perm, w_out)
@@ -337,9 +406,6 @@
 
 def pick_row(table, selector):
     return jnp.sum(jnp.where(selector, table[None, :], 0), 1)
-
-
-DISTANCES = ((0, -1), (1, 2), (-2, -3), (3, 4))
 
 
 def carry(distances, groups, count, back):
@@ -368,10 +434,12 @@
     kcols = w_keyval.shape[1]
 
     beside = lax.ppermute(own_rows, "tp", YHI)
-    kv_sent = after(kv_t, beside)
+    staged = stage(own_rows, norm_gain[None, :])
+    beside = after(beside, staged)
+    kv_sent = after(kv_t, staged)
     kv_y = lax.ppermute(kv_sent, "tp", YHI)
     kv_core = lax.ppermute(kv_sent, "tp", CORE)
-    pair = norm(own_rows, beside, norm_gain)
+    pair = norm(*staged, beside)
     others = [lax.ppermute(pair, "tp", xshift(-k)) for k in range(1, XN)]
     token = touch(pair, w_query, w_keyval.T)
     others = after(others, kv_y, token)
@@ -394,7 +462,7 @@
 
     request = row_ids // STEPS
     step_ids = row_ids % STEPS
-    lengths = cache_lengths[0]
+    lengths = after(cache_lengths[0], pair)
     zero_one = jnp.zeros((1,), jnp.int32)
     bases = jnp.concatenate([jnp.full((1,), cache_len + row_count, jnp.int32), lengths])
     before = jnp.arange(lengths.shape[0])[None, :] < jnp.arange(lengths.shape[0])[:, None]
@@ -432,6 +500,7 @@
     asked = [lax.ppermute(leads, axes, carry(d, groups, count, False)) for d in DISTANCES]
     kv = [kv_t, kv_core, kv_y, kv_both]
     me = jnp.reshape(tp % 4, (1,)).astype(jnp.int32)
+    flags = jnp.stack([side, group, tp % 2]).astype(jnp.int32)
     answers = attend_far(me, kv, packs, asked)
     answers = [
         lax.ppermute(answer, axes, carry(d, groups, count, True))
@@ -441,20 +510,12 @@
     attended, lead_own = attend_main(me, query, bounds, w_out, kv, packs)
 
     answers = after(answers, attended)
-    far = jnp.zeros_like(answers[0])
-    here = jnp.zeros((), jnp.bool_)
-    for answer, pair_of in zip(answers, DISTANCES):
-        distance = jnp.where(tp % 2 == 0, pair_of[0], pair_of[1])
-        valid = jnp.sum(
-            jnp.where(jnp.arange(groups) == (group + distance) % groups, match, 0)
-        ) == group
-        far = jnp.where(valid, answer, far)
-        here = here | valid
+    far = pick(flags, match, answers)
     mate = lax.ppermute(far, "tp", CORE)
-    flags = jnp.stack([side, here.astype(jnp.int32)])
     keep, give = merge(flags, attended, lead_own, far, mate, perm, w_out)
 
     across = lax.ppermute(give, "tp", CORE)
+    keep = shares(keep, w_out)
     parts = add_core(keep, across)
     parts = [parts[0]] + [lax.ppermute(parts[k], "tp", xshift(k)) for k in range(1, XN)]
     summed, send = add_x(parts)

time: 80.4 us -> 76.5 us (0.951)
  the two profiles are of different devices: /device:TPU:1 before, /device:TPU:10 now
where the time goes in v4:
time: 76.5 us; the launch traced here: 76.1 us
  starting transfers between devices  37.2 us (49%)
  waiting for transfers between devices  22 us (29%)
  local copies, waits for them, and re-layouts  7.38 us (10%)
  Pallas kernels  7.24 us (9%)
  other arithmetic  1.88 us (2%)
    ppermute x4, starting transfers between devices, local(): lax.ppermute(leads, axes, carry(d, groups, count, False))  12.5 us
    unnamed x24, local copies, waits for them, and re-layouts  7.25 us
    ppermute x3, waiting for transfers between devices, local(): lax.ppermute(parts[k], 'tp', xshift(k))  6.49 us
    ppermute x4, starting transfers between devices, local(): lax.ppermute(answer, axes, carry(d, groups, count, True))  5.17 us
    ppermute x3, starting transfers between devices, local(): lax.ppermute(parts[k], 'tp', xshift(k))  4.84 us
    ppermute x3, starting transfers between devices, local(): others = [lax.ppermute(pair, 'tp', xshift(-k)) for k in range(1, XN)]  4.83 us
    ppermute x1, waiting for transfers between devices, local(): summed = summed + lax.ppermute(send, 'tp', YHI).astype(F32)  4.48 us
    ppermute x4, waiting for transfers between devices, local(): lax.ppermute(answer, axes, carry(d, groups, count, True))  3.04 us
  transfers between devices with their start and end apart: 25, of which 15 were waited for; matrix products, arithmetic and copies ran while one was open for 2% of the time, Pallas kernels for 5%

profile of v4, /device:TPU:10, one launch (start us, length us, event | category | flops | bytes accessed | tf_op | source)
XLA Modules:
  0.0 76.1 jit_solution(16486418131189050915)
XLA Ops:
  0.0 2.3 %collective-permute-start = (bf16[4,8192]{1,0:T(4,128)(2,1)}, bf16[4,8192]{1,0:T(4,128)(2,1)S(1)}, u32[]{:S(2)}, u32[]{:S(2)}) collective-permute-start(bf16[4,8192]{1,0:T(4,128)(2,1)} %bitcast.24), channel_id=1, source_target_pairs={{0,2},{1,3},{2,0},{3,1},{4,6},{5,7},{6,4},{7,5},{8,10},{9,11},{10,... | collective-permute-start | bytes 196616 | tf_op jit(solution)/shard_map/ppermute | solution.py:436
  2.3 0.9 %copy-done.7 = bf16[1,1,4,8192]{3,2,1,0:T(4,128)(2,1)S(1)} copy-done((bf16[1,1,4,8192]{3,2,1,0:T(4,128)(2,1)S(1)}, bf16[1,1,4,8192]{3,2,1,0:T(4,128)(2,1)}, u32[]{:S(2)}) %copy-start.7) | copy-done | bytes 65560
  3.2 0.8 copy-done.9
  3.9 0.2 shard_map.82
  4.1 1.3 %collective-permute-start.4 = (bf16[64,4096]{1,0:T(8,128)(2,1)}, bf16[64,4096]{1,0:T(8,128)(2,1)S(1)}, u32[]{:S(2)}, u32[]{:S(2)}) collective-permute-start(bf16[64,4096]{1,0:T(8,128)(2,1)} %bitcast.20), channel_id=1, source_target_pairs={{0,2},{1,3},{2,0},{3,1},{4,6},{5,7},{6,4},{7,5},{8,10},{9,11},{10,... | collective-permute-start | bytes 1572872 | tf_op jit(solution)/shard_map/ppermute | solution.py:440
  5.6 0.3 collective-permute-done.beside_ref
  6.0 0.2 shard_map.83.refs_0_
  6.2 0.6 collective-permute-start.1
  6.8 2.4 %collective-permute-start.2 = (bf16[8,8192]{1,0:T(8,128)(2,1)S(1)}, bf16[8,8192]{1,0:T(8,128)(2,1)S(1)}, u32[]{:S(2)}, u32[]{:S(2)}) collective-permute-start(bf16[8,8192]{1,0:T(8,128)(2,1)S(1)} %shard_map.83.refs_0_), channel_id=1, source_target_pairs={{0,8},{1,9},{2,10},{3,11},{4,12},{5,13},{6,14},{7,15},{8,0},{9,1},... | collective-permute-start | bytes 393224 | tf_op jit(solution)/shard_map/ppermute | solution.py:443
  9.2 1.8 %collective-permute-start.3 = (bf16[8,8192]{1,0:T(8,128)(2,1)S(1)}, bf16[8,8192]{1,0:T(8,128)(2,1)S(1)}, u32[]{:S(2)}, u32[]{:S(2)}) collective-permute-start(bf16[8,8192]{1,0:T(8,128)(2,1)S(1)} %shard_map.83.refs_0_), channel_id=1, source_target_pairs={{0,4},{1,5},{2,6},{3,7},{4,8},{5,9},{6,10},{7,11},{8,12},{9,13},{1... | collective-permute-start | bytes 393224 | tf_op jit(solution)/shard_map/ppermute | solution.py:443
  11.0 2.2 %copy-done.2 = bf16[8192,256]{1,0:T(8,128)(2,1)S(1)} copy-done((bf16[8192,256]{1,0:T(8,128)(2,1)S(1)}, bf16[8192,256]{1,0:T(8,128)(2,1)}, u32[]{:S(2)}) %copy-start.2) | copy-done | bytes 4194328
  13.2 1.2 %copy-done.4 = bf16[8192,64]{0,1:T(8,128)(2,1)S(1)} copy-done((bf16[8192,64]{0,1:T(8,128)(2,1)S(1)}, bf16[8192,64]{0,1:T(8,128)(2,1)}, u32[]{:S(2)}) %copy-start.4) | copy-done | bytes 1048600
  14.5 0.1 select_reduce_fusion.3
  14.6 0.1 pad_add_fusion.3
  14.7 0.1 select_reduce_fusion.1
  14.8 0.8 %collective-permute-done.2 = bf16[8,8192]{1,0:T(8,128)(2,1)S(1)} collective-permute-done((bf16[8,8192]{1,0:T(8,128)(2,1)S(1)}, bf16[8,8192]{1,0:T(8,128)(2,1)S(1)}, u32[]{:S(2)}, u32[]{:S(2)}) %collective-permute-start.2) | collective-permute-done | bytes 131104 | tf_op jit(solution)/shard_map/ppermute | solution.py:443
  15.6 0.9 %collective-permute-done.3 = bf16[8,8192]{1,0:T(8,128)(2,1)S(1)} collective-permute-done((bf16[8,8192]{1,0:T(8,128)(2,1)S(1)}, bf16[8,8192]{1,0:T(8,128)(2,1)S(1)}, u32[]{:S(2)}, u32[]{:S(2)}) %collective-permute-start.3) | collective-permute-done | bytes 131104 | tf_op jit(solution)/shard_map/ppermute | solution.py:443
  16.4 2.9 %collective-permute-done.4.refs_2_ = bf16[64,4096]{1,0:T(8,128)(2,1)S(1)} collective-permute-done((bf16[64,4096]{1,0:T(8,128)(2,1)}, bf16[64,4096]{1,0:T(8,128)(2,1)S(1)}, u32[]{:S(2)}, u32[]{:S(2)}) %collective-permute-start.4) | collective-permute-done | bytes 524320 | tf_op jit(solution)/shard_map/ppermute | solution.py:440
  19.3 0.1 collective-permute-start.5
  19.4 0.1 select_reduce_fusion
  19.5 0.6 collective-permute-start.8
  20.1 0.2 fusion.4
  20.3 0.3 fusion
  20.6 0.7 collective-permute-done.5.mate_ref
  21.3 1.4 %shard_map.85 = (bf16[64,256]{1,0:T(8,128)(2,1)S(1)}, bf16[80,128]{1,0:T(8,128)(2,1)S(1)}) custom-call(bf16[32,8192]{1,0:T(8,128)(2,1)S(1)} %pad_maximum_fusion.own_ref, bf16[32,8192]{1,0:T(8,128)(2,1)S(1)} %collective-permute-done.5.mate_ref, bf16[8192,256]{1,0:T(8,128)(2,1)S(1)} %copy-done.3, bf16[64,8192]{1,0:T(8,128)(2,1)S(1)} %bitcast.19, ...), custom_call_target="tpu_custom_call" | custom-call | flops 1 | bytes 1 | tf_op jit(solution)/shard_map/pallas_call | solution.py:130
  22.7 0.2 collective-permute-start.7
  22.9 0.1 pad_add_fusion.2.flags_ref
  23.0 1.3 %collective-permute-start.13 = (bf16[80,128]{1,0:T(8,128)(2,1)S(1)}, bf16[80,128]{1,0:T(8,128)(2,1)S(1)}, u32[]{:S(2)}, u32[]{:S(2)}) collective-permute-start(bf16[80,128]{1,0:T(8,128)(2,1)S(1)} %get-tuple-element.46.refs_4_), channel_id=1, source_target_pairs={{0,2},{1,3},{2,0},{3,1},{4,6},{5,7},{6,4},{7,5},{8,10},{9,11},{10,... | collective-permute-start | bytes 61448 | tf_op jit(solution)/shard_map/ppermute | solution.py:495
  24.3 2.9 %collective-permute-start.9 = (bf16[32,128]{1,0:T(8,128)(2,1)S(1)}, bf16[32,128]{1,0:T(8,128)(2,1)S(1)}, u32[]{:S(2)}, u32[]{:S(2)}) collective-permute-start(bf16[32,128]{1,0:T(8,128)(2,1)S(1)} %pad_maximum_fusion.1), channel_id=1, source_target_pairs={{128,0},{129,113},{130,2},{131,115},{132,4},{133,117},{134,6},{135... | collective-permute-start | bytes 24584 | tf_op jit(solution)/shard_map/ppermute | solution.py:500
  27.3 2.6 %collective-permute-start.10 = (bf16[32,128]{1,0:T(8,128)(2,1)S(1)}, bf16[32,128]{1,0:T(8,128)(2,1)S(1)}, u32[]{:S(2)}, u32[]{:S(2)}) collective-permute-start(bf16[32,128]{1,0:T(8,128)(2,1)S(1)} %pad_maximum_fusion.1), channel_id=1, source_target_pairs={{128,16},{129,33},{130,18},{131,35},{132,20},{133,37},{134,22},{13... | collective-permute-start | bytes 24584 | tf_op jit(solution)/shard_map/ppermute | solution.py:500
  29.9 5.7 %collective-permute-start.11 = (bf16[32,128]{1,0:T(8,128)(2,1)S(1)}, bf16[32,128]{1,0:T(8,128)(2,1)S(1)}, u32[]{:S(2)}, u32[]{:S(2)}) collective-permute-start(bf16[32,128]{1,0:T(8,128)(2,1)S(1)} %pad_maximum_fusion.1), channel_id=1, source_target_pairs={{128,96},{129,81},{130,98},{131,83},{132,100},{133,85},{134,102},{... | collective-permute-start | bytes 24584 | tf_op jit(solution)/shard_map/ppermute | solution.py:500
  35.6 1.3 %collective-permute-start.12 = (bf16[32,128]{1,0:T(8,128)(2,1)S(1)}, bf16[32,128]{1,0:T(8,128)(2,1)S(1)}, u32[]{:S(2)}, u32[]{:S(2)}) collective-permute-start(bf16[32,128]{1,0:T(8,128)(2,1)S(1)} %pad_maximum_fusion.1), channel_id=1, source_target_pairs={{128,48},{129,65},{130,50},{131,67},{132,52},{133,69},{134,54},{13... | collective-permute-start | bytes 24584 | tf_op jit(solution)/shard_map/ppermute | solution.py:500
  36.9 0.8 %collective-permute-start.14 = (bf16[80,128]{1,0:T(8,128)(2,1)S(1)}, bf16[80,128]{1,0:T(8,128)(2,1)S(1)}, u32[]{:S(2)}, u32[]{:S(2)}) collective-permute-start(bf16[80,128]{1,0:T(8,128)(2,1)S(1)} %collective-permute-done.13.refs_6_), channel_id=1, source_target_pairs={{0,1},{1,0},{2,3},{3,2},{4,5},{5,4},{6,7},{7,6},{8,9},{9,8},{10,11... | collective-permute-start | bytes 61448 | tf_op jit(solution)/shard_map/ppermute | solution.py:497
  37.8 0.5 collective-permute-done.12.refs_11_
  38.2 0.4 collective-permute-done.14.refs_7_
  38.6 0.8 %shard_map.87 = (f32[8,256]{1,0:T(8,128)S(1)}, f32[8,256]{1,0:T(8,128)S(1)}, f32[8,256]{1,0:T(8,128)S(1)}, f32[8,256]{1,0:T(8,128)S(1)}) custom-call(s32[1]{0:T(128)} %bitcast.4.me_ref, bf16[64,4096]{1,0:T(8,128)(2,1)S(1)} %bitcast.22, bf16[64,4096]{1,0:T(8,128)(2,1)S(1)} %collective-permute-done.6.refs_1_, ...), custom_call_target="tpu_custom_call" | custom-call | flops 1 | bytes 1 | tf_op jit(solution)/shard_map/pallas_call | solution.py:268
  39.4 1.3 %collective-permute-start.15 = (f32[8,256]{1,0:T(8,128)S(1)}, f32[8,256]{1,0:T(8,128)S(1)}, u32[]{:S(2)}, u32[]{:S(2)}) collective-permute-start(f32[8,256]{1,0:T(8,128)S(1)} %get-tuple-element.51), channel_id=1, source_target_pairs={{0,128},{113,129},{2,130},{115,131},{4,132},{117,133},{6,134},{119... | collective-permute-start | bytes 24584 | tf_op jit(solution)/shard_map/ppermute | solution.py:506
  40.7 1.3 %collective-permute-start.16 = (f32[8,256]{1,0:T(8,128)S(1)}, f32[8,256]{1,0:T(8,128)S(1)}, u32[]{:S(2)}, u32[]{:S(2)}) collective-permute-start(f32[8,256]{1,0:T(8,128)S(1)} %get-tuple-element.52), channel_id=1, source_target_pairs={{16,128},{33,129},{18,130},{35,131},{20,132},{37,133},{22,134},{39... | collective-permute-start | bytes 24584 | tf_op jit(solution)/shard_map/ppermute | solution.py:506
  42.0 1.3 %collective-permute-start.17 = (f32[8,256]{1,0:T(8,128)S(1)}, f32[8,256]{1,0:T(8,128)S(1)}, u32[]{:S(2)}, u32[]{:S(2)}) collective-permute-start(f32[8,256]{1,0:T(8,128)S(1)} %get-tuple-element.53), channel_id=1, source_target_pairs={{96,128},{81,129},{98,130},{83,131},{100,132},{85,133},{102,134},{... | collective-permute-start | bytes 24584 | tf_op jit(solution)/shard_map/ppermute | solution.py:506
  43.3 1.3 %collective-permute-start.18 = (f32[8,256]{1,0:T(8,128)S(1)}, f32[8,256]{1,0:T(8,128)S(1)}, u32[]{:S(2)}, u32[]{:S(2)}) collective-permute-start(f32[8,256]{1,0:T(8,128)S(1)} %get-tuple-element.54), channel_id=1, source_target_pairs={{48,128},{65,129},{50,130},{67,131},{52,132},{69,133},{54,134},{71... | collective-permute-start | bytes 24584 | tf_op jit(solution)/shard_map/ppermute | solution.py:506
  44.6 0.1 add_add_fusion
  44.7 0.1 copy.12.bounds_ref
  44.8 2.2 %copy-done = bf16[256,8192]{1,0:T(8,128)(2,1)S(1)} copy-done((bf16[256,8192]{1,0:T(8,128)(2,1)S(1)}, bf16[256,8192]{1,0:T(8,128)(2,1)}, u32[]{:S(2)}) %copy-start) | copy-done | bytes 4194328
  47.0 1.5 %shard_map.86 = (bf16[64,256]{1,0:T(8,128)(2,1)S(1)}, f32[8,256]{1,0:T(8,128)S(1)}) custom-call(s32[1]{0:T(128)} %bitcast.4.me_ref, bf16[64,256]{1,0:T(8,128)(2,1)S(1)} %get-tuple-element.48.q_ref, s32[128,4]{1,0:T(8,128)S(1)} %copy.12.bounds_ref, bf16[256,8192]{1,0:T(8,128)(2,1)S(1)} %copy-done, bf16[64,4096]{1,0:T(8,128)(2,1)S(1)} %bitcast.23, ...), custom_call_target="tpu_custom_call" | custom-call | flops 1 | bytes 1 | tf_op jit(solution)/shard_map/pallas_call | solution.py:253
  48.5 2.3 %collective-permute-done.17.refs_2_ = f32[8,256]{1,0:T(8,128)S(1)} collective-permute-done((f32[8,256]{1,0:T(8,128)S(1)}, f32[8,256]{1,0:T(8,128)S(1)}, u32[]{:S(2)}, u32[]{:S(2)}) %collective-permute-start.17) | collective-permute-done | bytes 8224 | tf_op jit(solution)/shard_map/ppermute | solution.py:506
  50.8 0.8 %collective-permute-done.18.refs_3_ = f32[8,256]{1,0:T(8,128)S(1)} collective-permute-done((f32[8,256]{1,0:T(8,128)S(1)}, f32[8,256]{1,0:T(8,128)S(1)}, u32[]{:S(2)}, u32[]{:S(2)}) %collective-permute-start.18) | collective-permute-done | bytes 8224 | tf_op jit(solution)/shard_map/ppermute | solution.py:506
  51.6 0.6 shard_map.88.far_ref
  52.1 1.4 %collective-permute-start.19 = (f32[8,256]{1,0:T(8,128)S(1)}, f32[8,256]{1,0:T(8,128)S(1)}, u32[]{:S(2)}, u32[]{:S(2)}) collective-permute-start(f32[8,256]{1,0:T(8,128)S(1)} %shard_map.88.far_ref), channel_id=1, source_target_pairs={{0,1},{1,0},{2,3},{3,2},{4,5},{5,4},{6,7},{7,6},{8,9},{9,8},{10,11... | collective-permute-start | bytes 24584 | tf_op jit(solution)/shard_map/ppermute | solution.py:514
  53.5 0.8 %collective-permute-done.19.mate_ref = f32[8,256]{1,0:T(8,128)S(1)} collective-permute-done((f32[8,256]{1,0:T(8,128)S(1)}, f32[8,256]{1,0:T(8,128)S(1)}, u32[]{:S(2)}, u32[]{:S(2)}) %collective-permute-start.19) | collective-permute-done | bytes 8224 | tf_op jit(solution)/shard_map/ppermute | solution.py:514
  54.4 1.6 %shard_map.89 = (bf16[32,256]{1,0:T(8,128)(2,1)S(1)}, bf16[32,8192]{1,0:T(8,128)(2,1)S(1)}) custom-call(s32[3]{0:T(128)S(1)} %pad_add_fusion.2.flags_ref, bf16[64,256]{1,0:T(8,128)(2,1)S(1)} %get-tuple-element.49.attended_ref, f32[8,256]{1,0:T(8,128)S(1)} %get-tuple-element.50.own_ref, f32[8,256]{1,0:T(8,128)S(1)} %shard_map.88.far_ref, ...), custom_call_target="tpu_custom_call" | custom-call | flops 1 | bytes 1 | tf_op jit(solution)/shard_map/pallas_call | solution.py:354
  56.0 0.4 collective-permute-start.20
  56.4 0.8 %shard_map.90.own_ref = bf16[32,8192]{1,0:T(8,128)(2,1)S(1)} custom-call(bf16[32,256]{1,0:T(8,128)(2,1)S(1)} %get-tuple-element.59.attended_ref, bf16[256,8192]{1,0:T(8,128)(2,1)S(1)} %copy-done.1), custom_call_target="tpu_custom_call" | custom-call | flops 1 | bytes 1 | tf_op jit(solution)/shard_map/pallas_call | solution.py:342
  57.3 0.7 collective-permute-done.20.across_ref
  58.0 0.1 shard_map.91
  58.1 1.6 %collective-permute-start.21 = (bf16[8,8192]{1,0:T(8,128)(2,1)S(1)}, bf16[8,8192]{1,0:T(8,128)(2,1)S(1)}, u32[]{:S(2)}, u32[]{:S(2)}) collective-permute-start(bf16[8,8192]{1,0:T(8,128)(2,1)S(1)} %get-tuple-element.62), channel_id=1, source_target_pairs={{0,4},{1,5},{2,6},{3,7},{4,8},{5,9},{6,10},{7,11},{8,12},{9,13},{1... | collective-permute-start | bytes 393224 | tf_op jit(solution)/shard_map/ppermute | solution.py:520
  59.7 1.8 %collective-permute-start.22 = (bf16[8,8192]{1,0:T(8,128)(2,1)S(1)}, bf16[8,8192]{1,0:T(8,128)(2,1)S(1)}, u32[]{:S(2)}, u32[]{:S(2)}) collective-permute-start(bf16[8,8192]{1,0:T(8,128)(2,1)S(1)} %get-tuple-element.63), channel_id=1, source_target_pairs={{0,8},{1,9},{2,10},{3,11},{4,12},{5,13},{6,14},{7,15},{8,0},{9,1},... | collective-permute-start | bytes 393224 | tf_op jit(solution)/shard_map/ppermute | solution.py:520
  61.5 1.5 %collective-permute-start.23 = (bf16[8,8192]{1,0:T(8,128)(2,1)S(1)}, bf16[8,8192]{1,0:T(8,128)(2,1)S(1)}, u32[]{:S(2)}, u32[]{:S(2)}) collective-permute-start(bf16[8,8192]{1,0:T(8,128)(2,1)S(1)} %get-tuple-element.64), channel_id=1, source_target_pairs={{0,12},{1,13},{2,14},{3,15},{4,0},{5,1},{6,2},{7,3},{8,4},{9,5},{1... | collective-permute-start | bytes 393224 | tf_op jit(solution)/shard_map/ppermute | solution.py:520
  63.0 1.3 %collective-permute-done.21.b_ref = bf16[8,8192]{1,0:T(8,128)(2,1)S(1)} collective-permute-done((bf16[8,8192]{1,0:T(8,128)(2,1)S(1)}, bf16[8,8192]{1,0:T(8,128)(2,1)S(1)}, u32[]{:S(2)}, u32[]{:S(2)}) %collective-permute-start.21) | collective-permute-done | bytes 131104 | tf_op jit(solution)/shard_map/ppermute | solution.py:520
  64.2 3.4 %collective-permute-done.22.c_ref = bf16[8,8192]{1,0:T(8,128)(2,1)S(1)} collective-permute-done((bf16[8,8192]{1,0:T(8,128)(2,1)S(1)}, bf16[8,8192]{1,0:T(8,128)(2,1)S(1)}, u32[]{:S(2)}, u32[]{:S(2)}) %collective-permute-start.22) | collective-permute-done | bytes 131104 | tf_op jit(solution)/shard_map/ppermute | solution.py:520
  67.6 1.9 %collective-permute-done.23.d_ref = bf16[8,8192]{1,0:T(8,128)(2,1)S(1)} collective-permute-done((bf16[8,8192]{1,0:T(8,128)(2,1)S(1)}, bf16[8,8192]{1,0:T(8,128)(2,1)S(1)}, u32[]{:S(2)}, u32[]{:S(2)}) %collective-permute-start.23) | collective-permute-done | bytes 131104 | tf_op jit(solution)/shard_map/ppermute | solution.py:520
  69.4 0.1 shard_map.92
  69.5 1.4 %collective-permute-start.24 = (bf16[4,8192]{1,0:T(4,128)(2,1)S(1)}, bf16[4,8192]{1,0:T(4,128)(2,1)S(1)}, u32[]{:S(2)}, u32[]{:S(2)}) collective-permute-start(bf16[4,8192]{1,0:T(4,128)(2,1)S(1)} %get-tuple-element.66), channel_id=1, source_target_pairs={{0,2},{1,3},{2,0},{3,1},{4,6},{5,7},{6,4},{7,5},{8,10},{9,11},{10,... | collective-permute-start | bytes 196616 | tf_op jit(solution)/shard_map/ppermute | solution.py:522
  70.9 4.5 %collective-permute-done.24 = bf16[4,8192]{1,0:T(4,128)(2,1)S(1)} collective-permute-done((bf16[4,8192]{1,0:T(4,128)(2,1)S(1)}, bf16[4,8192]{1,0:T(4,128)(2,1)S(1)}, u32[]{:S(2)}, u32[]{:S(2)}) %collective-permute-start.24) | collective-permute-done | bytes 65568 | tf_op jit(solution)/shard_map/ppermute | solution.py:522
  75.4 0.7 fusion.1
  (46 shorter events, 0.2 us)
Async XLA Ops:
  0.0 14.4 %copy-start.11 = (s32[1,31]{1,0:T(1,128)S(1)}, s32[1,31]{1,0:T(1,128)}, u32[]{:S(2)}) copy-start(s32[1,31]{1,0:T(1,128)} %param.15) | copy-start | bytes 376
  0.0 6.0 %collective-permute-start = (bf16[4,8192]{1,0:T(4,128)(2,1)}, bf16[4,8192]{1,0:T(4,128)(2,1)S(1)}, u32[]{:S(2)}, u32[]{:S(2)}) collective-permute-start(bf16[4,8192]{1,0:T(4,128)(2,1)} %bitcast.24), channel_id=1, source_target_pairs={{0,2},{1,3},{2,0},{3,1},{4,6},{5,7},{6,4},{7,5},{8,10},{9,11},{10,... | collective-permute-start | bytes 196616 | tf_op jit(solution)/shard_map/ppermute | solution.py:436
  2.3 0.9 %copy-start.7 = (bf16[1,1,4,8192]{3,2,1,0:T(4,128)(2,1)S(1)}, bf16[1,1,4,8192]{3,2,1,0:T(4,128)(2,1)}, u32[]{:S(2)}) copy-start(bf16[1,1,4,8192]{3,2,1,0:T(4,128)(2,1)} %param.8) | copy-start | bytes 196612
  3.2 0.8 copy-start.9
  4.1 15.2 %collective-permute-start.4 = (bf16[64,4096]{1,0:T(8,128)(2,1)}, bf16[64,4096]{1,0:T(8,128)(2,1)S(1)}, u32[]{:S(2)}, u32[]{:S(2)}) collective-permute-start(bf16[64,4096]{1,0:T(8,128)(2,1)} %bitcast.20), channel_id=1, source_target_pairs={{0,2},{1,3},{2,0},{3,1},{4,6},{5,7},{6,4},{7,5},{8,10},{9,11},{10,... | collective-permute-start | bytes 1572872 | tf_op jit(solution)/shard_map/ppermute | solution.py:440
  5.4 15.2 %collective-permute-start.6 = (bf16[64,4096]{1,0:T(8,128)(2,1)}, bf16[64,4096]{1,0:T(8,128)(2,1)S(1)}, u32[]{:S(2)}, u32[]{:S(2)}) collective-permute-start(bf16[64,4096]{1,0:T(8,128)(2,1)} %bitcast.21), channel_id=1, source_target_pairs={{0,1},{1,0},{2,3},{3,2},{4,5},{5,4},{6,7},{7,6},{8,9},{9,8},{10,11... | collective-permute-start | bytes 1572872 | tf_op jit(solution)/shard_map/ppermute | solution.py:441
  6.2 8.6 %collective-permute-start.1 = (bf16[8,8192]{1,0:T(8,128)(2,1)S(1)}, bf16[8,8192]{1,0:T(8,128)(2,1)S(1)}, u32[]{:S(2)}, u32[]{:S(2)}) collective-permute-start(bf16[8,8192]{1,0:T(8,128)(2,1)S(1)} %shard_map.83.refs_0_), channel_id=1, source_target_pairs={{0,12},{1,13},{2,14},{3,15},{4,0},{5,1},{6,2},{7,3},{8,4},{9,5},{1... | collective-permute-start | bytes 393224 | tf_op jit(solution)/shard_map/ppermute | solution.py:443
  6.8 8.8 %collective-permute-start.2 = (bf16[8,8192]{1,0:T(8,128)(2,1)S(1)}, bf16[8,8192]{1,0:T(8,128)(2,1)S(1)}, u32[]{:S(2)}, u32[]{:S(2)}) collective-permute-start(bf16[8,8192]{1,0:T(8,128)(2,1)S(1)} %shard_map.83.refs_0_), channel_id=1, source_target_pairs={{0,8},{1,9},{2,10},{3,11},{4,12},{5,13},{6,14},{7,15},{8,0},{9,1},... | collective-permute-start | bytes 393224 | tf_op jit(solution)/shard_map/ppermute | solution.py:443
  9.2 7.2 %collective-permute-start.3 = (bf16[8,8192]{1,0:T(8,128)(2,1)S(1)}, bf16[8,8192]{1,0:T(8,128)(2,1)S(1)}, u32[]{:S(2)}, u32[]{:S(2)}) collective-permute-start(bf16[8,8192]{1,0:T(8,128)(2,1)S(1)} %shard_map.83.refs_0_), channel_id=1, source_target_pairs={{0,4},{1,5},{2,6},{3,7},{4,8},{5,9},{6,10},{7,11},{8,12},{9,13},{1... | collective-permute-start | bytes 393224 | tf_op jit(solution)/shard_map/ppermute | solution.py:443
  11.0 2.2 %copy-start.2 = (bf16[8192,256]{1,0:T(8,128)(2,1)S(1)}, bf16[8192,256]{1,0:T(8,128)(2,1)}, u32[]{:S(2)}) copy-start(bf16[8192,256]{1,0:T(8,128)(2,1)} %wq_ref.1) | copy-start | bytes 12582916
  13.2 1.2 %copy-start.4 = (bf16[8192,64]{0,1:T(8,128)(2,1)S(1)}, bf16[8192,64]{0,1:T(8,128)(2,1)}, u32[]{:S(2)}) copy-start(bf16[8192,64]{0,1:T(8,128)(2,1)} %param.11) | copy-start | bytes 3145732
  14.4 6.9 %copy-start.3 = (bf16[8192,256]{1,0:T(8,128)(2,1)S(1)}, bf16[8192,256]{1,0:T(8,128)(2,1)}, u32[]{:S(2)}) copy-start(bf16[8192,256]{1,0:T(8,128)(2,1)} %wq_ref.1) | copy-start | bytes 12582916
  14.4 6.9 %copy-start.5 = (bf16[8192,64]{0,1:T(8,128)(2,1)S(1)}, bf16[8192,64]{0,1:T(8,128)(2,1)}, u32[]{:S(2)}) copy-start(bf16[8192,64]{0,1:T(8,128)(2,1)} %param.11) | copy-start | bytes 3145732
  14.4 24.2 %copy-start.6 = (bf16[1,1,4096,64]{2,3,1,0:T(8,128)(2,1)S(1)}, bf16[1,1,4096,64]{2,3,1,0:T(8,128)(2,1)}, u32[]{:S(2)}) copy-start(bf16[1,1,4096,64]{2,3,1,0:T(8,128)(2,1)} %param.13) | copy-start | bytes 1572868
  19.3 2.0 %collective-permute-start.5 = (bf16[32,8192]{1,0:T(8,128)(2,1)S(1)}, bf16[32,8192]{1,0:T(8,128)(2,1)S(1)}, u32[]{:S(2)}, u32[]{:S(2)}) collective-permute-start(bf16[32,8192]{1,0:T(8,128)(2,1)S(1)} %pad_maximum_fusion.own_ref), channel_id=1, source_target_pairs={{0,1},{1,0},{2,3},{3,2},{4,5},{5,4},{6,7},{7,6},{8,9},{9,8},{10,11... | collective-permute-start | bytes 1572872 | tf_op jit(solution)/shard_map/ppermute | solution.py:447
  19.5 4.8 %collective-permute-start.8 = (bf16[64,4096]{1,0:T(8,128)(2,1)S(1)}, bf16[64,4096]{1,0:T(8,128)(2,1)S(1)}, u32[]{:S(2)}, u32[]{:S(2)}) collective-permute-start(bf16[64,4096]{1,0:T(8,128)(2,1)S(1)} %collective-permute-done.4.refs_2_), channel_id=1, source_target_pairs={{0,1},{1,0},{2,3},{3,2},{4,5},{5,4},{6,7},{7,6},{8,9},{9,8},{10,11... | collective-permute-start | bytes 1572872 | tf_op jit(solution)/shard_map/ppermute | solution.py:448
  22.7 1.6 %collective-permute-start.7 = (bf16[80,128]{1,0:T(8,128)(2,1)S(1)}, bf16[80,128]{1,0:T(8,128)(2,1)S(1)}, u32[]{:S(2)}, u32[]{:S(2)}) collective-permute-start(bf16[80,128]{1,0:T(8,128)(2,1)S(1)} %get-tuple-element.46.refs_4_), channel_id=1, source_target_pairs={{0,1},{1,0},{2,3},{3,2},{4,5},{5,4},{6,7},{7,6},{8,9},{9,8},{10,11... | collective-permute-start | bytes 61448 | tf_op jit(solution)/shard_map/ppermute | solution.py:496
  23.0 13.9 %collective-permute-start.13 = (bf16[80,128]{1,0:T(8,128)(2,1)S(1)}, bf16[80,128]{1,0:T(8,128)(2,1)S(1)}, u32[]{:S(2)}, u32[]{:S(2)}) collective-permute-start(bf16[80,128]{1,0:T(8,128)(2,1)S(1)} %get-tuple-element.46.refs_4_), channel_id=1, source_target_pairs={{0,2},{1,3},{2,0},{3,1},{4,6},{5,7},{6,4},{7,5},{8,10},{9,11},{10,... | collective-permute-start | bytes 61448 | tf_op jit(solution)/shard_map/ppermute | solution.py:495
  24.3 13.4 %collective-permute-start.9 = (bf16[32,128]{1,0:T(8,128)(2,1)S(1)}, bf16[32,128]{1,0:T(8,128)(2,1)S(1)}, u32[]{:S(2)}, u32[]{:S(2)}) collective-permute-start(bf16[32,128]{1,0:T(8,128)(2,1)S(1)} %pad_maximum_fusion.1), channel_id=1, source_target_pairs={{128,0},{129,113},{130,2},{131,115},{132,4},{133,117},{134,6},{135... | collective-permute-start | bytes 24584 | tf_op jit(solution)/shard_map/ppermute | solution.py:500
  27.3 10.5 %collective-permute-start.10 = (bf16[32,128]{1,0:T(8,128)(2,1)S(1)}, bf16[32,128]{1,0:T(8,128)(2,1)S(1)}, u32[]{:S(2)}, u32[]{:S(2)}) collective-permute-start(bf16[32,128]{1,0:T(8,128)(2,1)S(1)} %pad_maximum_fusion.1), channel_id=1, source_target_pairs={{128,16},{129,33},{130,18},{131,35},{132,20},{133,37},{134,22},{13... | collective-permute-start | bytes 24584 | tf_op jit(solution)/shard_map/ppermute | solution.py:500
  29.9 7.9 %collective-permute-start.11 = (bf16[32,128]{1,0:T(8,128)(2,1)S(1)}, bf16[32,128]{1,0:T(8,128)(2,1)S(1)}, u32[]{:S(2)}, u32[]{:S(2)}) collective-permute-start(bf16[32,128]{1,0:T(8,128)(2,1)S(1)} %pad_maximum_fusion.1), channel_id=1, source_target_pairs={{128,96},{129,81},{130,98},{131,83},{132,100},{133,85},{134,102},{... | collective-permute-start | bytes 24584 | tf_op jit(solution)/shard_map/ppermute | solution.py:500
  35.6 2.6 %collective-permute-start.12 = (bf16[32,128]{1,0:T(8,128)(2,1)S(1)}, bf16[32,128]{1,0:T(8,128)(2,1)S(1)}, u32[]{:S(2)}, u32[]{:S(2)}) collective-permute-start(bf16[32,128]{1,0:T(8,128)(2,1)S(1)} %pad_maximum_fusion.1), channel_id=1, source_target_pairs={{128,48},{129,65},{130,50},{131,67},{132,52},{133,69},{134,54},{13... | collective-permute-start | bytes 24584 | tf_op jit(solution)/shard_map/ppermute | solution.py:500
  36.9 1.7 %collective-permute-start.14 = (bf16[80,128]{1,0:T(8,128)(2,1)S(1)}, bf16[80,128]{1,0:T(8,128)(2,1)S(1)}, u32[]{:S(2)}, u32[]{:S(2)}) collective-permute-start(bf16[80,128]{1,0:T(8,128)(2,1)S(1)} %collective-permute-done.13.refs_6_), channel_id=1, source_target_pairs={{0,1},{1,0},{2,3},{3,2},{4,5},{5,4},{6,7},{7,6},{8,9},{9,8},{10,11... | collective-permute-start | bytes 61448 | tf_op jit(solution)/shard_map/ppermute | solution.py:497
  38.6 13.0 %copy-start.10 = (s32[8]{0:T(128)S(1)}, s32[8]{0:T(128)}, u32[]{:S(2)}) copy-start(s32[8]{0:T(128)} %match_ref.1) | copy-start | bytes 100
  39.4 9.1 %collective-permute-start.15 = (f32[8,256]{1,0:T(8,128)S(1)}, f32[8,256]{1,0:T(8,128)S(1)}, u32[]{:S(2)}, u32[]{:S(2)}) collective-permute-start(f32[8,256]{1,0:T(8,128)S(1)} %get-tuple-element.51), channel_id=1, source_target_pairs={{0,128},{113,129},{2,130},{115,131},{4,132},{117,133},{6,134},{119... | collective-permute-start | bytes 24584 | tf_op jit(solution)/shard_map/ppermute | solution.py:506
  40.7 7.8 %collective-permute-start.16 = (f32[8,256]{1,0:T(8,128)S(1)}, f32[8,256]{1,0:T(8,128)S(1)}, u32[]{:S(2)}, u32[]{:S(2)}) collective-permute-start(f32[8,256]{1,0:T(8,128)S(1)} %get-tuple-element.52), channel_id=1, source_target_pairs={{16,128},{33,129},{18,130},{35,131},{20,132},{37,133},{22,134},{39... | collective-permute-start | bytes 24584 | tf_op jit(solution)/shard_map/ppermute | solution.py:506
  42.0 8.8 %collective-permute-start.17 = (f32[8,256]{1,0:T(8,128)S(1)}, f32[8,256]{1,0:T(8,128)S(1)}, u32[]{:S(2)}, u32[]{:S(2)}) collective-permute-start(f32[8,256]{1,0:T(8,128)S(1)} %get-tuple-element.53), channel_id=1, source_target_pairs={{96,128},{81,129},{98,130},{83,131},{100,132},{85,133},{102,134},{... | collective-permute-start | bytes 24584 | tf_op jit(solution)/shard_map/ppermute | solution.py:506
  43.3 8.2 %collective-permute-start.18 = (f32[8,256]{1,0:T(8,128)S(1)}, f32[8,256]{1,0:T(8,128)S(1)}, u32[]{:S(2)}, u32[]{:S(2)}) collective-permute-start(f32[8,256]{1,0:T(8,128)S(1)} %get-tuple-element.54), channel_id=1, source_target_pairs={{48,128},{65,129},{50,130},{67,131},{52,132},{69,133},{54,134},{71... | collective-permute-start | bytes 24584 | tf_op jit(solution)/shard_map/ppermute | solution.py:506
  44.8 2.2 %copy-start = (bf16[256,8192]{1,0:T(8,128)(2,1)S(1)}, bf16[256,8192]{1,0:T(8,128)(2,1)}, u32[]{:S(2)}) copy-start(bf16[256,8192]{1,0:T(8,128)(2,1)} %w_ref.5) | copy-start | bytes 12582916
  47.0 7.4 %copy-start.1 = (bf16[256,8192]{1,0:T(8,128)(2,1)S(1)}, bf16[256,8192]{1,0:T(8,128)(2,1)}, u32[]{:S(2)}) copy-start(bf16[256,8192]{1,0:T(8,128)(2,1)} %w_ref.5) | copy-start | bytes 12582916
  52.1 2.2 %collective-permute-start.19 = (f32[8,256]{1,0:T(8,128)S(1)}, f32[8,256]{1,0:T(8,128)S(1)}, u32[]{:S(2)}, u32[]{:S(2)}) collective-permute-start(f32[8,256]{1,0:T(8,128)S(1)} %shard_map.88.far_ref), channel_id=1, source_target_pairs={{0,1},{1,0},{2,3},{3,2},{4,5},{5,4},{6,7},{7,6},{8,9},{9,8},{10,11... | collective-permute-start | bytes 24584 | tf_op jit(solution)/shard_map/ppermute | solution.py:514
  56.0 19.4 %copy-start.8 = (bf16[1,1,4,8192]{3,2,1,0:T(4,128)(2,1)S(1)}, bf16[1,1,4,8192]{3,2,1,0:T(4,128)(2,1)}, u32[]{:S(2)}) copy-start(bf16[1,1,4,8192]{3,2,1,0:T(4,128)(2,1)} %param.8) | copy-start | bytes 196612
  56.0 2.0 %collective-permute-start.20 = (bf16[32,8192]{1,0:T(8,128)(2,1)S(1)}, bf16[32,8192]{1,0:T(8,128)(2,1)S(1)}, u32[]{:S(2)}, u32[]{:S(2)}) collective-permute-start(bf16[32,8192]{1,0:T(8,128)(2,1)S(1)} %get-tuple-element.60), channel_id=1, source_target_pairs={{0,1},{1,0},{2,3},{3,2},{4,5},{5,4},{6,7},{7,6},{8,9},{9,8},{10,11... | collective-permute-start | bytes 1572872 | tf_op jit(solution)/shard_map/ppermute | solution.py:517
  58.1 6.1 %collective-permute-start.21 = (bf16[8,8192]{1,0:T(8,128)(2,1)S(1)}, bf16[8,8192]{1,0:T(8,128)(2,1)S(1)}, u32[]{:S(2)}, u32[]{:S(2)}) collective-permute-start(bf16[8,8192]{1,0:T(8,128)(2,1)S(1)} %get-tuple-element.62), channel_id=1, source_target_pairs={{0,4},{1,5},{2,6},{3,7},{4,8},{5,9},{6,10},{7,11},{8,12},{9,13},{1... | collective-permute-start | bytes 393224 | tf_op jit(solution)/shard_map/ppermute | solution.py:520
  59.7 7.9 %collective-permute-start.22 = (bf16[8,8192]{1,0:T(8,128)(2,1)S(1)}, bf16[8,8192]{1,0:T(8,128)(2,1)S(1)}, u32[]{:S(2)}, u32[]{:S(2)}) collective-permute-start(bf16[8,8192]{1,0:T(8,128)(2,1)S(1)} %get-tuple-element.63), channel_id=1, source_target_pairs={{0,8},{1,9},{2,10},{3,11},{4,12},{5,13},{6,14},{7,15},{8,0},{9,1},... | collective-permute-start | bytes 393224 | tf_op jit(solution)/shard_map/ppermute | solution.py:520
  61.5 8.0 %collective-permute-start.23 = (bf16[8,8192]{1,0:T(8,128)(2,1)S(1)}, bf16[8,8192]{1,0:T(8,128)(2,1)S(1)}, u32[]{:S(2)}, u32[]{:S(2)}) collective-permute-start(bf16[8,8192]{1,0:T(8,128)(2,1)S(1)} %get-tuple-element.64), channel_id=1, source_target_pairs={{0,12},{1,13},{2,14},{3,15},{4,0},{5,1},{6,2},{7,3},{8,4},{9,5},{1... | collective-permute-start | bytes 393224 | tf_op jit(solution)/shard_map/ppermute | solution.py:520
  69.5 5.9 %collective-permute-start.24 = (bf16[4,8192]{1,0:T(4,128)(2,1)S(1)}, bf16[4,8192]{1,0:T(4,128)(2,1)S(1)}, u32[]{:S(2)}, u32[]{:S(2)}) collective-permute-start(bf16[4,8192]{1,0:T(4,128)(2,1)S(1)} %get-tuple-element.66), channel_id=1, source_target_pairs={{0,2},{1,3},{2,0},{3,1},{4,6},{5,7},{6,4},{7,5},{8,10},{9,11},{10,... | collective-permute-start | bytes 196616 | tf_op jit(solution)/shard_map/ppermute | solution.py:522

commit v5 on v4

--- a/solution.py
+++ b/solution.py
@@ -11,6 +11,7 @@
 HD = 128
 STEPS = 2
 XN = 4
+X_ORDER = (2, 1, 3)
 NEG = -math.inf
 F32 = jnp.float32
 BF16 = jnp.bfloat16
@@ -27,41 +28,41 @@
     return [(i, (i + 4 * k) % 16) for i in range(16)]
 
 
-DISTANCES = ((0, -1), (1, 2), (-2, -3), (3, 4))
+DISTANCES = ((3, 4), (-2, -3), (1, 2), (0, -1))
 
 
 def after(value, *others):
     return lax.optimization_barrier((value,) + others)[0]
 
 
-def scaled(rows, gain):
+def scaled(rows):
     floated = rows.astype(F32)
     spread = jnp.mean(floated * floated, axis=-1, keepdims=True)
-    return floated * lax.rsqrt(spread + 1e-05) * gain
-
-
-def stage_kernel(own_ref, gain_ref, out_ref, kept_ref):
-    out_ref[...] = scaled(own_ref[...], gain_ref[...])
+    return floated * lax.rsqrt(spread + 1e-05)
+
+
+def stage_kernel(own_ref, out_ref):
+    out_ref[...] = scaled(own_ref[...])
+
+
+def keep_kernel(gain_ref, kept_ref):
     kept_ref[...] = gain_ref[...]
 
 
 def norm_kernel(own_ref, gain_ref, beside_ref, out_ref):
-    beside = scaled(beside_ref[...], gain_ref[...])
-    out_ref[...] = jnp.concatenate([own_ref[...], beside], 0).astype(BF16)
-
-
-def stage(own, gain):
-    return pl.pallas_call(
-        stage_kernel,
-        cost_estimate=COST,
-        compiler_params=LIMIT,
-        out_shape=(
-            jax.ShapeDtypeStruct(own.shape, F32),
-            jax.ShapeDtypeStruct(gain.shape, F32),
-        ),
-        in_specs=[VMEM] * 2,
-        out_specs=(VMEM,) * 2,
-    )(own, gain)
+    both = jnp.concatenate([own_ref[...], scaled(beside_ref[...])], 0)
+    out_ref[...] = (both * gain_ref[...]).astype(BF16)
+
+
+def stage(kernel, value):
+    return pl.pallas_call(
+        kernel,
+        cost_estimate=COST,
+        compiler_params=LIMIT,
+        out_shape=jax.ShapeDtypeStruct(value.shape, F32),
+        in_specs=[VMEM],
+        out_specs=VMEM,
+    )(value)
 
 
 def norm(own, gain, beside):
@@ -362,10 +363,10 @@
 
 
 def add_core_kernel(own_ref, across_ref, *out_refs):
-    total = (own_ref[...].astype(F32) + across_ref[...].astype(F32)).astype(BF16)
+    total = own_ref[...].astype(F32) + across_ref[...].astype(F32)
     width = total.shape[0] // len(out_refs)
     for i, ref in enumerate(out_refs):
-        ref[...] = total[i * width : (i + 1) * width]
+        ref[...] = total[i * width : (i + 1) * width].astype(BF16)
 
 
 def add_core(own, across):
@@ -434,13 +435,15 @@
     kcols = w_keyval.shape[1]
 
     beside = lax.ppermute(own_rows, "tp", YHI)
-    staged = stage(own_rows, norm_gain[None, :])
-    beside = after(beside, staged)
+    staged = stage(stage_kernel, own_rows)
+    gain = stage(keep_kernel, after(norm_gain[None, :], staged))
+    beside = after(beside, staged, gain)
     kv_sent = after(kv_t, staged)
     kv_y = lax.ppermute(kv_sent, "tp", YHI)
     kv_core = lax.ppermute(kv_sent, "tp", CORE)
-    pair = norm(*staged, beside)
-    others = [lax.ppermute(pair, "tp", xshift(-k)) for k in range(1, XN)]
+    pair = norm(staged, gain, beside)
+    others = {k: lax.ppermute(pair, "tp", xshift(-k)) for k in X_ORDER}
+    others = [others[k] for k in range(1, XN)]
     token = touch(pair, w_query, w_keyval.T)
     others = after(others, kv_y, token)
     own_half = jnp.concatenate([pair] + others, 0)
@@ -517,7 +520,8 @@
     across = lax.ppermute(give, "tp", CORE)
     keep = shares(keep, w_out)
     parts = add_core(keep, across)
-    parts = [parts[0]] + [lax.ppermute(parts[k], "tp", xshift(k)) for k in range(1, XN)]
+    sent = {k: lax.ppermute(parts[k], "tp", xshift(k)) for k in X_ORDER}
+    parts = [parts[0]] + [sent[k] for k in X_ORDER]
     summed, send = add_x(parts)
     summed = summed + lax.ppermute(send, "tp", YHI).astype(F32)
     return (own_rows.astype(F32) + summed).astype(BF16)[None, None]

time: 76.5 us -> 75.5 us (0.987)
  the two profiles are of different devices: /device:TPU:10 before, /device:TPU:1 now
where the time goes in v5:
time: 75.5 us; the launch traced here: 75 us
  starting transfers between devices  31 us (41%)
  waiting for transfers between devices  27.1 us (36%)
  local copies, waits for them, and re-layouts  7.37 us (10%)
  Pallas kernels  7.23 us (10%)
  other arithmetic  1.88 us (2%)
    ppermute x4, waiting for transfers between devices, local(): lax.ppermute(leads, axes, carry(d, groups, count, False))  9.63 us
    ppermute x4, starting transfers between devices, local(): lax.ppermute(answer, axes, carry(d, groups, count, True))  7.3 us
    unnamed x24, local copies, waits for them, and re-layouts  7.25 us
    ppermute x3, waiting for transfers between devices, local(): sent = {k: lax.ppermute(parts[k], 'tp', xshift(k)) for k in X_ORDER}  5.72 us
    ppermute x4, starting transfers between devices, local(): lax.ppermute(leads, axes, carry(d, groups, count, False))  5.17 us
    ppermute x3, waiting for transfers between devices, local(): others = {k: lax.ppermute(pair, 'tp', xshift(-k)) for k in X_ORDER}  4.85 us
    ppermute x3, starting transfers between devices, local(): sent = {k: lax.ppermute(parts[k], 'tp', xshift(k)) for k in X_ORDER}  4.11 us
    ppermute x1, waiting for transfers between devices, local(): summed = summed + lax.ppermute(send, 'tp', YHI).astype(F32)  4.01 us
  transfers between devices with their start and end apart: 25, of which 11 were waited for; matrix products, arithmetic and copies ran while one was open for 2% of the time, Pallas kernels for 5%

profile of v5, /device:TPU:1, one launch (start us, length us, event | category | flops | bytes accessed | tf_op | source)
XLA Modules:
  0.0 75.0 jit_solution(2082548511743143069)
XLA Ops:
  0.0 3.7 %collective-permute-start = (bf16[4,8192]{1,0:T(4,128)(2,1)}, bf16[4,8192]{1,0:T(4,128)(2,1)S(1)}, u32[]{:S(2)}, u32[]{:S(2)}) collective-permute-start(bf16[4,8192]{1,0:T(4,128)(2,1)} %bitcast.24), channel_id=1, source_target_pairs={{0,2},{1,3},{2,0},{3,1},{4,6},{5,7},{6,4},{7,5},{8,10},{9,11},{10,... | collective-permute-start | bytes 196616 | tf_op jit(solution)/shard_map/ppermute | solution.py:437
  3.7 0.9 %copy-done.7 = bf16[1,1,4,8192]{3,2,1,0:T(4,128)(2,1)S(1)} copy-done((bf16[1,1,4,8192]{3,2,1,0:T(4,128)(2,1)S(1)}, bf16[1,1,4,8192]{3,2,1,0:T(4,128)(2,1)}, u32[]{:S(2)}) %copy-start.7) | copy-done | bytes 65560
  4.6 0.2 shard_map.82.own_ref
  4.8 0.1 collective-permute-start.4
  4.9 3.0 %collective-permute-start.6 = (bf16[64,4096]{1,0:T(8,128)(2,1)}, bf16[64,4096]{1,0:T(8,128)(2,1)S(1)}, u32[]{:S(2)}, u32[]{:S(2)}) collective-permute-start(bf16[64,4096]{1,0:T(8,128)(2,1)} %bitcast.21), channel_id=1, source_target_pairs={{0,1},{1,0},{2,3},{3,2},{4,5},{5,4},{6,7},{7,6},{8,9},{9,8},{10,11... | collective-permute-start | bytes 1572872 | tf_op jit(solution)/shard_map/ppermute | solution.py:443
  8.0 0.0 copy-start.9
  8.0 0.7 copy-done.9
  8.8 0.0 collective-permute-done.beside_ref
  8.9 0.2 shard_map.84.refs_0_
  9.1 0.8 %collective-permute-start.1 = (bf16[8,8192]{1,0:T(8,128)(2,1)S(1)}, bf16[8,8192]{1,0:T(8,128)(2,1)S(1)}, u32[]{:S(2)}, u32[]{:S(2)}) collective-permute-start(bf16[8,8192]{1,0:T(8,128)(2,1)S(1)} %shard_map.84.refs_0_), channel_id=1, source_target_pairs={{0,12},{1,13},{2,14},{3,15},{4,0},{5,1},{6,2},{7,3},{8,4},{9,5},{1... | collective-permute-start | bytes 393224 | tf_op jit(solution)/shard_map/ppermute | solution.py:445
  9.9 0.5 collective-permute-start.2
  10.4 0.6 collective-permute-start.3
  11.0 2.2 %copy-done.2 = bf16[8192,256]{1,0:T(8,128)(2,1)S(1)} copy-done((bf16[8192,256]{1,0:T(8,128)(2,1)S(1)}, bf16[8192,256]{1,0:T(8,128)(2,1)}, u32[]{:S(2)}) %copy-start.2) | copy-done | bytes 4194328
  13.2 1.2 %copy-done.4 = bf16[8192,64]{0,1:T(8,128)(2,1)S(1)} copy-done((bf16[8192,64]{0,1:T(8,128)(2,1)S(1)}, bf16[8192,64]{0,1:T(8,128)(2,1)}, u32[]{:S(2)}) %copy-start.4) | copy-done | bytes 1048600
  14.4 0.0 copy-start.6
  14.5 0.1 select_reduce_fusion.3
  14.6 0.1 pad_add_fusion.3
  14.6 0.1 select_reduce_fusion.1
  14.8 1.0 %collective-permute-done.2 = bf16[8,8192]{1,0:T(8,128)(2,1)S(1)} collective-permute-done((bf16[8,8192]{1,0:T(8,128)(2,1)S(1)}, bf16[8,8192]{1,0:T(8,128)(2,1)S(1)}, u32[]{:S(2)}, u32[]{:S(2)}) %collective-permute-start.2) | collective-permute-done | bytes 131104 | tf_op jit(solution)/shard_map/ppermute | solution.py:445
  15.8 3.8 %collective-permute-done.3 = bf16[8,8192]{1,0:T(8,128)(2,1)S(1)} collective-permute-done((bf16[8,8192]{1,0:T(8,128)(2,1)S(1)}, bf16[8,8192]{1,0:T(8,128)(2,1)S(1)}, u32[]{:S(2)}, u32[]{:S(2)}) %collective-permute-start.3) | collective-permute-done | bytes 131104 | tf_op jit(solution)/shard_map/ppermute | solution.py:445
  19.7 1.4 %collective-permute-start.5 = (bf16[32,8192]{1,0:T(8,128)(2,1)S(1)}, bf16[32,8192]{1,0:T(8,128)(2,1)S(1)}, u32[]{:S(2)}, u32[]{:S(2)}) collective-permute-start(bf16[32,8192]{1,0:T(8,128)(2,1)S(1)} %pad_maximum_fusion.own_ref), channel_id=1, source_target_pairs={{0,1},{1,0},{2,3},{3,2},{4,5},{5,4},{6,7},{7,6},{8,9},{9,8},{10,11... | collective-permute-start | bytes 1572872 | tf_op jit(solution)/shard_map/ppermute | solution.py:450
  21.1 0.1 select_reduce_fusion
  21.2 0.1 collective-permute-start.8
  21.3 0.2 fusion.4
  21.5 0.3 fusion
  21.8 0.8 %collective-permute-done.5.mate_ref = bf16[32,8192]{1,0:T(8,128)(2,1)S(1)} collective-permute-done((bf16[32,8192]{1,0:T(8,128)(2,1)S(1)}, bf16[32,8192]{1,0:T(8,128)(2,1)S(1)}, u32[]{:S(2)}, u32[]{:S(2)}) %collective-permute-start.5) | collective-permute-done | bytes 524320 | tf_op jit(solution)/shard_map/ppermute | solution.py:450
  22.6 1.4 %shard_map.86 = (bf16[64,256]{1,0:T(8,128)(2,1)S(1)}, bf16[80,128]{1,0:T(8,128)(2,1)S(1)}) custom-call(bf16[32,8192]{1,0:T(8,128)(2,1)S(1)} %pad_maximum_fusion.own_ref, bf16[32,8192]{1,0:T(8,128)(2,1)S(1)} %collective-permute-done.5.mate_ref, bf16[8192,256]{1,0:T(8,128)(2,1)S(1)} %copy-done.3, bf16[64,8192]{1,0:T(8,128)(2,1)S(1)} %bitcast.19, ...), custom_call_target="tpu_custom_call" | custom-call | flops 1 | bytes 1 | tf_op jit(solution)/shard_map/pallas_call | solution.py:131
  24.0 0.5 collective-permute-start.7
  24.4 0.1 pad_add_fusion.2.flags_ref
  24.5 2.1 %collective-permute-start.13 = (bf16[80,128]{1,0:T(8,128)(2,1)S(1)}, bf16[80,128]{1,0:T(8,128)(2,1)S(1)}, u32[]{:S(2)}, u32[]{:S(2)}) collective-permute-start(bf16[80,128]{1,0:T(8,128)(2,1)S(1)} %get-tuple-element.44.refs_4_), channel_id=1, source_target_pairs={{0,2},{1,3},{2,0},{3,1},{4,6},{5,7},{6,4},{7,5},{8,10},{9,11},{10,... | collective-permute-start | bytes 61448 | tf_op jit(solution)/shard_map/ppermute | solution.py:498
  26.7 1.3 %collective-permute-start.9 = (bf16[32,128]{1,0:T(8,128)(2,1)S(1)}, bf16[32,128]{1,0:T(8,128)(2,1)S(1)}, u32[]{:S(2)}, u32[]{:S(2)}) collective-permute-start(bf16[32,128]{1,0:T(8,128)(2,1)S(1)} %pad_maximum_fusion.1), channel_id=1, source_target_pairs={{128,48},{129,65},{130,50},{131,67},{132,52},{133,69},{134,54},{13... | collective-permute-start | bytes 24584 | tf_op jit(solution)/shard_map/ppermute | solution.py:503
  28.0 1.3 %collective-permute-start.10 = (bf16[32,128]{1,0:T(8,128)(2,1)S(1)}, bf16[32,128]{1,0:T(8,128)(2,1)S(1)}, u32[]{:S(2)}, u32[]{:S(2)}) collective-permute-start(bf16[32,128]{1,0:T(8,128)(2,1)S(1)} %pad_maximum_fusion.1), channel_id=1, source_target_pairs={{128,96},{129,81},{130,98},{131,83},{132,100},{133,85},{134,102},{... | collective-permute-start | bytes 24584 | tf_op jit(solution)/shard_map/ppermute | solution.py:503
  29.3 1.3 %collective-permute-start.11 = (bf16[32,128]{1,0:T(8,128)(2,1)S(1)}, bf16[32,128]{1,0:T(8,128)(2,1)S(1)}, u32[]{:S(2)}, u32[]{:S(2)}) collective-permute-start(bf16[32,128]{1,0:T(8,128)(2,1)S(1)} %pad_maximum_fusion.1), channel_id=1, source_target_pairs={{128,16},{129,33},{130,18},{131,35},{132,20},{133,37},{134,22},{13... | collective-permute-start | bytes 24584 | tf_op jit(solution)/shard_map/ppermute | solution.py:503
  30.6 1.3 %collective-permute-start.12 = (bf16[32,128]{1,0:T(8,128)(2,1)S(1)}, bf16[32,128]{1,0:T(8,128)(2,1)S(1)}, u32[]{:S(2)}, u32[]{:S(2)}) collective-permute-start(bf16[32,128]{1,0:T(8,128)(2,1)S(1)} %pad_maximum_fusion.1), channel_id=1, source_target_pairs={{128,0},{129,113},{130,2},{131,115},{132,4},{133,117},{134,6},{135... | collective-permute-start | bytes 24584 | tf_op jit(solution)/shard_map/ppermute | solution.py:503
  31.9 0.5 collective-permute-start.14
  32.4 3.6 %collective-permute-done.9.refs_8_ = bf16[32,128]{1,0:T(8,128)(2,1)S(1)} collective-permute-done((bf16[32,128]{1,0:T(8,128)(2,1)S(1)}, bf16[32,128]{1,0:T(8,128)(2,1)S(1)}, u32[]{:S(2)}, u32[]{:S(2)}) %collective-permute-start.9) | collective-permute-done | bytes 8224 | tf_op jit(solution)/shard_map/ppermute | solution.py:503
  36.0 4.4 %collective-permute-done.10.refs_9_ = bf16[32,128]{1,0:T(8,128)(2,1)S(1)} collective-permute-done((bf16[32,128]{1,0:T(8,128)(2,1)S(1)}, bf16[32,128]{1,0:T(8,128)(2,1)S(1)}, u32[]{:S(2)}, u32[]{:S(2)}) %collective-permute-start.10) | collective-permute-done | bytes 8224 | tf_op jit(solution)/shard_map/ppermute | solution.py:503
  40.4 1.6 %collective-permute-done.12.refs_11_ = bf16[32,128]{1,0:T(8,128)(2,1)S(1)} collective-permute-done((bf16[32,128]{1,0:T(8,128)(2,1)S(1)}, bf16[32,128]{1,0:T(8,128)(2,1)S(1)}, u32[]{:S(2)}, u32[]{:S(2)}) %collective-permute-start.12) | collective-permute-done | bytes 8224 | tf_op jit(solution)/shard_map/ppermute | solution.py:503
  42.0 0.8 %shard_map.88 = (f32[8,256]{1,0:T(8,128)S(1)}, f32[8,256]{1,0:T(8,128)S(1)}, f32[8,256]{1,0:T(8,128)S(1)}, f32[8,256]{1,0:T(8,128)S(1)}) custom-call(s32[1]{0:T(128)} %bitcast.4.me_ref, bf16[64,4096]{1,0:T(8,128)(2,1)S(1)} %bitcast.22, bf16[64,4096]{1,0:T(8,128)(2,1)S(1)} %collective-permute-done.6.refs_1_, ...), custom_call_target="tpu_custom_call" | custom-call | flops 1 | bytes 1 | tf_op jit(solution)/shard_map/pallas_call | solution.py:269
  42.9 3.4 %collective-permute-start.15 = (f32[8,256]{1,0:T(8,128)S(1)}, f32[8,256]{1,0:T(8,128)S(1)}, u32[]{:S(2)}, u32[]{:S(2)}) collective-permute-start(f32[8,256]{1,0:T(8,128)S(1)} %get-tuple-element.49), channel_id=1, source_target_pairs={{48,128},{65,129},{50,130},{67,131},{52,132},{69,133},{54,134},{71... | collective-permute-start | bytes 24584 | tf_op jit(solution)/shard_map/ppermute | solution.py:509
  46.3 1.3 %collective-permute-start.16 = (f32[8,256]{1,0:T(8,128)S(1)}, f32[8,256]{1,0:T(8,128)S(1)}, u32[]{:S(2)}, u32[]{:S(2)}) collective-permute-start(f32[8,256]{1,0:T(8,128)S(1)} %get-tuple-element.50), channel_id=1, source_target_pairs={{96,128},{81,129},{98,130},{83,131},{100,132},{85,133},{102,134},{... | collective-permute-start | bytes 24584 | tf_op jit(solution)/shard_map/ppermute | solution.py:509
  47.6 1.3 %collective-permute-start.17 = (f32[8,256]{1,0:T(8,128)S(1)}, f32[8,256]{1,0:T(8,128)S(1)}, u32[]{:S(2)}, u32[]{:S(2)}) collective-permute-start(f32[8,256]{1,0:T(8,128)S(1)} %get-tuple-element.51), channel_id=1, source_target_pairs={{16,128},{33,129},{18,130},{35,131},{20,132},{37,133},{22,134},{39... | collective-permute-start | bytes 24584 | tf_op jit(solution)/shard_map/ppermute | solution.py:509
  48.9 1.3 %collective-permute-start.18 = (f32[8,256]{1,0:T(8,128)S(1)}, f32[8,256]{1,0:T(8,128)S(1)}, u32[]{:S(2)}, u32[]{:S(2)}) collective-permute-start(f32[8,256]{1,0:T(8,128)S(1)} %get-tuple-element.52), channel_id=1, source_target_pairs={{0,128},{113,129},{2,130},{115,131},{4,132},{117,133},{6,134},{119... | collective-permute-start | bytes 24584 | tf_op jit(solution)/shard_map/ppermute | solution.py:509
  50.2 0.1 add_add_fusion
  50.3 0.1 copy.12.bounds_ref
  50.4 2.2 %copy-done = bf16[256,8192]{1,0:T(8,128)(2,1)S(1)} copy-done((bf16[256,8192]{1,0:T(8,128)(2,1)S(1)}, bf16[256,8192]{1,0:T(8,128)(2,1)}, u32[]{:S(2)}) %copy-start) | copy-done | bytes 4194328
  52.6 1.5 %shard_map.87 = (bf16[64,256]{1,0:T(8,128)(2,1)S(1)}, f32[8,256]{1,0:T(8,128)S(1)}) custom-call(s32[1]{0:T(128)} %bitcast.4.me_ref, bf16[64,256]{1,0:T(8,128)(2,1)S(1)} %get-tuple-element.46.q_ref, s32[128,4]{1,0:T(8,128)S(1)} %copy.12.bounds_ref, bf16[256,8192]{1,0:T(8,128)(2,1)S(1)} %copy-done, bf16[64,4096]{1,0:T(8,128)(2,1)S(1)} %bitcast.23, ...), custom_call_target="tpu_custom_call" | custom-call | flops 1 | bytes 1 | tf_op jit(solution)/shard_map/pallas_call | solution.py:254
  54.1 0.6 shard_map.89.far_ref
  54.7 0.1 collective-permute-start.19
  54.8 1.2 %collective-permute-done.19.mate_ref = f32[8,256]{1,0:T(8,128)S(1)} collective-permute-done((f32[8,256]{1,0:T(8,128)S(1)}, f32[8,256]{1,0:T(8,128)S(1)}, u32[]{:S(2)}, u32[]{:S(2)}) %collective-permute-start.19) | collective-permute-done | bytes 8224 | tf_op jit(solution)/shard_map/ppermute | solution.py:517
  56.0 1.6 %shard_map.90 = (bf16[32,256]{1,0:T(8,128)(2,1)S(1)}, bf16[32,8192]{1,0:T(8,128)(2,1)S(1)}) custom-call(s32[3]{0:T(128)S(1)} %pad_add_fusion.2.flags_ref, bf16[64,256]{1,0:T(8,128)(2,1)S(1)} %get-tuple-element.47.attended_ref, f32[8,256]{1,0:T(8,128)S(1)} %get-tuple-element.48.own_ref, f32[8,256]{1,0:T(8,128)S(1)} %shard_map.89.far_ref, ...), custom_call_target="tpu_custom_call" | custom-call | flops 1 | bytes 1 | tf_op jit(solution)/shard_map/pallas_call | solution.py:355
  57.6 0.3 collective-permute-start.20
  57.9 0.8 %shard_map.91.own_ref = bf16[32,8192]{1,0:T(8,128)(2,1)S(1)} custom-call(bf16[32,256]{1,0:T(8,128)(2,1)S(1)} %get-tuple-element.57.attended_ref, bf16[256,8192]{1,0:T(8,128)(2,1)S(1)} %copy-done.1), custom_call_target="tpu_custom_call" | custom-call | flops 1 | bytes 1 | tf_op jit(solution)/shard_map/pallas_call | solution.py:343
  58.7 0.9 %collective-permute-done.20.across_ref = bf16[32,8192]{1,0:T(8,128)(2,1)S(1)} collective-permute-done((bf16[32,8192]{1,0:T(8,128)(2,1)S(1)}, bf16[32,8192]{1,0:T(8,128)(2,1)S(1)}, u32[]{:S(2)}, u32[]{:S(2)}) %collective-permute-start.20) | collective-permute-done | bytes 524320 | tf_op jit(solution)/shard_map/ppermute | solution.py:520
  59.6 0.1 shard_map.92
  59.7 1.4 %collective-permute-start.21 = (bf16[8,8192]{1,0:T(8,128)(2,1)S(1)}, bf16[8,8192]{1,0:T(8,128)(2,1)S(1)}, u32[]{:S(2)}, u32[]{:S(2)}) collective-permute-start(bf16[8,8192]{1,0:T(8,128)(2,1)S(1)} %get-tuple-element.60), channel_id=1, source_target_pairs={{0,8},{1,9},{2,10},{3,11},{4,12},{5,13},{6,14},{7,15},{8,0},{9,1},... | collective-permute-start | bytes 393224 | tf_op jit(solution)/shard_map/ppermute | solution.py:523
  61.2 0.3 collective-permute-start.22
  61.5 2.4 %collective-permute-start.23 = (bf16[8,8192]{1,0:T(8,128)(2,1)S(1)}, bf16[8,8192]{1,0:T(8,128)(2,1)S(1)}, u32[]{:S(2)}, u32[]{:S(2)}) collective-permute-start(bf16[8,8192]{1,0:T(8,128)(2,1)S(1)} %get-tuple-element.62), channel_id=1, source_target_pairs={{0,12},{1,13},{2,14},{3,15},{4,0},{5,1},{6,2},{7,3},{8,4},{9,5},{1... | collective-permute-start | bytes 393224 | tf_op jit(solution)/shard_map/ppermute | solution.py:523
  63.8 2.4 %collective-permute-done.21.b_ref = bf16[8,8192]{1,0:T(8,128)(2,1)S(1)} collective-permute-done((bf16[8,8192]{1,0:T(8,128)(2,1)S(1)}, bf16[8,8192]{1,0:T(8,128)(2,1)S(1)}, u32[]{:S(2)}, u32[]{:S(2)}) %collective-permute-start.21) | collective-permute-done | bytes 131104 | tf_op jit(solution)/shard_map/ppermute | solution.py:523
  66.3 3.3 %collective-permute-done.22.c_ref = bf16[8,8192]{1,0:T(8,128)(2,1)S(1)} collective-permute-done((bf16[8,8192]{1,0:T(8,128)(2,1)S(1)}, bf16[8,8192]{1,0:T(8,128)(2,1)S(1)}, u32[]{:S(2)}, u32[]{:S(2)}) %collective-permute-start.22) | collective-permute-done | bytes 131104 | tf_op jit(solution)/shard_map/ppermute | solution.py:523
  69.6 0.1 shard_map.93
  69.6 0.7 collective-permute-start.24
  70.3 4.0 %collective-permute-done.24 = bf16[4,8192]{1,0:T(4,128)(2,1)S(1)} collective-permute-done((bf16[4,8192]{1,0:T(4,128)(2,1)S(1)}, bf16[4,8192]{1,0:T(4,128)(2,1)S(1)}, u32[]{:S(2)}, u32[]{:S(2)}) %collective-permute-start.24) | collective-permute-done | bytes 65568 | tf_op jit(solution)/shard_map/ppermute | solution.py:526
  74.4 0.7 fusion.1
  (47 shorter events, 0.2 us)
Async XLA Ops:
  0.0 14.4 %copy-start.11 = (s32[1,31]{1,0:T(1,128)S(1)}, s32[1,31]{1,0:T(1,128)}, u32[]{:S(2)}) copy-start(s32[1,31]{1,0:T(1,128)} %param.15) | copy-start | bytes 376
  0.0 8.8 %collective-permute-start = (bf16[4,8192]{1,0:T(4,128)(2,1)}, bf16[4,8192]{1,0:T(4,128)(2,1)S(1)}, u32[]{:S(2)}, u32[]{:S(2)}) collective-permute-start(bf16[4,8192]{1,0:T(4,128)(2,1)} %bitcast.24), channel_id=1, source_target_pairs={{0,2},{1,3},{2,0},{3,1},{4,6},{5,7},{6,4},{7,5},{8,10},{9,11},{10,... | collective-permute-start | bytes 196616 | tf_op jit(solution)/shard_map/ppermute | solution.py:437
  3.7 0.9 %copy-start.7 = (bf16[1,1,4,8192]{3,2,1,0:T(4,128)(2,1)S(1)}, bf16[1,1,4,8192]{3,2,1,0:T(4,128)(2,1)}, u32[]{:S(2)}) copy-start(bf16[1,1,4,8192]{3,2,1,0:T(4,128)(2,1)} %param.8) | copy-start | bytes 196612
  4.8 14.8 %collective-permute-start.4 = (bf16[64,4096]{1,0:T(8,128)(2,1)}, bf16[64,4096]{1,0:T(8,128)(2,1)S(1)}, u32[]{:S(2)}, u32[]{:S(2)}) collective-permute-start(bf16[64,4096]{1,0:T(8,128)(2,1)} %bitcast.20), channel_id=1, source_target_pairs={{0,2},{1,3},{2,0},{3,1},{4,6},{5,7},{6,4},{7,5},{8,10},{9,11},{10,... | collective-permute-start | bytes 1572872 | tf_op jit(solution)/shard_map/ppermute | solution.py:442
  4.9 16.9 %collective-permute-start.6 = (bf16[64,4096]{1,0:T(8,128)(2,1)}, bf16[64,4096]{1,0:T(8,128)(2,1)S(1)}, u32[]{:S(2)}, u32[]{:S(2)}) collective-permute-start(bf16[64,4096]{1,0:T(8,128)(2,1)} %bitcast.21), channel_id=1, source_target_pairs={{0,1},{1,0},{2,3},{3,2},{4,5},{5,4},{6,7},{7,6},{8,9},{9,8},{10,11... | collective-permute-start | bytes 1572872 | tf_op jit(solution)/shard_map/ppermute | solution.py:443
  8.0 0.8 %copy-start.9 = (f32[8192]{0:T(1024)S(1)}, f32[8192]{0:T(1024)}, u32[]{:S(2)}) copy-start(f32[8192]{0:T(1024)} %param.9) | copy-start | bytes 98308
  9.1 5.7 %collective-permute-start.1 = (bf16[8,8192]{1,0:T(8,128)(2,1)S(1)}, bf16[8,8192]{1,0:T(8,128)(2,1)S(1)}, u32[]{:S(2)}, u32[]{:S(2)}) collective-permute-start(bf16[8,8192]{1,0:T(8,128)(2,1)S(1)} %shard_map.84.refs_0_), channel_id=1, source_target_pairs={{0,12},{1,13},{2,14},{3,15},{4,0},{5,1},{6,2},{7,3},{8,4},{9,5},{1... | collective-permute-start | bytes 393224 | tf_op jit(solution)/shard_map/ppermute | solution.py:445
  9.9 5.9 %collective-permute-start.2 = (bf16[8,8192]{1,0:T(8,128)(2,1)S(1)}, bf16[8,8192]{1,0:T(8,128)(2,1)S(1)}, u32[]{:S(2)}, u32[]{:S(2)}) collective-permute-start(bf16[8,8192]{1,0:T(8,128)(2,1)S(1)} %shard_map.84.refs_0_), channel_id=1, source_target_pairs={{0,8},{1,9},{2,10},{3,11},{4,12},{5,13},{6,14},{7,15},{8,0},{9,1},... | collective-permute-start | bytes 393224 | tf_op jit(solution)/shard_map/ppermute | solution.py:445
  10.4 9.2 %collective-permute-start.3 = (bf16[8,8192]{1,0:T(8,128)(2,1)S(1)}, bf16[8,8192]{1,0:T(8,128)(2,1)S(1)}, u32[]{:S(2)}, u32[]{:S(2)}) collective-permute-start(bf16[8,8192]{1,0:T(8,128)(2,1)S(1)} %shard_map.84.refs_0_), channel_id=1, source_target_pairs={{0,4},{1,5},{2,6},{3,7},{4,8},{5,9},{6,10},{7,11},{8,12},{9,13},{1... | collective-permute-start | bytes 393224 | tf_op jit(solution)/shard_map/ppermute | solution.py:445
  11.0 2.2 %copy-start.2 = (bf16[8192,256]{1,0:T(8,128)(2,1)S(1)}, bf16[8192,256]{1,0:T(8,128)(2,1)}, u32[]{:S(2)}) copy-start(bf16[8192,256]{1,0:T(8,128)(2,1)} %wq_ref.1) | copy-start | bytes 12582916
  13.2 1.2 %copy-start.4 = (bf16[8192,64]{0,1:T(8,128)(2,1)S(1)}, bf16[8192,64]{0,1:T(8,128)(2,1)}, u32[]{:S(2)}) copy-start(bf16[8192,64]{0,1:T(8,128)(2,1)} %param.11) | copy-start | bytes 3145732
  14.4 8.2 %copy-start.3 = (bf16[8192,256]{1,0:T(8,128)(2,1)S(1)}, bf16[8192,256]{1,0:T(8,128)(2,1)}, u32[]{:S(2)}) copy-start(bf16[8192,256]{1,0:T(8,128)(2,1)} %wq_ref.1) | copy-start | bytes 12582916
  14.4 8.2 %copy-start.5 = (bf16[8192,64]{0,1:T(8,128)(2,1)S(1)}, bf16[8192,64]{0,1:T(8,128)(2,1)}, u32[]{:S(2)}) copy-start(bf16[8192,64]{0,1:T(8,128)(2,1)} %param.11) | copy-start | bytes 3145732
  14.4 27.6 %copy-start.6 = (bf16[1,1,4096,64]{2,3,1,0:T(8,128)(2,1)S(1)}, bf16[1,1,4096,64]{2,3,1,0:T(8,128)(2,1)}, u32[]{:S(2)}) copy-start(bf16[1,1,4096,64]{2,3,1,0:T(8,128)(2,1)} %param.13) | copy-start | bytes 1572868
  19.7 2.9 %collective-permute-start.5 = (bf16[32,8192]{1,0:T(8,128)(2,1)S(1)}, bf16[32,8192]{1,0:T(8,128)(2,1)S(1)}, u32[]{:S(2)}, u32[]{:S(2)}) collective-permute-start(bf16[32,8192]{1,0:T(8,128)(2,1)S(1)} %pad_maximum_fusion.own_ref), channel_id=1, source_target_pairs={{0,1},{1,0},{2,3},{3,2},{4,5},{5,4},{6,7},{7,6},{8,9},{9,8},{10,11... | collective-permute-start | bytes 1572872 | tf_op jit(solution)/shard_map/ppermute | solution.py:450
  21.2 5.5 %collective-permute-start.8 = (bf16[64,4096]{1,0:T(8,128)(2,1)S(1)}, bf16[64,4096]{1,0:T(8,128)(2,1)S(1)}, u32[]{:S(2)}, u32[]{:S(2)}) collective-permute-start(bf16[64,4096]{1,0:T(8,128)(2,1)S(1)} %collective-permute-done.4.refs_2_), channel_id=1, source_target_pairs={{0,1},{1,0},{2,3},{3,2},{4,5},{5,4},{6,7},{7,6},{8,9},{9,8},{10,11... | collective-permute-start | bytes 1572872 | tf_op jit(solution)/shard_map/ppermute | solution.py:451
  24.0 2.7 %collective-permute-start.7 = (bf16[80,128]{1,0:T(8,128)(2,1)S(1)}, bf16[80,128]{1,0:T(8,128)(2,1)S(1)}, u32[]{:S(2)}, u32[]{:S(2)}) collective-permute-start(bf16[80,128]{1,0:T(8,128)(2,1)S(1)} %get-tuple-element.44.refs_4_), channel_id=1, source_target_pairs={{0,1},{1,0},{2,3},{3,2},{4,5},{5,4},{6,7},{7,6},{8,9},{9,8},{10,11... | collective-permute-start | bytes 61448 | tf_op jit(solution)/shard_map/ppermute | solution.py:499
  24.5 7.4 %collective-permute-start.13 = (bf16[80,128]{1,0:T(8,128)(2,1)S(1)}, bf16[80,128]{1,0:T(8,128)(2,1)S(1)}, u32[]{:S(2)}, u32[]{:S(2)}) collective-permute-start(bf16[80,128]{1,0:T(8,128)(2,1)S(1)} %get-tuple-element.44.refs_4_), channel_id=1, source_target_pairs={{0,2},{1,3},{2,0},{3,1},{4,6},{5,7},{6,4},{7,5},{8,10},{9,11},{10,... | collective-permute-start | bytes 61448 | tf_op jit(solution)/shard_map/ppermute | solution.py:498
  26.7 9.3 %collective-permute-start.9 = (bf16[32,128]{1,0:T(8,128)(2,1)S(1)}, bf16[32,128]{1,0:T(8,128)(2,1)S(1)}, u32[]{:S(2)}, u32[]{:S(2)}) collective-permute-start(bf16[32,128]{1,0:T(8,128)(2,1)S(1)} %pad_maximum_fusion.1), channel_id=1, source_target_pairs={{128,48},{129,65},{130,50},{131,67},{132,52},{133,69},{134,54},{13... | collective-permute-start | bytes 24584 | tf_op jit(solution)/shard_map/ppermute | solution.py:503
  28.0 12.5 %collective-permute-start.10 = (bf16[32,128]{1,0:T(8,128)(2,1)S(1)}, bf16[32,128]{1,0:T(8,128)(2,1)S(1)}, u32[]{:S(2)}, u32[]{:S(2)}) collective-permute-start(bf16[32,128]{1,0:T(8,128)(2,1)S(1)} %pad_maximum_fusion.1), channel_id=1, source_target_pairs={{128,96},{129,81},{130,98},{131,83},{132,100},{133,85},{134,102},{... | collective-permute-start | bytes 24584 | tf_op jit(solution)/shard_map/ppermute | solution.py:503
  29.3 11.2 %collective-permute-start.11 = (bf16[32,128]{1,0:T(8,128)(2,1)S(1)}, bf16[32,128]{1,0:T(8,128)(2,1)S(1)}, u32[]{:S(2)}, u32[]{:S(2)}) collective-permute-start(bf16[32,128]{1,0:T(8,128)(2,1)S(1)} %pad_maximum_fusion.1), channel_id=1, source_target_pairs={{128,16},{129,33},{130,18},{131,35},{132,20},{133,37},{134,22},{13... | collective-permute-start | bytes 24584 | tf_op jit(solution)/shard_map/ppermute | solution.py:503
  30.6 11.5 %collective-permute-start.12 = (bf16[32,128]{1,0:T(8,128)(2,1)S(1)}, bf16[32,128]{1,0:T(8,128)(2,1)S(1)}, u32[]{:S(2)}, u32[]{:S(2)}) collective-permute-start(bf16[32,128]{1,0:T(8,128)(2,1)S(1)} %pad_maximum_fusion.1), channel_id=1, source_target_pairs={{128,0},{129,113},{130,2},{131,115},{132,4},{133,117},{134,6},{135... | collective-permute-start | bytes 24584 | tf_op jit(solution)/shard_map/ppermute | solution.py:503
  31.9 10.2 %collective-permute-start.14 = (bf16[80,128]{1,0:T(8,128)(2,1)S(1)}, bf16[80,128]{1,0:T(8,128)(2,1)S(1)}, u32[]{:S(2)}, u32[]{:S(2)}) collective-permute-start(bf16[80,128]{1,0:T(8,128)(2,1)S(1)} %collective-permute-done.13.refs_6_), channel_id=1, source_target_pairs={{0,1},{1,0},{2,3},{3,2},{4,5},{5,4},{6,7},{7,6},{8,9},{9,8},{10,11... | collective-permute-start | bytes 61448 | tf_op jit(solution)/shard_map/ppermute | solution.py:500
  42.0 12.1 %copy-start.10 = (s32[8]{0:T(128)S(1)}, s32[8]{0:T(128)}, u32[]{:S(2)}) copy-start(s32[8]{0:T(128)} %match_ref.1) | copy-start | bytes 100
  42.9 11.2 %collective-permute-start.15 = (f32[8,256]{1,0:T(8,128)S(1)}, f32[8,256]{1,0:T(8,128)S(1)}, u32[]{:S(2)}, u32[]{:S(2)}) collective-permute-start(f32[8,256]{1,0:T(8,128)S(1)} %get-tuple-element.49), channel_id=1, source_target_pairs={{48,128},{65,129},{50,130},{67,131},{52,132},{69,133},{54,134},{71... | collective-permute-start | bytes 24584 | tf_op jit(solution)/shard_map/ppermute | solution.py:509
  46.3 7.8 %collective-permute-start.16 = (f32[8,256]{1,0:T(8,128)S(1)}, f32[8,256]{1,0:T(8,128)S(1)}, u32[]{:S(2)}, u32[]{:S(2)}) collective-permute-start(f32[8,256]{1,0:T(8,128)S(1)} %get-tuple-element.50), channel_id=1, source_target_pairs={{96,128},{81,129},{98,130},{83,131},{100,132},{85,133},{102,134},{... | collective-permute-start | bytes 24584 | tf_op jit(solution)/shard_map/ppermute | solution.py:509
  47.6 6.5 %collective-permute-start.17 = (f32[8,256]{1,0:T(8,128)S(1)}, f32[8,256]{1,0:T(8,128)S(1)}, u32[]{:S(2)}, u32[]{:S(2)}) collective-permute-start(f32[8,256]{1,0:T(8,128)S(1)} %get-tuple-element.51), channel_id=1, source_target_pairs={{16,128},{33,129},{18,130},{35,131},{20,132},{37,133},{22,134},{39... | collective-permute-start | bytes 24584 | tf_op jit(solution)/shard_map/ppermute | solution.py:509
  48.9 5.2 %collective-permute-start.18 = (f32[8,256]{1,0:T(8,128)S(1)}, f32[8,256]{1,0:T(8,128)S(1)}, u32[]{:S(2)}, u32[]{:S(2)}) collective-permute-start(f32[8,256]{1,0:T(8,128)S(1)} %get-tuple-element.52), channel_id=1, source_target_pairs={{0,128},{113,129},{2,130},{115,131},{4,132},{117,133},{6,134},{119... | collective-permute-start | bytes 24584 | tf_op jit(solution)/shard_map/ppermute | solution.py:509
  50.4 2.2 %copy-start = (bf16[256,8192]{1,0:T(8,128)(2,1)S(1)}, bf16[256,8192]{1,0:T(8,128)(2,1)}, u32[]{:S(2)}) copy-start(bf16[256,8192]{1,0:T(8,128)(2,1)} %w_ref.5) | copy-start | bytes 12582916
  52.6 3.4 %copy-start.1 = (bf16[256,8192]{1,0:T(8,128)(2,1)S(1)}, bf16[256,8192]{1,0:T(8,128)(2,1)}, u32[]{:S(2)}) copy-start(bf16[256,8192]{1,0:T(8,128)(2,1)} %w_ref.5) | copy-start | bytes 12582916
  54.7 1.3 %collective-permute-start.19 = (f32[8,256]{1,0:T(8,128)S(1)}, f32[8,256]{1,0:T(8,128)S(1)}, u32[]{:S(2)}, u32[]{:S(2)}) collective-permute-start(f32[8,256]{1,0:T(8,128)S(1)} %shard_map.89.far_ref), channel_id=1, source_target_pairs={{0,1},{1,0},{2,3},{3,2},{4,5},{5,4},{6,7},{7,6},{8,9},{9,8},{10,11... | collective-permute-start | bytes 24584 | tf_op jit(solution)/shard_map/ppermute | solution.py:517
  57.6 16.8 %copy-start.8 = (bf16[1,1,4,8192]{3,2,1,0:T(4,128)(2,1)S(1)}, bf16[1,1,4,8192]{3,2,1,0:T(4,128)(2,1)}, u32[]{:S(2)}) copy-start(bf16[1,1,4,8192]{3,2,1,0:T(4,128)(2,1)} %param.8) | copy-start | bytes 196612
  57.6 2.0 %collective-permute-start.20 = (bf16[32,8192]{1,0:T(8,128)(2,1)S(1)}, bf16[32,8192]{1,0:T(8,128)(2,1)S(1)}, u32[]{:S(2)}, u32[]{:S(2)}) collective-permute-start(bf16[32,8192]{1,0:T(8,128)(2,1)S(1)} %get-tuple-element.58), channel_id=1, source_target_pairs={{0,1},{1,0},{2,3},{3,2},{4,5},{5,4},{6,7},{7,6},{8,9},{9,8},{10,11... | collective-permute-start | bytes 1572872 | tf_op jit(solution)/shard_map/ppermute | solution.py:520
  59.7 6.5 %collective-permute-start.21 = (bf16[8,8192]{1,0:T(8,128)(2,1)S(1)}, bf16[8,8192]{1,0:T(8,128)(2,1)S(1)}, u32[]{:S(2)}, u32[]{:S(2)}) collective-permute-start(bf16[8,8192]{1,0:T(8,128)(2,1)S(1)} %get-tuple-element.60), channel_id=1, source_target_pairs={{0,8},{1,9},{2,10},{3,11},{4,12},{5,13},{6,14},{7,15},{8,0},{9,1},... | collective-permute-start | bytes 393224 | tf_op jit(solution)/shard_map/ppermute | solution.py:523
  61.2 8.4 %collective-permute-start.22 = (bf16[8,8192]{1,0:T(8,128)(2,1)S(1)}, bf16[8,8192]{1,0:T(8,128)(2,1)S(1)}, u32[]{:S(2)}, u32[]{:S(2)}) collective-permute-start(bf16[8,8192]{1,0:T(8,128)(2,1)S(1)} %get-tuple-element.61), channel_id=1, source_target_pairs={{0,4},{1,5},{2,6},{3,7},{4,8},{5,9},{6,10},{7,11},{8,12},{9,13},{1... | collective-permute-start | bytes 393224 | tf_op jit(solution)/shard_map/ppermute | solution.py:523
  61.5 8.1 %collective-permute-start.23 = (bf16[8,8192]{1,0:T(8,128)(2,1)S(1)}, bf16[8,8192]{1,0:T(8,128)(2,1)S(1)}, u32[]{:S(2)}, u32[]{:S(2)}) collective-permute-start(bf16[8,8192]{1,0:T(8,128)(2,1)S(1)} %get-tuple-element.62), channel_id=1, source_target_pairs={{0,12},{1,13},{2,14},{3,15},{4,0},{5,1},{6,2},{7,3},{8,4},{9,5},{1... | collective-permute-start | bytes 393224 | tf_op jit(solution)/shard_map/ppermute | solution.py:523
  69.6 4.7 %collective-permute-start.24 = (bf16[4,8192]{1,0:T(4,128)(2,1)S(1)}, bf16[4,8192]{1,0:T(4,128)(2,1)S(1)}, u32[]{:S(2)}, u32[]{:S(2)}) collective-permute-start(bf16[4,8192]{1,0:T(4,128)(2,1)S(1)} %get-tuple-element.64), channel_id=1, source_target_pairs={{0,2},{1,3},{2,0},{3,1},{4,6},{5,7},{6,4},{7,5},{8,10},{9,11},{10,... | collective-permute-start | bytes 196616 | tf_op jit(solution)/shard_map/ppermute | solution.py:526

commit v6 on v5

--- a/solution.py
+++ b/solution.py
@@ -191,16 +191,17 @@
     return [held[place ^ part] for part in range(4)]
 
 
-def each_place(me_ref, body):
+def each_place(body):
+    here = lax.rem(lax.axis_index("tp"), 4)
     for place in range(4):
-        pl.when(me_ref[0] == place)(functools.partial(body, place))
+        pl.when(here == place)(functools.partial(body, place))
 
 
 def held_fresh(pack_refs, size):
     return [ref[:size, :size] for ref in pack_refs]
 
 
-def main_kernel(me_ref, q_ref, bounds_ref, w_ref, *refs):
+def main_kernel(q_ref, bounds_ref, w_ref, *refs):
     del w_ref
     kv_refs, pack_refs = refs[:4], refs[4:8]
     out_ref, lead_ref, scores = refs[8:]
@@ -221,10 +222,10 @@
         packed = pack_parts(mixed, peak, total)
         lead_ref[...] = lead_rows(packed[:8], packed[rows : rows + 8])
 
-    each_place(me_ref, body)
-
-
-def far_kernel(me_ref, *refs):
+    each_place(body)
+
+
+def far_kernel(*refs):
     kv_refs, pack_refs, asked = refs[:4], refs[4:8], refs[8:12]
     answers, scores = refs[12:16], refs[16]
 
@@ -244,13 +245,13 @@
         for i, ref in enumerate(answers):
             ref[...] = packed[8 * i : 8 * i + 8]
 
-    each_place(me_ref, body)
+    each_place(body)
 
 
 SMEM = pl.BlockSpec(memory_space=pltpu.SMEM)
 
 
-def attend_main(me, query, bounds, w_out, kv, packs):
+def attend_main(query, bounds, w_out, kv, packs):
     return pl.pallas_call(
         main_kernel,
         cost_estimate=COST,
@@ -259,49 +260,49 @@
             jax.ShapeDtypeStruct(query.shape, BF16),
             jax.ShapeDtypeStruct((8, 2 * HD), F32),
         ),
-        in_specs=[SMEM] + [VMEM] * 11,
+        in_specs=[VMEM] * 11,
         out_specs=(VMEM,) * 2,
         scratch_shapes=[pltpu.VMEM((bounds.shape[0], kv[0].shape[1]), F32)],
-    )(me, query, bounds, w_out, *kv, *packs)
-
-
-def attend_far(me, kv, packs, asked):
+    )(query, bounds, w_out, *kv, *packs)
+
+
+def attend_far(kv, packs, asked):
     return pl.pallas_call(
         far_kernel,
         cost_estimate=COST,
         compiler_params=LIMIT,
         out_shape=(jax.ShapeDtypeStruct((8, 2 * HD), F32),) * 4,
-        in_specs=[SMEM] + [VMEM] * 12,
+        in_specs=[VMEM] * 12,
         out_specs=(VMEM,) * 4,
         scratch_shapes=[pltpu.VMEM((32, kv[0].shape[1]), F32)],
-    )(me, *kv, *packs, *asked)
-
-
-def distance_of(flags_ref, distances):
-    return jnp.where(flags_ref[2] == 0, distances[0], distances[1])
-
-
-def pick_kernel(flags_ref, match_ref, *refs):
+    )(*kv, *packs, *asked)
+
+
+def distance_of(distances):
+    return jnp.where(lax.rem(lax.axis_index("tp"), 2) == 0, distances[0], distances[1])
+
+
+def pick_kernel(match_ref, *refs):
     far = jnp.zeros(refs[-1].shape, F32)
-    group, groups = flags_ref[1], match_ref.shape[0]
+    group, groups = lax.axis_index("grp"), match_ref.shape[0]
     for ref, distances in zip(refs, DISTANCES):
-        prompt = lax.rem(group + distance_of(flags_ref, distances) + groups, groups)
+        prompt = lax.rem(group + distance_of(distances) + groups, groups)
         far = jnp.where(match_ref[prompt] == group, ref[...], far)
     refs[-1][...] = far
 
 
-def pick(flags, match, answers):
+def pick(match, answers):
     return pl.pallas_call(
         pick_kernel,
         cost_estimate=COST,
         compiler_params=LIMIT,
         out_shape=jax.ShapeDtypeStruct(answers[0].shape, F32),
-        in_specs=[SMEM] * 2 + [VMEM] * len(answers),
+        in_specs=[SMEM] + [VMEM] * len(answers),
         out_specs=VMEM,
-    )(flags, match, *answers)
-
-
-def merge_kernel(flags_ref, attended_ref, own_ref, far_ref, mate_ref, perm_ref, w_ref, keep_ref, give_ref):
+    )(match, *answers)
+
+
+def merge_kernel(attended_ref, own_ref, far_ref, mate_ref, perm_ref, w_ref, keep_ref, give_ref):
     own = own_ref[...]
     far = far_ref[:4] + mate_ref[4:]
     far = jnp.concatenate([far, far], 0)
@@ -319,7 +320,7 @@
     rows = attended.shape[0]
     lead = jnp.concatenate([ready] + [jnp.zeros_like(ready)] * (rows // STEPS - 1), 0)
     row = lax.broadcasted_iota(jnp.int32, lead.shape, 0)
-    swap = (row < STEPS) & (flags_ref[0] == 1)
+    swap = (row < STEPS) & (lax.axis_index("role") == 1)
     attended = jnp.where(swap, lead, attended.astype(F32)).astype(BF16)
     attended = lax.dot_general(
         perm_ref[...], attended, (((0,), (0,)), ((), ())), preferred_element_type=F32
@@ -350,16 +351,16 @@
     )(attended, w_out)
 
 
-def merge(flags, attended, own, far, mate, perm, w_out):
+def merge(attended, own, far, mate, perm, w_out):
     half = jax.ShapeDtypeStruct((attended.shape[0] // 2, w_out.shape[1]), BF16)
     return pl.pallas_call(
         merge_kernel,
         cost_estimate=COST,
         compiler_params=LIMIT,
         out_shape=(jax.ShapeDtypeStruct((half.shape[0], attended.shape[1]), BF16), half),
-        in_specs=[SMEM] + [VMEM] * 6,
+        in_specs=[VMEM] * 6,
         out_specs=(VMEM,) * 2,
-    )(flags, attended, own, far, mate, perm, w_out)
+    )(attended, own, far, mate, perm, w_out)
 
 
 def add_core_kernel(own_ref, across_ref, *out_refs):
@@ -502,20 +503,18 @@
     axes = ("role", "grp", "tp")
     asked = [lax.ppermute(leads, axes, carry(d, groups, count, False)) for d in DISTANCES]
     kv = [kv_t, kv_core, kv_y, kv_both]
-    me = jnp.reshape(tp % 4, (1,)).astype(jnp.int32)
-    flags = jnp.stack([side, group, tp % 2]).astype(jnp.int32)
-    answers = attend_far(me, kv, packs, asked)
+    answers = attend_far(kv, packs, asked)
     answers = [
         lax.ppermute(answer, axes, carry(d, groups, count, True))
         for answer, d in zip(answers, DISTANCES)
     ]
     query = after(query, asked)
-    attended, lead_own = attend_main(me, query, bounds, w_out, kv, packs)
+    attended, lead_own = attend_main(query, bounds, w_out, kv, packs)
 
     answers = after(answers, attended)
-    far = pick(flags, match, answers)
+    far = pick(match, answers)
     mate = lax.ppermute(far, "tp", CORE)
-    keep, give = merge(flags, attended, lead_own, far, mate, perm, w_out)
+    keep, give = merge(attended, lead_own, far, mate, perm, w_out)
 
     across = lax.ppermute(give, "tp", CORE)
     keep = shares(keep, w_out)

time: 75.5 us -> 74.9 us (level)
  transfers between devices with their start and end apart: 25 -> 25, of which waited for: 11 -> 12; matrix products, arithmetic and copies ran while one was open for 2% -> 2% of each run, Pallas kernels for 5% -> 5%
where the time goes in v6:
time: 74.9 us; the launch traced here: 74.4 us
  starting transfers between devices  30.6 us (41%)
  waiting for transfers between devices  27.7 us (37%)
  local copies, waits for them, and re-layouts  7.37 us (10%)
  Pallas kernels  6.66 us (9%)
  other arithmetic  1.8 us (2%)
    ppermute x4, waiting for transfers between devices, local(): lax.ppermute(leads, axes, carry(d, groups, count, False))  10.2 us
    unnamed x24, local copies, waits for them, and re-layouts  7.25 us
    ppermute x4, starting transfers between devices, local(): lax.ppermute(answer, axes, carry(d, groups, count, True))  6.72 us
    ppermute x3, waiting for transfers between devices, local(): sent = {k: lax.ppermute(parts[k], 'tp', xshift(k)) for k in X_ORDER}  5.68 us
    ppermute x4, starting transfers between devices, local(): lax.ppermute(leads, axes, carry(d, groups, count, False))  5.17 us
    ppermute x3, waiting for transfers between devices, local(): others = {k: lax.ppermute(pair, 'tp', xshift(-k)) for k in X_ORDER}  4.85 us
    ppermute x3, starting transfers between devices, local(): sent = {k: lax.ppermute(parts[k], 'tp', xshift(k)) for k in X_ORDER}  4.15 us
    ppermute x1, waiting for transfers between devices, local(): summed = summed + lax.ppermute(send, 'tp', YHI).astype(F32)  3.97 us
  transfers between devices with their start and end apart: 25, of which 12 were waited for; matrix products, arithmetic and copies ran while one was open for 2% of the time, Pallas kernels for 5%

profile of v6, /device:TPU:1, one launch (start us, length us, event | category | flops | bytes accessed | tf_op | source)
XLA Modules:
  0.0 74.4 jit_solution(454698324699491344)
XLA Ops:
  0.0 3.7 %collective-permute-start = (bf16[4,8192]{1,0:T(4,128)(2,1)}, bf16[4,8192]{1,0:T(4,128)(2,1)S(1)}, u32[]{:S(2)}, u32[]{:S(2)}) collective-permute-start(bf16[4,8192]{1,0:T(4,128)(2,1)} %bitcast.20), channel_id=1, source_target_pairs={{0,2},{1,3},{2,0},{3,1},{4,6},{5,7},{6,4},{7,5},{8,10},{9,11},{10,... | collective-permute-start | bytes 196616 | tf_op jit(solution)/shard_map/ppermute | solution.py:438
  3.7 0.9 %copy-done.7 = bf16[1,1,4,8192]{3,2,1,0:T(4,128)(2,1)S(1)} copy-done((bf16[1,1,4,8192]{3,2,1,0:T(4,128)(2,1)S(1)}, bf16[1,1,4,8192]{3,2,1,0:T(4,128)(2,1)}, u32[]{:S(2)}) %copy-start.7) | copy-done | bytes 65560
  4.6 0.2 shard_map.82.own_ref
  4.8 0.1 collective-permute-start.4
  4.9 3.0 %collective-permute-start.6 = (bf16[64,4096]{1,0:T(8,128)(2,1)}, bf16[64,4096]{1,0:T(8,128)(2,1)S(1)}, u32[]{:S(2)}, u32[]{:S(2)}) collective-permute-start(bf16[64,4096]{1,0:T(8,128)(2,1)} %bitcast.17), channel_id=1, source_target_pairs={{0,1},{1,0},{2,3},{3,2},{4,5},{5,4},{6,7},{7,6},{8,9},{9,8},{10,11... | collective-permute-start | bytes 1572872 | tf_op jit(solution)/shard_map/ppermute | solution.py:444
  7.9 0.0 copy-start.9
  7.9 0.7 %copy-done.9 = f32[8192]{0:T(1024)S(1)} copy-done((f32[8192]{0:T(1024)S(1)}, f32[8192]{0:T(1024)}, u32[]{:S(2)}) %copy-start.9) | copy-done | bytes 32792
  8.8 0.2 shard_map.84.refs_0_
  9.0 0.8 %collective-permute-start.1 = (bf16[8,8192]{1,0:T(8,128)(2,1)S(1)}, bf16[8,8192]{1,0:T(8,128)(2,1)S(1)}, u32[]{:S(2)}, u32[]{:S(2)}) collective-permute-start(bf16[8,8192]{1,0:T(8,128)(2,1)S(1)} %shard_map.84.refs_0_), channel_id=1, source_target_pairs={{0,12},{1,13},{2,14},{3,15},{4,0},{5,1},{6,2},{7,3},{8,4},{9,5},{1... | collective-permute-start | bytes 393224 | tf_op jit(solution)/shard_map/ppermute | solution.py:446
  9.9 0.5 collective-permute-start.2
  10.4 0.6 collective-permute-start.3
  11.0 2.2 %copy-done.2 = bf16[8192,256]{1,0:T(8,128)(2,1)S(1)} copy-done((bf16[8192,256]{1,0:T(8,128)(2,1)S(1)}, bf16[8192,256]{1,0:T(8,128)(2,1)}, u32[]{:S(2)}) %copy-start.2) | copy-done | bytes 4194328
  13.2 1.2 %copy-done.4 = bf16[8192,64]{0,1:T(8,128)(2,1)S(1)} copy-done((bf16[8192,64]{0,1:T(8,128)(2,1)S(1)}, bf16[8192,64]{0,1:T(8,128)(2,1)}, u32[]{:S(2)}) %copy-start.4) | copy-done | bytes 1048600
  14.4 0.0 copy-start.6
  14.4 0.1 select_reduce_fusion.3
  14.5 0.1 pad_add_fusion.2
  14.6 0.1 select_reduce_fusion.1
  14.7 1.0 %collective-permute-done.2 = bf16[8,8192]{1,0:T(8,128)(2,1)S(1)} collective-permute-done((bf16[8,8192]{1,0:T(8,128)(2,1)S(1)}, bf16[8,8192]{1,0:T(8,128)(2,1)S(1)}, u32[]{:S(2)}, u32[]{:S(2)}) %collective-permute-start.2) | collective-permute-done | bytes 131104 | tf_op jit(solution)/shard_map/ppermute | solution.py:446
  15.7 3.9 %collective-permute-done.3 = bf16[8,8192]{1,0:T(8,128)(2,1)S(1)} collective-permute-done((bf16[8,8192]{1,0:T(8,128)(2,1)S(1)}, bf16[8,8192]{1,0:T(8,128)(2,1)S(1)}, u32[]{:S(2)}, u32[]{:S(2)}) %collective-permute-start.3) | collective-permute-done | bytes 131104 | tf_op jit(solution)/shard_map/ppermute | solution.py:446
  19.6 1.4 %collective-permute-start.5 = (bf16[32,8192]{1,0:T(8,128)(2,1)S(1)}, bf16[32,8192]{1,0:T(8,128)(2,1)S(1)}, u32[]{:S(2)}, u32[]{:S(2)}) collective-permute-start(bf16[32,8192]{1,0:T(8,128)(2,1)S(1)} %pad_maximum_fusion.own_ref), channel_id=1, source_target_pairs={{0,1},{1,0},{2,3},{3,2},{4,5},{5,4},{6,7},{7,6},{8,9},{9,8},{10,11... | collective-permute-start | bytes 1572872 | tf_op jit(solution)/shard_map/ppermute | solution.py:451
  21.1 0.1 select_reduce_fusion
  21.2 0.1 collective-permute-start.8
  21.3 0.2 fusion.4
  21.5 0.3 fusion
  21.8 0.0 collective-permute-done.6.refs_1_
  21.8 0.8 %collective-permute-done.5.mate_ref = bf16[32,8192]{1,0:T(8,128)(2,1)S(1)} collective-permute-done((bf16[32,8192]{1,0:T(8,128)(2,1)S(1)}, bf16[32,8192]{1,0:T(8,128)(2,1)S(1)}, u32[]{:S(2)}, u32[]{:S(2)}) %collective-permute-start.5) | collective-permute-done | bytes 524320 | tf_op jit(solution)/shard_map/ppermute | solution.py:451
  22.6 1.4 %shard_map.86 = (bf16[64,256]{1,0:T(8,128)(2,1)S(1)}, bf16[80,128]{1,0:T(8,128)(2,1)S(1)}) custom-call(bf16[32,8192]{1,0:T(8,128)(2,1)S(1)} %pad_maximum_fusion.own_ref, bf16[32,8192]{1,0:T(8,128)(2,1)S(1)} %collective-permute-done.5.mate_ref, bf16[8192,256]{1,0:T(8,128)(2,1)S(1)} %copy-done.3, bf16[64,8192]{1,0:T(8,128)(2,1)S(1)} %bitcast.15, ...), custom_call_target="tpu_custom_call" | custom-call | flops 1 | bytes 1 | tf_op jit(solution)/shard_map/pallas_call | solution.py:131
  24.0 0.5 collective-permute-start.7
  24.4 2.2 %collective-permute-start.13 = (bf16[80,128]{1,0:T(8,128)(2,1)S(1)}, bf16[80,128]{1,0:T(8,128)(2,1)S(1)}, u32[]{:S(2)}, u32[]{:S(2)}) collective-permute-start(bf16[80,128]{1,0:T(8,128)(2,1)S(1)} %get-tuple-element.44.refs_4_), channel_id=1, source_target_pairs={{0,2},{1,3},{2,0},{3,1},{4,6},{5,7},{6,4},{7,5},{8,10},{9,11},{10,... | collective-permute-start | bytes 61448 | tf_op jit(solution)/shard_map/ppermute | solution.py:499
  26.6 1.3 %collective-permute-start.10 = (bf16[32,128]{1,0:T(8,128)(2,1)S(1)}, bf16[32,128]{1,0:T(8,128)(2,1)S(1)}, u32[]{:S(2)}, u32[]{:S(2)}) collective-permute-start(bf16[32,128]{1,0:T(8,128)(2,1)S(1)} %pad_maximum_fusion.1), channel_id=1, source_target_pairs={{128,96},{129,81},{130,98},{131,83},{132,100},{133,85},{134,102},{... | collective-permute-start | bytes 24584 | tf_op jit(solution)/shard_map/ppermute | solution.py:504
  27.9 1.3 %collective-permute-start.11 = (bf16[32,128]{1,0:T(8,128)(2,1)S(1)}, bf16[32,128]{1,0:T(8,128)(2,1)S(1)}, u32[]{:S(2)}, u32[]{:S(2)}) collective-permute-start(bf16[32,128]{1,0:T(8,128)(2,1)S(1)} %pad_maximum_fusion.1), channel_id=1, source_target_pairs={{128,16},{129,33},{130,18},{131,35},{132,20},{133,37},{134,22},{13... | collective-permute-start | bytes 24584 | tf_op jit(solution)/shard_map/ppermute | solution.py:504
  29.2 1.3 %collective-permute-start.12 = (bf16[32,128]{1,0:T(8,128)(2,1)S(1)}, bf16[32,128]{1,0:T(8,128)(2,1)S(1)}, u32[]{:S(2)}, u32[]{:S(2)}) collective-permute-start(bf16[32,128]{1,0:T(8,128)(2,1)S(1)} %pad_maximum_fusion.1), channel_id=1, source_target_pairs={{128,0},{129,113},{130,2},{131,115},{132,4},{133,117},{134,6},{135... | collective-permute-start | bytes 24584 | tf_op jit(solution)/shard_map/ppermute | solution.py:504
  30.5 1.3 %collective-permute-start.9 = (bf16[32,128]{1,0:T(8,128)(2,1)S(1)}, bf16[32,128]{1,0:T(8,128)(2,1)S(1)}, u32[]{:S(2)}, u32[]{:S(2)}) collective-permute-start(bf16[32,128]{1,0:T(8,128)(2,1)S(1)} %pad_maximum_fusion.1), channel_id=1, source_target_pairs={{128,48},{129,65},{130,50},{131,67},{132,52},{133,69},{134,54},{13... | collective-permute-start | bytes 24584 | tf_op jit(solution)/shard_map/ppermute | solution.py:504
  31.8 0.5 collective-permute-start.14
  32.3 1.4 %collective-permute-done.10.refs_9_ = bf16[32,128]{1,0:T(8,128)(2,1)S(1)} collective-permute-done((bf16[32,128]{1,0:T(8,128)(2,1)S(1)}, bf16[32,128]{1,0:T(8,128)(2,1)S(1)}, u32[]{:S(2)}, u32[]{:S(2)}) %collective-permute-start.10) | collective-permute-done | bytes 8224 | tf_op jit(solution)/shard_map/ppermute | solution.py:504
  33.8 4.7 %collective-permute-done.11.refs_10_ = bf16[32,128]{1,0:T(8,128)(2,1)S(1)} collective-permute-done((bf16[32,128]{1,0:T(8,128)(2,1)S(1)}, bf16[32,128]{1,0:T(8,128)(2,1)S(1)}, u32[]{:S(2)}, u32[]{:S(2)}) %collective-permute-start.11) | collective-permute-done | bytes 8224 | tf_op jit(solution)/shard_map/ppermute | solution.py:504
  38.5 1.8 %collective-permute-done.12.refs_11_ = bf16[32,128]{1,0:T(8,128)(2,1)S(1)} collective-permute-done((bf16[32,128]{1,0:T(8,128)(2,1)S(1)}, bf16[32,128]{1,0:T(8,128)(2,1)S(1)}, u32[]{:S(2)}, u32[]{:S(2)}) %collective-permute-start.12) | collective-permute-done | bytes 8224 | tf_op jit(solution)/shard_map/ppermute | solution.py:504
  40.3 2.3 %collective-permute-done.9.refs_8_ = bf16[32,128]{1,0:T(8,128)(2,1)S(1)} collective-permute-done((bf16[32,128]{1,0:T(8,128)(2,1)S(1)}, bf16[32,128]{1,0:T(8,128)(2,1)S(1)}, u32[]{:S(2)}, u32[]{:S(2)}) %collective-permute-start.9) | collective-permute-done | bytes 8224 | tf_op jit(solution)/shard_map/ppermute | solution.py:504
  42.6 0.8 %shard_map.88 = (f32[8,256]{1,0:T(8,128)S(1)}, f32[8,256]{1,0:T(8,128)S(1)}, f32[8,256]{1,0:T(8,128)S(1)}, f32[8,256]{1,0:T(8,128)S(1)}) custom-call(bf16[64,4096]{1,0:T(8,128)(2,1)S(1)} %bitcast.18, bf16[64,4096]{1,0:T(8,128)(2,1)S(1)} %collective-permute-done.6.refs_1_, bf16[64,4096]{1,0:T(8,128)(2,1)S(1)} %collective-permute-done.4.refs_2_, ...), custom_call_target="tpu_custom_call" | custom-call | flops 1 | bytes 1 | tf_op jit(solution)/shard_map/pallas_call | solution.py:270
  43.4 2.8 %collective-permute-start.15 = (f32[8,256]{1,0:T(8,128)S(1)}, f32[8,256]{1,0:T(8,128)S(1)}, u32[]{:S(2)}, u32[]{:S(2)}) collective-permute-start(f32[8,256]{1,0:T(8,128)S(1)} %get-tuple-element.49), channel_id=1, source_target_pairs={{48,128},{65,129},{50,130},{67,131},{52,132},{69,133},{54,134},{71... | collective-permute-start | bytes 24584 | tf_op jit(solution)/shard_map/ppermute | solution.py:508
  46.2 1.3 %collective-permute-start.16 = (f32[8,256]{1,0:T(8,128)S(1)}, f32[8,256]{1,0:T(8,128)S(1)}, u32[]{:S(2)}, u32[]{:S(2)}) collective-permute-start(f32[8,256]{1,0:T(8,128)S(1)} %get-tuple-element.50), channel_id=1, source_target_pairs={{96,128},{81,129},{98,130},{83,131},{100,132},{85,133},{102,134},{... | collective-permute-start | bytes 24584 | tf_op jit(solution)/shard_map/ppermute | solution.py:508
  47.5 1.3 %collective-permute-start.17 = (f32[8,256]{1,0:T(8,128)S(1)}, f32[8,256]{1,0:T(8,128)S(1)}, u32[]{:S(2)}, u32[]{:S(2)}) collective-permute-start(f32[8,256]{1,0:T(8,128)S(1)} %get-tuple-element.51), channel_id=1, source_target_pairs={{16,128},{33,129},{18,130},{35,131},{20,132},{37,133},{22,134},{39... | collective-permute-start | bytes 24584 | tf_op jit(solution)/shard_map/ppermute | solution.py:508
  48.8 1.3 %collective-permute-start.18 = (f32[8,256]{1,0:T(8,128)S(1)}, f32[8,256]{1,0:T(8,128)S(1)}, u32[]{:S(2)}, u32[]{:S(2)}) collective-permute-start(f32[8,256]{1,0:T(8,128)S(1)} %get-tuple-element.52), channel_id=1, source_target_pairs={{0,128},{113,129},{2,130},{115,131},{4,132},{117,133},{6,134},{119... | collective-permute-start | bytes 24584 | tf_op jit(solution)/shard_map/ppermute | solution.py:508
  50.1 0.1 add_add_fusion
  50.2 0.1 copy.12.bounds_ref
  50.4 2.2 %copy-done = bf16[256,8192]{1,0:T(8,128)(2,1)S(1)} copy-done((bf16[256,8192]{1,0:T(8,128)(2,1)S(1)}, bf16[256,8192]{1,0:T(8,128)(2,1)}, u32[]{:S(2)}) %copy-start) | copy-done | bytes 4194328
  52.5 1.5 %shard_map.87 = (bf16[64,256]{1,0:T(8,128)(2,1)S(1)}, f32[8,256]{1,0:T(8,128)S(1)}) custom-call(bf16[64,256]{1,0:T(8,128)(2,1)S(1)} %get-tuple-element.46.q_ref, s32[128,4]{1,0:T(8,128)S(1)} %copy.12.bounds_ref, bf16[256,8192]{1,0:T(8,128)(2,1)S(1)} %copy-done, bf16[64,4096]{1,0:T(8,128)(2,1)S(1)} %bitcast.19, ...), custom_call_target="tpu_custom_call" | custom-call | flops 1 | bytes 1 | tf_op jit(solution)/shard_map/pallas_call | solution.py:255
  54.1 0.6 shard_map.89.far_ref
  54.7 0.1 collective-permute-start.19
  54.8 1.2 %collective-permute-done.19.mate_ref = f32[8,256]{1,0:T(8,128)S(1)} collective-permute-done((f32[8,256]{1,0:T(8,128)S(1)}, f32[8,256]{1,0:T(8,128)S(1)}, u32[]{:S(2)}, u32[]{:S(2)}) %collective-permute-start.19) | collective-permute-done | bytes 8224 | tf_op jit(solution)/shard_map/ppermute | solution.py:516
  55.9 1.1 %shard_map.90 = (bf16[32,256]{1,0:T(8,128)(2,1)S(1)}, bf16[32,8192]{1,0:T(8,128)(2,1)S(1)}) custom-call(bf16[64,256]{1,0:T(8,128)(2,1)S(1)} %get-tuple-element.47.attended_ref, f32[8,256]{1,0:T(8,128)S(1)} %get-tuple-element.48.own_ref, f32[8,256]{1,0:T(8,128)S(1)} %shard_map.89.far_ref, f32[8,256]{1,0:T(8,128)S(1)} %collective-permute-done.19.mate_ref, ...), custom_call_target="tpu_custom_call" | custom-call | flops 1 | bytes 1 | tf_op jit(solution)/shard_map/pallas_call | solution.py:356
  57.0 0.3 collective-permute-start.20
  57.3 0.8 %shard_map.91.own_ref = bf16[32,8192]{1,0:T(8,128)(2,1)S(1)} custom-call(bf16[32,256]{1,0:T(8,128)(2,1)S(1)} %get-tuple-element.57.attended_ref, bf16[256,8192]{1,0:T(8,128)(2,1)S(1)} %copy-done.1), custom_call_target="tpu_custom_call" | custom-call | flops 1 | bytes 1 | tf_op jit(solution)/shard_map/pallas_call | solution.py:344
  58.1 0.9 %collective-permute-done.20.across_ref = bf16[32,8192]{1,0:T(8,128)(2,1)S(1)} collective-permute-done((bf16[32,8192]{1,0:T(8,128)(2,1)S(1)}, bf16[32,8192]{1,0:T(8,128)(2,1)S(1)}, u32[]{:S(2)}, u32[]{:S(2)}) %collective-permute-start.20) | collective-permute-done | bytes 524320 | tf_op jit(solution)/shard_map/ppermute | solution.py:519
  59.0 0.1 shard_map.92
  59.1 1.5 %collective-permute-start.21 = (bf16[8,8192]{1,0:T(8,128)(2,1)S(1)}, bf16[8,8192]{1,0:T(8,128)(2,1)S(1)}, u32[]{:S(2)}, u32[]{:S(2)}) collective-permute-start(bf16[8,8192]{1,0:T(8,128)(2,1)S(1)} %get-tuple-element.60), channel_id=1, source_target_pairs={{0,8},{1,9},{2,10},{3,11},{4,12},{5,13},{6,14},{7,15},{8,0},{9,1},... | collective-permute-start | bytes 393224 | tf_op jit(solution)/shard_map/ppermute | solution.py:522
  60.6 0.3 collective-permute-start.22
  60.9 2.4 %collective-permute-start.23 = (bf16[8,8192]{1,0:T(8,128)(2,1)S(1)}, bf16[8,8192]{1,0:T(8,128)(2,1)S(1)}, u32[]{:S(2)}, u32[]{:S(2)}) collective-permute-start(bf16[8,8192]{1,0:T(8,128)(2,1)S(1)} %get-tuple-element.62), channel_id=1, source_target_pairs={{0,12},{1,13},{2,14},{3,15},{4,0},{5,1},{6,2},{7,3},{8,4},{9,5},{1... | collective-permute-start | bytes 393224 | tf_op jit(solution)/shard_map/ppermute | solution.py:522
  63.3 2.4 %collective-permute-done.21.b_ref = bf16[8,8192]{1,0:T(8,128)(2,1)S(1)} collective-permute-done((bf16[8,8192]{1,0:T(8,128)(2,1)S(1)}, bf16[8,8192]{1,0:T(8,128)(2,1)S(1)}, u32[]{:S(2)}, u32[]{:S(2)}) %collective-permute-start.21) | collective-permute-done | bytes 131104 | tf_op jit(solution)/shard_map/ppermute | solution.py:522
  65.7 3.3 %collective-permute-done.22.c_ref = bf16[8,8192]{1,0:T(8,128)(2,1)S(1)} collective-permute-done((bf16[8,8192]{1,0:T(8,128)(2,1)S(1)}, bf16[8,8192]{1,0:T(8,128)(2,1)S(1)}, u32[]{:S(2)}, u32[]{:S(2)}) %collective-permute-start.22) | collective-permute-done | bytes 131104 | tf_op jit(solution)/shard_map/ppermute | solution.py:522
  69.0 0.1 shard_map.93
  69.0 0.7 collective-permute-start.24
  69.8 4.0 %collective-permute-done.24 = bf16[4,8192]{1,0:T(4,128)(2,1)S(1)} collective-permute-done((bf16[4,8192]{1,0:T(4,128)(2,1)S(1)}, bf16[4,8192]{1,0:T(4,128)(2,1)S(1)}, u32[]{:S(2)}, u32[]{:S(2)}) %collective-permute-start.24) | collective-permute-done | bytes 65568 | tf_op jit(solution)/shard_map/ppermute | solution.py:525
  73.8 0.7 fusion.1
  (46 shorter events, 0.2 us)
Async XLA Ops:
  0.0 14.4 %copy-start.11 = (s32[1,31]{1,0:T(1,128)S(1)}, s32[1,31]{1,0:T(1,128)}, u32[]{:S(2)}) copy-start(s32[1,31]{1,0:T(1,128)} %param.15) | copy-start | bytes 376
  0.0 8.8 %collective-permute-start = (bf16[4,8192]{1,0:T(4,128)(2,1)}, bf16[4,8192]{1,0:T(4,128)(2,1)S(1)}, u32[]{:S(2)}, u32[]{:S(2)}) collective-permute-start(bf16[4,8192]{1,0:T(4,128)(2,1)} %bitcast.20), channel_id=1, source_target_pairs={{0,2},{1,3},{2,0},{3,1},{4,6},{5,7},{6,4},{7,5},{8,10},{9,11},{10,... | collective-permute-start | bytes 196616 | tf_op jit(solution)/shard_map/ppermute | solution.py:438
  3.7 0.9 %copy-start.7 = (bf16[1,1,4,8192]{3,2,1,0:T(4,128)(2,1)S(1)}, bf16[1,1,4,8192]{3,2,1,0:T(4,128)(2,1)}, u32[]{:S(2)}) copy-start(bf16[1,1,4,8192]{3,2,1,0:T(4,128)(2,1)} %param.8) | copy-start | bytes 196612
  4.8 14.8 %collective-permute-start.4 = (bf16[64,4096]{1,0:T(8,128)(2,1)}, bf16[64,4096]{1,0:T(8,128)(2,1)S(1)}, u32[]{:S(2)}, u32[]{:S(2)}) collective-permute-start(bf16[64,4096]{1,0:T(8,128)(2,1)} %bitcast.16), channel_id=1, source_target_pairs={{0,2},{1,3},{2,0},{3,1},{4,6},{5,7},{6,4},{7,5},{8,10},{9,11},{10,... | collective-permute-start | bytes 1572872 | tf_op jit(solution)/shard_map/ppermute | solution.py:443
  4.9 16.9 %collective-permute-start.6 = (bf16[64,4096]{1,0:T(8,128)(2,1)}, bf16[64,4096]{1,0:T(8,128)(2,1)S(1)}, u32[]{:S(2)}, u32[]{:S(2)}) collective-permute-start(bf16[64,4096]{1,0:T(8,128)(2,1)} %bitcast.17), channel_id=1, source_target_pairs={{0,1},{1,0},{2,3},{3,2},{4,5},{5,4},{6,7},{7,6},{8,9},{9,8},{10,11... | collective-permute-start | bytes 1572872 | tf_op jit(solution)/shard_map/ppermute | solution.py:444
  7.9 0.8 %copy-start.9 = (f32[8192]{0:T(1024)S(1)}, f32[8192]{0:T(1024)}, u32[]{:S(2)}) copy-start(f32[8192]{0:T(1024)} %param.9) | copy-start | bytes 98308
  9.0 5.7 %collective-permute-start.1 = (bf16[8,8192]{1,0:T(8,128)(2,1)S(1)}, bf16[8,8192]{1,0:T(8,128)(2,1)S(1)}, u32[]{:S(2)}, u32[]{:S(2)}) collective-permute-start(bf16[8,8192]{1,0:T(8,128)(2,1)S(1)} %shard_map.84.refs_0_), channel_id=1, source_target_pairs={{0,12},{1,13},{2,14},{3,15},{4,0},{5,1},{6,2},{7,3},{8,4},{9,5},{1... | collective-permute-start | bytes 393224 | tf_op jit(solution)/shard_map/ppermute | solution.py:446
  9.9 5.9 %collective-permute-start.2 = (bf16[8,8192]{1,0:T(8,128)(2,1)S(1)}, bf16[8,8192]{1,0:T(8,128)(2,1)S(1)}, u32[]{:S(2)}, u32[]{:S(2)}) collective-permute-start(bf16[8,8192]{1,0:T(8,128)(2,1)S(1)} %shard_map.84.refs_0_), channel_id=1, source_target_pairs={{0,8},{1,9},{2,10},{3,11},{4,12},{5,13},{6,14},{7,15},{8,0},{9,1},... | collective-permute-start | bytes 393224 | tf_op jit(solution)/shard_map/ppermute | solution.py:446
  10.4 9.2 %collective-permute-start.3 = (bf16[8,8192]{1,0:T(8,128)(2,1)S(1)}, bf16[8,8192]{1,0:T(8,128)(2,1)S(1)}, u32[]{:S(2)}, u32[]{:S(2)}) collective-permute-start(bf16[8,8192]{1,0:T(8,128)(2,1)S(1)} %shard_map.84.refs_0_), channel_id=1, source_target_pairs={{0,4},{1,5},{2,6},{3,7},{4,8},{5,9},{6,10},{7,11},{8,12},{9,13},{1... | collective-permute-start | bytes 393224 | tf_op jit(solution)/shard_map/ppermute | solution.py:446
  11.0 2.2 %copy-start.2 = (bf16[8192,256]{1,0:T(8,128)(2,1)S(1)}, bf16[8192,256]{1,0:T(8,128)(2,1)}, u32[]{:S(2)}) copy-start(bf16[8192,256]{1,0:T(8,128)(2,1)} %wq_ref.1) | copy-start | bytes 12582916
  13.2 1.2 %copy-start.4 = (bf16[8192,64]{0,1:T(8,128)(2,1)S(1)}, bf16[8192,64]{0,1:T(8,128)(2,1)}, u32[]{:S(2)}) copy-start(bf16[8192,64]{0,1:T(8,128)(2,1)} %param.11) | copy-start | bytes 3145732
  14.4 8.2 %copy-start.3 = (bf16[8192,256]{1,0:T(8,128)(2,1)S(1)}, bf16[8192,256]{1,0:T(8,128)(2,1)}, u32[]{:S(2)}) copy-start(bf16[8192,256]{1,0:T(8,128)(2,1)} %wq_ref.1) | copy-start | bytes 12582916
  14.4 8.2 %copy-start.5 = (bf16[8192,64]{0,1:T(8,128)(2,1)S(1)}, bf16[8192,64]{0,1:T(8,128)(2,1)}, u32[]{:S(2)}) copy-start(bf16[8192,64]{0,1:T(8,128)(2,1)} %param.11) | copy-start | bytes 3145732
  14.4 28.2 %copy-start.6 = (bf16[1,1,4096,64]{2,3,1,0:T(8,128)(2,1)S(1)}, bf16[1,1,4096,64]{2,3,1,0:T(8,128)(2,1)}, u32[]{:S(2)}) copy-start(bf16[1,1,4096,64]{2,3,1,0:T(8,128)(2,1)} %param.13) | copy-start | bytes 1572868
  19.6 3.0 %collective-permute-start.5 = (bf16[32,8192]{1,0:T(8,128)(2,1)S(1)}, bf16[32,8192]{1,0:T(8,128)(2,1)S(1)}, u32[]{:S(2)}, u32[]{:S(2)}) collective-permute-start(bf16[32,8192]{1,0:T(8,128)(2,1)S(1)} %pad_maximum_fusion.own_ref), channel_id=1, source_target_pairs={{0,1},{1,0},{2,3},{3,2},{4,5},{5,4},{6,7},{7,6},{8,9},{9,8},{10,11... | collective-permute-start | bytes 1572872 | tf_op jit(solution)/shard_map/ppermute | solution.py:451
  21.2 5.4 %collective-permute-start.8 = (bf16[64,4096]{1,0:T(8,128)(2,1)S(1)}, bf16[64,4096]{1,0:T(8,128)(2,1)S(1)}, u32[]{:S(2)}, u32[]{:S(2)}) collective-permute-start(bf16[64,4096]{1,0:T(8,128)(2,1)S(1)} %collective-permute-done.4.refs_2_), channel_id=1, source_target_pairs={{0,1},{1,0},{2,3},{3,2},{4,5},{5,4},{6,7},{7,6},{8,9},{9,8},{10,11... | collective-permute-start | bytes 1572872 | tf_op jit(solution)/shard_map/ppermute | solution.py:452
  24.0 2.6 %collective-permute-start.7 = (bf16[80,128]{1,0:T(8,128)(2,1)S(1)}, bf16[80,128]{1,0:T(8,128)(2,1)S(1)}, u32[]{:S(2)}, u32[]{:S(2)}) collective-permute-start(bf16[80,128]{1,0:T(8,128)(2,1)S(1)} %get-tuple-element.44.refs_4_), channel_id=1, source_target_pairs={{0,1},{1,0},{2,3},{3,2},{4,5},{5,4},{6,7},{7,6},{8,9},{9,8},{10,11... | collective-permute-start | bytes 61448 | tf_op jit(solution)/shard_map/ppermute | solution.py:500
  24.4 7.4 %collective-permute-start.13 = (bf16[80,128]{1,0:T(8,128)(2,1)S(1)}, bf16[80,128]{1,0:T(8,128)(2,1)S(1)}, u32[]{:S(2)}, u32[]{:S(2)}) collective-permute-start(bf16[80,128]{1,0:T(8,128)(2,1)S(1)} %get-tuple-element.44.refs_4_), channel_id=1, source_target_pairs={{0,2},{1,3},{2,0},{3,1},{4,6},{5,7},{6,4},{7,5},{8,10},{9,11},{10,... | collective-permute-start | bytes 61448 | tf_op jit(solution)/shard_map/ppermute | solution.py:499
  26.6 7.2 %collective-permute-start.10 = (bf16[32,128]{1,0:T(8,128)(2,1)S(1)}, bf16[32,128]{1,0:T(8,128)(2,1)S(1)}, u32[]{:S(2)}, u32[]{:S(2)}) collective-permute-start(bf16[32,128]{1,0:T(8,128)(2,1)S(1)} %pad_maximum_fusion.1), channel_id=1, source_target_pairs={{128,96},{129,81},{130,98},{131,83},{132,100},{133,85},{134,102},{... | collective-permute-start | bytes 24584 | tf_op jit(solution)/shard_map/ppermute | solution.py:504
  27.9 10.6 %collective-permute-start.11 = (bf16[32,128]{1,0:T(8,128)(2,1)S(1)}, bf16[32,128]{1,0:T(8,128)(2,1)S(1)}, u32[]{:S(2)}, u32[]{:S(2)}) collective-permute-start(bf16[32,128]{1,0:T(8,128)(2,1)S(1)} %pad_maximum_fusion.1), channel_id=1, source_target_pairs={{128,16},{129,33},{130,18},{131,35},{132,20},{133,37},{134,22},{13... | collective-permute-start | bytes 24584 | tf_op jit(solution)/shard_map/ppermute | solution.py:504
  29.2 11.1 %collective-permute-start.12 = (bf16[32,128]{1,0:T(8,128)(2,1)S(1)}, bf16[32,128]{1,0:T(8,128)(2,1)S(1)}, u32[]{:S(2)}, u32[]{:S(2)}) collective-permute-start(bf16[32,128]{1,0:T(8,128)(2,1)S(1)} %pad_maximum_fusion.1), channel_id=1, source_target_pairs={{128,0},{129,113},{130,2},{131,115},{132,4},{133,117},{134,6},{135... | collective-permute-start | bytes 24584 | tf_op jit(solution)/shard_map/ppermute | solution.py:504
  30.5 12.1 %collective-permute-start.9 = (bf16[32,128]{1,0:T(8,128)(2,1)S(1)}, bf16[32,128]{1,0:T(8,128)(2,1)S(1)}, u32[]{:S(2)}, u32[]{:S(2)}) collective-permute-start(bf16[32,128]{1,0:T(8,128)(2,1)S(1)} %pad_maximum_fusion.1), channel_id=1, source_target_pairs={{128,48},{129,65},{130,50},{131,67},{132,52},{133,69},{134,54},{13... | collective-permute-start | bytes 24584 | tf_op jit(solution)/shard_map/ppermute | solution.py:504
  31.8 10.8 %collective-permute-start.14 = (bf16[80,128]{1,0:T(8,128)(2,1)S(1)}, bf16[80,128]{1,0:T(8,128)(2,1)S(1)}, u32[]{:S(2)}, u32[]{:S(2)}) collective-permute-start(bf16[80,128]{1,0:T(8,128)(2,1)S(1)} %collective-permute-done.13.refs_6_), channel_id=1, source_target_pairs={{0,1},{1,0},{2,3},{3,2},{4,5},{5,4},{6,7},{7,6},{8,9},{9,8},{10,11... | collective-permute-start | bytes 61448 | tf_op jit(solution)/shard_map/ppermute | solution.py:501
  32.3 21.7 %copy-start.10 = (s32[8]{0:T(128)S(1)}, s32[8]{0:T(128)}, u32[]{:S(2)}) copy-start(s32[8]{0:T(128)} %match_ref.1) | copy-start | bytes 100
  43.4 10.6 %collective-permute-start.15 = (f32[8,256]{1,0:T(8,128)S(1)}, f32[8,256]{1,0:T(8,128)S(1)}, u32[]{:S(2)}, u32[]{:S(2)}) collective-permute-start(f32[8,256]{1,0:T(8,128)S(1)} %get-tuple-element.49), channel_id=1, source_target_pairs={{48,128},{65,129},{50,130},{67,131},{52,132},{69,133},{54,134},{71... | collective-permute-start | bytes 24584 | tf_op jit(solution)/shard_map/ppermute | solution.py:508
  46.2 7.8 %collective-permute-start.16 = (f32[8,256]{1,0:T(8,128)S(1)}, f32[8,256]{1,0:T(8,128)S(1)}, u32[]{:S(2)}, u32[]{:S(2)}) collective-permute-start(f32[8,256]{1,0:T(8,128)S(1)} %get-tuple-element.50), channel_id=1, source_target_pairs={{96,128},{81,129},{98,130},{83,131},{100,132},{85,133},{102,134},{... | collective-permute-start | bytes 24584 | tf_op jit(solution)/shard_map/ppermute | solution.py:508
  47.5 6.5 %collective-permute-start.17 = (f32[8,256]{1,0:T(8,128)S(1)}, f32[8,256]{1,0:T(8,128)S(1)}, u32[]{:S(2)}, u32[]{:S(2)}) collective-permute-start(f32[8,256]{1,0:T(8,128)S(1)} %get-tuple-element.51), channel_id=1, source_target_pairs={{16,128},{33,129},{18,130},{35,131},{20,132},{37,133},{22,134},{39... | collective-permute-start | bytes 24584 | tf_op jit(solution)/shard_map/ppermute | solution.py:508
  48.8 5.2 %collective-permute-start.18 = (f32[8,256]{1,0:T(8,128)S(1)}, f32[8,256]{1,0:T(8,128)S(1)}, u32[]{:S(2)}, u32[]{:S(2)}) collective-permute-start(f32[8,256]{1,0:T(8,128)S(1)} %get-tuple-element.52), channel_id=1, source_target_pairs={{0,128},{113,129},{2,130},{115,131},{4,132},{117,133},{6,134},{119... | collective-permute-start | bytes 24584 | tf_op jit(solution)/shard_map/ppermute | solution.py:508
  50.3 2.2 %copy-start = (bf16[256,8192]{1,0:T(8,128)(2,1)S(1)}, bf16[256,8192]{1,0:T(8,128)(2,1)}, u32[]{:S(2)}) copy-start(bf16[256,8192]{1,0:T(8,128)(2,1)} %w_ref.5) | copy-start | bytes 12582916
  52.5 3.4 %copy-start.1 = (bf16[256,8192]{1,0:T(8,128)(2,1)S(1)}, bf16[256,8192]{1,0:T(8,128)(2,1)}, u32[]{:S(2)}) copy-start(bf16[256,8192]{1,0:T(8,128)(2,1)} %w_ref.5) | copy-start | bytes 12582916
  54.7 1.3 %collective-permute-start.19 = (f32[8,256]{1,0:T(8,128)S(1)}, f32[8,256]{1,0:T(8,128)S(1)}, u32[]{:S(2)}, u32[]{:S(2)}) collective-permute-start(f32[8,256]{1,0:T(8,128)S(1)} %shard_map.89.far_ref), channel_id=1, source_target_pairs={{0,1},{1,0},{2,3},{3,2},{4,5},{5,4},{6,7},{7,6},{8,9},{9,8},{10,11... | collective-permute-start | bytes 24584 | tf_op jit(solution)/shard_map/ppermute | solution.py:516
  57.0 16.8 %copy-start.8 = (bf16[1,1,4,8192]{3,2,1,0:T(4,128)(2,1)S(1)}, bf16[1,1,4,8192]{3,2,1,0:T(4,128)(2,1)}, u32[]{:S(2)}) copy-start(bf16[1,1,4,8192]{3,2,1,0:T(4,128)(2,1)} %param.8) | copy-start | bytes 196612
  57.0 2.0 %collective-permute-start.20 = (bf16[32,8192]{1,0:T(8,128)(2,1)S(1)}, bf16[32,8192]{1,0:T(8,128)(2,1)S(1)}, u32[]{:S(2)}, u32[]{:S(2)}) collective-permute-start(bf16[32,8192]{1,0:T(8,128)(2,1)S(1)} %get-tuple-element.58), channel_id=1, source_target_pairs={{0,1},{1,0},{2,3},{3,2},{4,5},{5,4},{6,7},{7,6},{8,9},{9,8},{10,11... | collective-permute-start | bytes 1572872 | tf_op jit(solution)/shard_map/ppermute | solution.py:519
  59.1 6.5 %collective-permute-start.21 = (bf16[8,8192]{1,0:T(8,128)(2,1)S(1)}, bf16[8,8192]{1,0:T(8,128)(2,1)S(1)}, u32[]{:S(2)}, u32[]{:S(2)}) collective-permute-start(bf16[8,8192]{1,0:T(8,128)(2,1)S(1)} %get-tuple-element.60), channel_id=1, source_target_pairs={{0,8},{1,9},{2,10},{3,11},{4,12},{5,13},{6,14},{7,15},{8,0},{9,1},... | collective-permute-start | bytes 393224 | tf_op jit(solution)/shard_map/ppermute | solution.py:522
  60.6 8.4 %collective-permute-start.22 = (bf16[8,8192]{1,0:T(8,128)(2,1)S(1)}, bf16[8,8192]{1,0:T(8,128)(2,1)S(1)}, u32[]{:S(2)}, u32[]{:S(2)}) collective-permute-start(bf16[8,8192]{1,0:T(8,128)(2,1)S(1)} %get-tuple-element.61), channel_id=1, source_target_pairs={{0,4},{1,5},{2,6},{3,7},{4,8},{5,9},{6,10},{7,11},{8,12},{9,13},{1... | collective-permute-start | bytes 393224 | tf_op jit(solution)/shard_map/ppermute | solution.py:522
  60.9 8.0 %collective-permute-start.23 = (bf16[8,8192]{1,0:T(8,128)(2,1)S(1)}, bf16[8,8192]{1,0:T(8,128)(2,1)S(1)}, u32[]{:S(2)}, u32[]{:S(2)}) collective-permute-start(bf16[8,8192]{1,0:T(8,128)(2,1)S(1)} %get-tuple-element.62), channel_id=1, source_target_pairs={{0,12},{1,13},{2,14},{3,15},{4,0},{5,1},{6,2},{7,3},{8,4},{9,5},{1... | collective-permute-start | bytes 393224 | tf_op jit(solution)/shard_map/ppermute | solution.py:522
  69.0 4.7 %collective-permute-start.24 = (bf16[4,8192]{1,0:T(4,128)(2,1)S(1)}, bf16[4,8192]{1,0:T(4,128)(2,1)S(1)}, u32[]{:S(2)}, u32[]{:S(2)}) collective-permute-start(bf16[4,8192]{1,0:T(4,128)(2,1)S(1)} %get-tuple-element.64), channel_id=1, source_target_pairs={{0,2},{1,3},{2,0},{3,1},{4,6},{5,7},{6,4},{7,5},{8,10},{9,11},{10,... | collective-permute-start | bytes 196616 | tf_op jit(solution)/shard_map/ppermute | solution.py:525
